TPU v7x, 32 devices: a whole 2x2x4 slice. The times are simulated.
32 devices in a mesh: ctx: 8 (over z, x), tp: 4 (over y, core).
Axes of the slice: x: 2, y: 2, z: 4, core: 2. Of those that a mesh axis runs over, the one named last changes fastest.
Arguments:
- streams: bfloat16 [1280, 3, 4096], P('ctx', None, 'tp'), may hold values from -6 to 6
- short_taps: float32 [7, 3, 4096], P(None, None, 'tp'), may hold values from -2 to 2
- mix_taps: float32 [128, 4096], P(None, 'tp'), may hold values from -0.5 to 0.5
- pole_rate: float32 [16, 4096], P(None, 'tp'), may hold values from 7.8125e-05 to 0.06, as said below
- pole_angle: float32 [16, 4096], P(None, 'tp'), may hold values from -3.140625 to 3.140625
- residue: float32 [2, 16, 4096], P(None, None, 'tp'), may hold values from -1.5 to 1.5
- skip: float32 [4096], P('tp'), may hold values from -3 to 3
- out_weight: bfloat16 [4096, 4096], P('tp', 'ctx'), may hold values from -0.125 to 0.125
Outputs:
- mixed: bfloat16 [1280, 4096], P('ctx', 'tp')
Inputs may be any that keep to these rules, and one draw needn't show every extreme that they name: `pole_rate`: each pole's decay rate is positive.
All inputs are finite; a program needn't handle non-finite values.
Results may differ from a plain program's by a relative error of at most 0.0057.
Values may be sent and summed in bfloat16 or wider, within the bound.
No kernel may reach another device: no remote copies, remote signals or barrier semaphores. Data moves between devices by JAX's collectives and lax.ppermute only.
A program may use at most 64 MiB of HBM per device.

v0:
```python
import jax
import jax.numpy as jnp
import ml_dtypes
import numpy as np
from jax import lax
from jax.experimental import pallas as pl
from jax.experimental.pallas import tpu as pltpu
from jax.sharding import PartitionSpec as P

F32 = jnp.float32
BF16 = jnp.bfloat16
AXES = ("ctx", "tp")
GROUP = 4
BIT_CORE, BIT_Y, BIT_PART = 1, 2, 16
SLOT_BITS = (0, 4, 8, 12)
VMEM = pl.BlockSpec(memory_space=pltpu.VMEM)
SMEM = pl.BlockSpec(memory_space=pltpu.SMEM)


def swap(block, bits):
    return lax.ppermute(block, AXES, [(i, i ^ bits) for i in range(32)])


def split_const(mat):
    hi = mat.astype(ml_dtypes.bfloat16)
    lo = (mat - hi.astype(np.float64)).astype(ml_dtypes.bfloat16)
    return hi, lo


def odd_dft(size, rows_in):
    freq = 2 * np.pi * (np.arange(size // 2) + 0.5) / size
    ang = freq[:, None] * np.arange(rows_in)
    return np.concatenate([np.cos(ang), -np.sin(ang)], 0)


def odd_idft(size, rows_out):
    freq = 2 * np.pi * (np.arange(size // 2) + 0.5) / size
    ang = np.asarray(rows_out)[:, None] * freq
    return np.concatenate([np.cos(ang), -np.sin(ang)], 1) * (2.0 / size)


def mm(a, b):
    return jnp.dot(a, b, preferred_element_type=F32)


def split(x):
    hi = x.astype(BF16)
    return hi, (x - hi.astype(F32)).astype(BF16)


def mm3(hi, lo, x):
    xh, xl = split(x)
    return mm(hi, xh) + mm(lo, xh) + mm(hi, xl)


def cmul(spec, filt):
    half = spec.shape[0] // 2
    a, b, c, d = spec[:half], spec[half:], filt[:half], filt[half:]
    return jnp.concatenate([a * c - b * d, a * d + b * c], 0)


def params(**kw):
    return pltpu.CompilerParams(vmem_limit_bytes=56 * 1024 * 1024, **kw)


def filters_kernel(rows, modes, taps_ref, rate_ref, angle_ref, res_ref, skip_ref, cmh, cml, clh, cll,
                   spec_ref, lspec_ref, qre_ref, qim_ref, par_ref):
    width = taps_ref.shape[1]
    ntap = taps_ref.shape[0]
    spec_ref[...] = mm3(cmh[:, :ntap], cml[:, :ntap], taps_ref[...])
    rate, angle = rate_ref[...], angle_ref[...]
    amp = jnp.sqrt(1.0 - jnp.exp(-2.0 * rate))
    rre, rim = res_ref[0] * amp, res_ref[1] * amp

    def power(n):
        mag = jnp.exp(-rate * n)
        return mag * jnp.cos(angle * n), mag * jnp.sin(angle * n)

    p1, p8, pend = power(1.0), power(8.0), power(float(rows))
    par_ref[0], par_ref[1] = rre * p1[0] - rim * p1[1], rre * p1[1] + rim * p1[0]
    par_ref[2], par_ref[3] = pend
    steps = lax.broadcasted_iota(jnp.int32, (8, width), 0).astype(F32)
    filt = [jnp.zeros((8, width), F32) for _ in range(rows // 8)]
    for m in range(modes):
        ang = angle[m:m + 1] * steps
        mag = jnp.exp(-rate[m:m + 1] * steps)
        cre, cim = mag * jnp.cos(ang), mag * jnp.sin(ang)
        sre, sim = p8[0][m:m + 1], p8[1][m:m + 1]
        wre, wim = rre[m:m + 1], rim[m:m + 1]
        for j in range(rows // 8):
            qre_ref[m, j * 8:j * 8 + 8] = cre
            qim_ref[m, j * 8:j * 8 + 8] = cim
            filt[j] = filt[j] + wre * cre - wim * cim
            cre, cim = cre * sre - cim * sim, cre * sim + cim * sre
    first = lax.broadcasted_iota(jnp.int32, (8, width), 0) == 0
    filt[0] = filt[0] + jnp.where(first, skip_ref[...], 0.0)
    lspec_ref[...] = mm3(clh[...], cll[...], jnp.concatenate(filt, 0))


def short_conv(ext_ref, taps, total):
    out = taps[0:1] * ext_ref[8:8 + total]
    for lag in range(1, 7):
        out = out + taps[lag:lag + 1] * ext_ref[8 - lag:8 - lag + total]
    return out


def gate_kernel(rows, g_ref, t_ref, s0, s1, s2, s3, gate_ref, msg_ref, head_ref, kx, vx):
    g = g_ref[0]
    total = GROUP * rows
    kx[:8] = jnp.zeros_like(kx[:8])
    vx[:8] = jnp.zeros_like(vx[:8])
    for m, s in enumerate((s0, s1, s2, s3)):
        at = pl.ds(pl.multiple_of((g ^ m) * rows + 8, 8), rows)
        kx[at, :] = s[0].astype(F32)
        vx[at, :] = s[1].astype(F32)
    sk = short_conv(kx, t_ref[1], total)
    sv = short_conv(vx, t_ref[2], total)
    gate = (sk * sv).astype(BF16)
    gate_ref[...] = gate
    head_ref[0], head_ref[1] = sk[:8], sv[:8]
    msg_ref[:128] = gate[total - 128:]
    tails = jnp.concatenate([kx[total:total + 8], vx[total:total + 8]], 0)
    msg_ref[128:144] = tails.astype(BF16)


def tail_part(tail, taps):
    ext = jnp.concatenate([tail, jnp.zeros_like(tail)], 0)
    out = taps[1:2] * ext[7:15]
    for lag in range(2, 7):
        out = out + taps[lag:lag + 1] * ext[8 - lag:16 - lag]
    return out


def medium_kernel(rows, modes, g_ref, t_ref, gate_ref, msg_ref, head_ref, spec_ref, qre_ref, qim_ref, par_ref,
                  cmh, cml, imh, iml, q0, q1, q2, q3,
                  med_ref, st_ref, out_ref, gx, flip, er, ei):
    g, part = g_ref[0], g_ref[1]
    width = gate_ref.shape[1]
    total = GROUP * rows
    live = (part > 0).astype(F32)
    gx[:128] = (msg_ref[:128].astype(F32) * live).astype(BF16)
    tails = msg_ref[128:144].astype(F32) * live
    sk = head_ref[0] + tail_part(tails[:8], t_ref[1])
    sv = head_ref[1] + tail_part(tails[8:], t_ref[2])
    gx[128:128 + total] = gate_ref[...]
    gx[128:144] = jnp.concatenate([(sk * sv).astype(BF16).astype(F32), gate_ref[:16].astype(F32)[8:]], 0).astype(BF16)
    for b in range(GROUP):
        gb = gx[b * rows:b * rows + rows + 128]
        y = cmul(mm(cmh[...], gb) + mm(cml[...], gb), spec_ref[...])
        both = mm3(imh[...], iml[...], y)
        med_ref[b] = both[:rows]
        flip[b] = both[rows:]
    lanes = width // 128
    per = 4
    for lt in range(lanes):
        ls = slice(lt * 128, lt * 128 + 128)
        for m0 in range(0, modes, per):
            def step(j, acc):
                at = pl.ds(pl.multiple_of(j * 8, 8), 8)
                x = [flip[b, at, ls] for b in range(GROUP)]
                out = []
                for i in range(per):
                    qr, qi = qre_ref[m0 + i, at, ls], qim_ref[m0 + i, at, ls]
                    for b in range(GROUP):
                        k = (i * GROUP + b) * 2
                        out += [acc[k] + x[b] * qr, acc[k + 1] + x[b] * qi]
                return tuple(out)
            acc = lax.fori_loop(0, rows // 8, step, (jnp.zeros((8, 128), F32),) * (2 * GROUP * per), unroll=4)
            for i in range(per):
                for b in range(GROUP):
                    k = (i * GROUP + b) * 2
                    er[b, m0 + i:m0 + i + 1, ls] = jnp.sum(acc[k], 0, keepdims=True)
                    ei[b, m0 + i:m0 + i + 1, ls] = jnp.sum(acc[k + 1], 0, keepdims=True)
    dre, dim = par_ref[2], par_ref[3]
    sre = jnp.zeros((modes, width), F32)
    sim = sre
    for b in range(GROUP):
        st_ref[b, 0], st_ref[b, 1] = sre, sim
        sre, sim = dre * sre - dim * sim + er[b], dre * sim + dim * sre + ei[b]
    out_ref[:modes] = sre
    out_ref[modes:2 * modes] = sim
    for m, q in enumerate((q0, q1, q2, q3)):
        @pl.when((g ^ m) == GROUP - 1)
        def _():
            out_ref[2 * modes:] = q[rows - 16:].astype(F32)[8:]


def intra_kernel(rows, g_ref, t_ref, med_ref, lspec_ref, clh, cll, ilh, ill, q0, q1, q2, q3, intra_ref, query_ref, qx):
    g = g_ref[0]
    for b in range(GROUP):
        y = cmul(mm3(clh[...], cll[...], med_ref[b]), lspec_ref[...])
        intra_ref[b] = mm3(ilh[...], ill[...], y)
    qx[:8] = jnp.zeros_like(qx[:8])
    for m, q in enumerate((q0, q1, q2, q3)):
        qx[pl.ds(pl.multiple_of((g ^ m) * rows + 8, 8), rows), :] = q[...].astype(F32)
    query_ref[...] = short_conv(qx, t_ref[0], GROUP * rows)


def hidden_kernel(rows, modes, g_ref, t_ref, in_ref, st_ref, par_ref, qre_ref, qim_ref, intra_ref, query_ref, hid_ref, amp):
    part = g_ref[1]
    live = (part > 0).astype(F32)
    width = query_ref.shape[1]
    rin, iin = in_ref[:modes] * live, in_ref[modes:2 * modes] * live
    rre, rim, dre, dim = par_ref[0], par_ref[1], par_ref[2], par_ref[3]
    for b in range(GROUP):
        sre, sim = st_ref[b, 0] + rin, st_ref[b, 1] + iin
        are, aim = rre * sre - rim * sim, rre * sim + rim * sre
        for m in range(modes):
            amp[b, m, 0] = jnp.broadcast_to(are[m:m + 1], (8, width))
            amp[b, m, 1] = jnp.broadcast_to(aim[m:m + 1], (8, width))
        rin, iin = dre * rin - dim * iin, dre * iin + dim * rin
    query_ref_head = query_ref[:8] + tail_part(in_ref[2 * modes:] * live, t_ref[0])
    query_ref[:8] = query_ref_head
    for lt in range(width // 128):
        ls = slice(lt * 128, lt * 128 + 128)

        def step(j, carry):
            at = [pl.ds(pl.multiple_of(j * 16 + 8 * i, 8), 8) for i in range(2)]
            acc = [[intra_ref[b, at[i], ls] for i in range(2)] for b in range(GROUP)]
            for m in range(modes):
                qr = [qre_ref[m, at[i], ls] for i in range(2)]
                qi = [qim_ref[m, at[i], ls] for i in range(2)]
                for b in range(GROUP):
                    ar, ai = amp[b, m, 0, :, ls], amp[b, m, 1, :, ls]
                    for i in range(2):
                        acc[b][i] = acc[b][i] + ar * qr[i] - ai * qi[i]
            for b in range(GROUP):
                row = pl.multiple_of(b * rows + j * 16, 16)
                long = jnp.concatenate(acc[b], 0)
                hid_ref[pl.ds(row, 16), ls] = (query_ref[pl.ds(row, 16), ls] * long).astype(BF16)
            return carry

        lax.fori_loop(0, rows // 16, step, 0)


def project_kernel(g_ref, h0, h1, h2, h3, wa_ref, wb_ref, keep_ref, send_ref):
    g, same, core = g_ref[0], g_ref[2], g_ref[3]
    quarter = h0.shape[1]
    half = wa_ref.shape[1] // 2
    mine = pl.ds(pl.multiple_of(core * half, half), half)
    other = pl.ds(pl.multiple_of((1 - core) * half, half), half)
    accs = [None] * 4
    for m, h in enumerate((h0, h1, h2, h3)):
        at = pl.ds(pl.multiple_of((g ^ m) * quarter, quarter), quarter)
        x = h[...]
        for n, cols in enumerate((mine, other)):
            a, b = wa_ref[at, cols], wb_ref[at, cols]
            for k, w in enumerate((a, b)):
                d = mm(x, w)
                accs[2 * k + n] = d if m == 0 else accs[2 * k + n] + d
    own = same > 0
    keep_ref[0] = jnp.where(own, accs[0], accs[2])
    keep_ref[1] = jnp.where(own, accs[2], accs[0])
    send_ref[0] = jnp.where(own, accs[1], accs[3]).astype(BF16)
    send_ref[1] = jnp.where(own, accs[3], accs[1]).astype(BF16)


def call(kernel, outs, args, scratch=(), flops=10**8):
    return pl.pallas_call(
        kernel,
        out_shape=tuple(jax.ShapeDtypeStruct(s, d) for s, d in outs),
        in_specs=[SMEM] + [VMEM] * (len(args) - 1),
        out_specs=(VMEM,) * len(outs),
        scratch_shapes=[pltpu.VMEM(s, d) for s, d in scratch],
        compiler_params=params(),
    )(*args)


def fast_body(streams, short_taps, mix_taps, pole_rate, pole_angle, residue, skip, out_weight):
    rows, _, width = streams.shape
    modes = pole_rate.shape[0]
    ntap = mix_taps.shape[0]
    quarter = width // GROUP
    total = GROUP * rows
    ctx, tp = lax.axis_index("ctx"), lax.axis_index("tp")
    g, part = ctx % GROUP, ctx // GROUP
    core, y = tp % 2, tp // 2
    scal = jnp.stack([g, part, (y == part).astype(jnp.int32), core]).astype(jnp.int32)

    def columns(x, slot=0):
        return lax.dynamic_slice_in_dim(x, (g ^ slot) * quarter, quarter, x.ndim - 1)

    kv = [columns(streams[:, 1:], m).transpose(1, 0, 2) for m in range(GROUP)]
    qs = [columns(streams[:, 0], m) for m in range(GROUP)]
    kv = [kv[0]] + [swap(kv[m], SLOT_BITS[m]) for m in (1, 2, 3)]
    qs = [qs[0]] + [swap(qs[m], SLOT_BITS[m]) for m in (1, 2, 3)]

    size_m, size_l = rows + ntap, 2 * rows
    cmh, cml = split_const(odd_dft(size_m, size_m))
    back = np.concatenate([np.arange(ntap, size_m), np.arange(ntap, size_m)[::-1]])
    imh, iml = split_const(odd_idft(size_m, back))
    clh, cll = split_const(odd_dft(size_l, rows))
    ilh, ill = split_const(odd_idft(size_l, np.arange(rows)))

    taps = columns(short_taps).transpose(1, 0, 2)
    args = (columns(mix_taps), columns(pole_rate), columns(pole_angle), columns(residue), columns(skip)[None], cmh, cml, clh, cll)
    spec, lspec, qre, qim, par = pl.pallas_call(
        lambda *refs: filters_kernel(rows, modes, *refs),
        out_shape=tuple(jax.ShapeDtypeStruct(s, F32) for s in (
            (size_m, quarter), (size_l, quarter), (modes, rows, quarter), (modes, rows, quarter), (4, modes, quarter))),
        in_specs=[VMEM] * len(args),
        out_specs=(VMEM,) * 5,
        compiler_params=params(),
    )(*args)

    gate, msg, head = call(
        lambda *refs: gate_kernel(rows, *refs),
        [((total, quarter), BF16), ((144, quarter), BF16), ((2, 8, quarter), F32)],
        (scal, taps, *kv),
        [((total + 8, quarter), F32)] * 2,
    )
    msg = swap(msg, BIT_PART)
    med, st, out = call(
        lambda *refs: medium_kernel(rows, modes, *refs),
        [((GROUP, rows, quarter), F32), ((GROUP, 2, modes, quarter), F32), ((2 * modes + 8, quarter), F32)],
        (scal, taps, gate, msg, head, spec, qre, qim, par, cmh, cml, imh, iml, *qs),
        [((total + 128, quarter), BF16), ((GROUP, rows, quarter), F32), ((GROUP, modes, quarter), F32), ((GROUP, modes, quarter), F32)],
    )
    state_in = swap(out, BIT_PART)
    intra, query = call(
        lambda *refs: intra_kernel(rows, *refs),
        [((GROUP, rows, quarter), F32), ((total, quarter), F32)],
        (scal, taps, med, lspec, clh, cll, ilh, ill, *qs),
        [((total + 8, quarter), F32)],
    )
    (hidden,) = call(
        lambda *refs: hidden_kernel(rows, modes, *refs),
        [((total, quarter), BF16)],
        (scal, taps, state_in, st, par, qre, qim, intra, query),
        [((GROUP, modes, 2, 8, quarter), F32)],
    )
    hid = [hidden] + [swap(hidden, SLOT_BITS[m]) for m in (1, 2, 3)]
    far_weight = swap(out_weight, BIT_PART)
    half = out_weight.shape[1] // 2
    keep, send = call(
        project_kernel,
        [((2, total, half), F32), ((2, total, half), BF16)],
        (scal, *hid, out_weight, far_weight),
    )
    chip = keep + swap(send, BIT_CORE).astype(F32)
    both = (chip[0] + swap(chip[1].astype(BF16), BIT_Y).astype(F32)).astype(BF16)
    blocks = [lax.dynamic_slice_in_dim(both, (g ^ m) * rows, rows, 0) for m in range(GROUP)]
    got = [blocks[0]] + [swap(blocks[m], SLOT_BITS[m]) for m in (1, 2, 3)]
    stay = (g // 2) == core
    near = [jnp.where(stay, got[0], got[2]), jnp.where(stay, got[1], got[3])]
    away = jnp.stack([jnp.where(stay, got[2], got[0]), jnp.where(stay, got[3], got[1])])
    far = swap(away, BIT_CORE)
    even = g % 2 == 0
    near = [jnp.where(even, near[0], near[1]), jnp.where(even, near[1], near[0])]
    far = [jnp.where(even, far[0], far[1]), jnp.where(even, far[1], far[0])]
    first = core == 0
    pieces = []
    for x in range(2):
        pieces += [jnp.where(first, near[x], far[x]), jnp.where(first, far[x], near[x])]
    return jnp.concatenate(pieces, 1)


def from_behind(block, axis, distance):
    devices = range(lax.axis_size(axis))
    route = [(i - distance, i) for i in devices if i - distance in devices]
    return lax.ppermute(block, axis, route)


def depthwise(ext, taps):
    width = taps.shape[1]
    kernel = taps[::-1][:, None, :]
    out = lax.conv_general_dilated(
        ext[None],
        kernel,
        (1,),
        "VALID",
        dimension_numbers=("NWC", "WIO", "NWC"),
        feature_group_count=width,
        precision=lax.Precision.HIGHEST,
    )
    return out[0]


def general_body(streams, short_taps, mix_taps, pole_rate, pole_angle, residue, skip, out_weight):
    rows, three, width = streams.shape
    modes = pole_rate.shape[0]
    short = short_taps.reshape(7, three * width)
    rim = from_behind(streams[rows - 6 :], "ctx", 1)
    ext = jnp.concatenate([rim, streams], 0).astype(jnp.float32).reshape(rows + 6, three * width)
    conv = depthwise(ext, short).reshape(rows, three, width)
    gate = (conv[:, 1] * conv[:, 2]).astype(jnp.bfloat16)
    gate_rim = from_behind(gate[rows - 127 :], "ctx", 1)
    gate_ext = jnp.concatenate([gate_rim, gate], 0)
    query = conv[:, 0]
    medium = depthwise(gate_ext.astype(jnp.float32), mix_taps)
    amp = jnp.sqrt(1.0 - jnp.exp(-2.0 * pole_rate))
    res_re = residue[0] * amp
    res_im = residue[1] * amp
    steps = jnp.arange(rows).astype(jnp.float32)[:, None]
    flipped = medium[::-1]

    def first_pass(mode, carry):
        filt, end_re, end_im = carry
        rate = pole_rate[mode][None]
        angle = pole_angle[mode][None]
        mag = jnp.exp(-rate * steps)
        cosk = mag * jnp.cos(angle * steps)
        sink = mag * jnp.sin(angle * steps)
        filt = filt + res_re[mode][None] * cosk - res_im[mode][None] * sink
        end_re = end_re.at[mode].set(jnp.sum(flipped * cosk, 0))
        end_im = end_im.at[mode].set(jnp.sum(flipped * sink, 0))
        return (filt, end_re, end_im)

    zero_state = jnp.zeros((modes, width), jnp.float32)
    filt, end_re, end_im = lax.fori_loop(
        0, modes, first_pass, (jnp.zeros((rows, width), jnp.float32), zero_state, zero_state)
    )
    dec_mag = jnp.exp(-pole_rate * rows)
    dec_re = dec_mag * jnp.cos(pole_angle * rows)
    dec_im = dec_mag * jnp.sin(pole_angle * rows)

    def relay_step(turn, received):
        in_re, in_im = received
        out_re = dec_re * in_re - dec_im * in_im + end_re
        out_im = dec_re * in_im + dec_im * in_re + end_im
        return from_behind((out_re, out_im), "ctx", 1)

    st_re, st_im = lax.fori_loop(0, lax.axis_size("ctx") - 1, relay_step, (zero_state, zero_state))
    later = steps + 1.0

    def second_pass(mode, inflow):
        rate = pole_rate[mode][None]
        angle = pole_angle[mode][None]
        mag = jnp.exp(-rate * later)
        cos1 = mag * jnp.cos(angle * later)
        sin1 = mag * jnp.sin(angle * later)
        are = res_re[mode] * st_re[mode] - res_im[mode] * st_im[mode]
        aim = res_re[mode] * st_im[mode] + res_im[mode] * st_re[mode]
        return inflow + are[None] * cos1 - aim[None] * sin1

    inflow = lax.fori_loop(0, modes, second_pass, jnp.zeros((rows, width), jnp.float32))
    padded = jnp.concatenate([jnp.zeros((rows - 1, width), jnp.float32), medium], 0)
    intra = depthwise(padded, filt)
    longf = intra + inflow + skip[None] * medium
    hidden = (query * longf).astype(jnp.bfloat16)
    partial_out = jnp.dot(
        hidden,
        lax.all_gather(out_weight, "ctx", axis=1, tiled=True),
        preferred_element_type=jnp.float32,
    )
    return lax.psum_scatter(partial_out, "tp", scatter_dimension=1, tiled=True).astype(jnp.bfloat16)


def solution(mesh):
    fast = dict(mesh.shape) == {"ctx": 8, "tp": 4}
    return jax.shard_map(
        fast_body if fast else general_body,
        mesh=mesh,
        in_specs=(
            P("ctx", None, "tp"),
            P(None, None, "tp"),
            P(None, "tp"),
            P(None, "tp"),
            P(None, "tp"),
            P(None, None, "tp"),
            P("tp"),
            P("tp", "ctx"),
        ),
        out_specs=P("ctx", "tp"),
        check_vma=False,
    )
```

profile of v0, /device:TPU:0, one launch (start us, length us, event | category | flops | bytes accessed | tf_op | source)
XLA Modules:
  0.0 129.0 jit_solution(463604701441949016)
XLA Ops:
  0.0 1.5 %slice-done = bf16[160,2,1024]{2,0,1:T(8,128)(2,1)S(1)} async-done(((bf16[160,3,1024]{2,0,1:T(8,128)(2,1)}), bf16[160,2,1024]{2,0,1:T(8,128)(2,1)S(1)}, s32[]{:S(2)}) %slice-start) | async-done | bytes 655384 | tf_op jit(solution)/shard_map/slice | solution.py:283
  2.3 2.9 %collective-permute-start = (bf16[2,160,256]{2,1,0:T(8,128)(2,1)S(1)}, bf16[2,160,256]{2,1,0:T(8,128)(2,1)S(1)}, u32[]{:S(2)}, u32[]{:S(2)}) collective-permute-start(bf16[2,160,256]{2,1,0:T(8,128)(2,1)S(1)} %get-tuple-element.40), channel_id=1, source_target_pairs={{0,4},{1,5},{2,6},{3,7},{4,0},{5,1},{6,2},{7,3},{8,12},{9,13},{10,... | collective-permute-start | bytes 491528 | tf_op jit(solution)/shard_map/ppermute | solution.py:21
  5.2 1.6 %collective-permute-start.1 = (bf16[2,160,256]{2,1,0:T(8,128)(2,1)S(1)}, bf16[2,160,256]{2,1,0:T(8,128)(2,1)S(1)}, u32[]{:S(2)}, u32[]{:S(2)}) collective-permute-start(bf16[2,160,256]{2,1,0:T(8,128)(2,1)S(1)} %get-tuple-element.39), channel_id=1, source_target_pairs={{0,8},{1,9},{2,10},{3,11},{4,12},{5,13},{6,14},{7,15},{8,0},{9,1},... | collective-permute-start | bytes 491528 | tf_op jit(solution)/shard_map/ppermute | solution.py:21
  6.8 3.0 %collective-permute-start.11 = (bf16[1024,512]{1,0:T(8,128)(2,1)S(1)}, bf16[1024,512]{1,0:T(8,128)(2,1)}, u32[]{:S(2)}, u32[]{:S(2)}) collective-permute-start(bf16[1024,512]{1,0:T(8,128)(2,1)S(1)} %copy-done.1), channel_id=1, source_target_pairs={{0,16},{1,17},{2,18},{3,19},{4,20},{5,21},{6,22},{7,23},{8,24},{9,... | collective-permute-start | bytes 3145736 | tf_op jit(solution)/shard_map/ppermute | solution.py:21
  10.5 1.5 %collective-permute-start.4 = (bf16[160,256]{1,0:T(8,128)(2,1)S(1)}, bf16[160,256]{1,0:T(8,128)(2,1)S(1)}, u32[]{:S(2)}, u32[]{:S(2)}) collective-permute-start(bf16[160,256]{1,0:T(8,128)(2,1)S(1)} %get-tuple-element.50), channel_id=1, source_target_pairs={{0,4},{1,5},{2,6},{3,7},{4,0},{5,1},{6,2},{7,3},{8,12},{9,13},{10,... | collective-permute-start | bytes 245768 | tf_op jit(solution)/shard_map/ppermute | solution.py:21
  17.3 1.6 %collective-permute-start.5 = (bf16[160,256]{1,0:T(8,128)(2,1)S(1)}, bf16[160,256]{1,0:T(8,128)(2,1)S(1)}, u32[]{:S(2)}, u32[]{:S(2)}) collective-permute-start(bf16[160,256]{1,0:T(8,128)(2,1)S(1)} %get-tuple-element.49), channel_id=1, source_target_pairs={{0,8},{1,9},{2,10},{3,11},{4,12},{5,13},{6,14},{7,15},{8,0},{9,1},... | collective-permute-start | bytes 245768 | tf_op jit(solution)/shard_map/ppermute | solution.py:21
  19.3 1.8 %collective-permute-done.2.refs_5_ = bf16[2,160,256]{2,1,0:T(8,128)(2,1)S(1)} collective-permute-done((bf16[2,160,256]{2,1,0:T(8,128)(2,1)S(1)}, bf16[2,160,256]{2,1,0:T(8,128)(2,1)S(1)}, u32[]{:S(2)}, u32[]{:S(2)}) %collective-permute-start.2) | collective-permute-done | bytes 163872 | tf_op jit(solution)/shard_map/ppermute | solution.py:21
  21.8 3.6 %shard_map.154 = (bf16[640,256]{1,0:T(8,128)(2,1)}, bf16[144,256]{1,0:T(8,128)(2,1)}, f32[2,8,256]{2,1,0:T(8,128)}) custom-call(s32[4]{0:T(128)} %pad_add_fusion.refs_0_.g_ref, f32[3,7,256]{2,1,0:T(8,128)} %dynamic-slice_bitcast_fusion.8.refs_1_, bf16[2,160,256]{2,1,0:T(8,128)(2,1)} %get-tuple-element.41.refs_2_, bf16[2,160,256]{2,1,0:T(8,128)(2,1)} %copy-done.8, ...), custom_call_target="tpu_custom_call" | custom-call | tf_op jit(solution)/shard_map/pallas_call | solution.py:259
  27.7 5.2 %shard_map.155 = (f32[288,256]{1,0:T(8,128)}, f32[320,256]{1,0:T(8,128)}, f32[16,160,256]{2,1,0:T(8,128)}, f32[16,160,256]{2,1,0:T(8,128)}, f32[4,16,256]{2,1,0:T(8,128)}) custom-call(f32[128,256]{1,0:T(8,128)} %constant_dynamic-slice_fusion.6.refs_0_, f32[16,256]{1,0:T(8,128)} %get-tuple-element.53.refs_1_, f32[16,256]{1,0:T(8,128)} %get-tuple-element.52.refs_2_, ...), custom_call_target="tpu_custom_call" | custom-call | tf_op jit(solution)/shard_map/pallas_call | solution.py:297
  33.0 6.3 %collective-permute-done.5.refs_15_.refs_10_ = bf16[160,256]{1,0:T(8,128)(2,1)S(1)} collective-permute-done((bf16[160,256]{1,0:T(8,128)(2,1)S(1)}, bf16[160,256]{1,0:T(8,128)(2,1)S(1)}, u32[]{:S(2)}, u32[]{:S(2)}) %collective-permute-start.5) | collective-permute-done | bytes 81952 | tf_op jit(solution)/shard_map/ppermute | solution.py:21
  40.3 17.5 %collective-permute-done.3.refs_3_ = bf16[144,256]{1,0:T(8,128)(2,1)S(1)} collective-permute-done((bf16[144,256]{1,0:T(8,128)(2,1)}, bf16[144,256]{1,0:T(8,128)(2,1)S(1)}, u32[]{:S(2)}, u32[]{:S(2)}) %collective-permute-start.3) | collective-permute-done | bytes 73760 | tf_op jit(solution)/shard_map/ppermute | solution.py:21
  58.5 9.0 %shard_map.156 = (f32[4,160,256]{2,1,0:T(8,128)}, f32[4,2,16,256]{3,2,1,0:T(8,128)}, f32[40,256]{1,0:T(8,128)}) custom-call(s32[4]{0:T(128)} %pad_add_fusion.refs_0_.g_ref, f32[3,7,256]{2,1,0:T(8,128)} %dynamic-slice_bitcast_fusion.8.refs_1_, bf16[640,256]{1,0:T(8,128)(2,1)} %get-tuple-element.20.refs_2_, bf16[144,256]{1,0:T(8,128)(2,1)} %copy-done.11, ...), custom_call_target="tpu_custom_call" | custom-call | tf_op jit(solution)/shard_map/pallas_call | solution.py:259
  67.4 4.8 %shard_map.157 = (f32[4,160,256]{2,1,0:T(8,128)}, f32[640,256]{1,0:T(8,128)}) custom-call(s32[4]{0:T(128)} %pad_add_fusion.refs_0_.g_ref, f32[3,7,256]{2,1,0:T(8,128)} %dynamic-slice_bitcast_fusion.8.refs_1_, f32[4,160,256]{2,1,0:T(8,128)} %get-tuple-element.29.refs_2_, f32[320,256]{1,0:T(8,128)} %get-tuple-element.30.refs_3_, ...), custom_call_target="tpu_custom_call" | custom-call | tf_op jit(solution)/shard_map/pallas_call | solution.py:259
  73.1 5.9 %shard_map.158.h0 = bf16[640,256]{1,0:T(8,128)(2,1)} custom-call(s32[4]{0:T(128)} %pad_add_fusion.refs_0_.g_ref, f32[3,7,256]{2,1,0:T(8,128)} %dynamic-slice_bitcast_fusion.8.refs_1_, f32[40,256]{1,0:T(8,128)} %copy-done.12, f32[4,2,16,256]{3,2,1,0:T(8,128)} %get-tuple-element.28.refs_3_, f32[4,16,256]{2,1,0:T(8,128)} %get-tuple-element.26.refs_8_.refs_4_, ...), custom_call_target="tpu_custom_call" | custom-call | tf_op jit(solution)/shard_map/pallas_call | solution.py:259
  79.1 4.8 %collective-permute-start.10 = (bf16[640,256]{1,0:T(8,128)(2,1)}, bf16[640,256]{1,0:T(8,128)(2,1)S(1)}, u32[]{:S(2)}, u32[]{:S(2)}) collective-permute-start(bf16[640,256]{1,0:T(8,128)(2,1)} %shard_map.158.h0), channel_id=1, source_target_pairs={{0,12},{1,13},{2,14},{3,15},{4,8},{5,9},{6,10},{7,11},{8,4},{9,5},... | collective-permute-start | bytes 983048 | tf_op jit(solution)/shard_map/ppermute | solution.py:21
  84.4 8.3 %collective-permute-done.10.h3 = bf16[640,256]{1,0:T(8,128)(2,1)S(1)} collective-permute-done((bf16[640,256]{1,0:T(8,128)(2,1)}, bf16[640,256]{1,0:T(8,128)(2,1)S(1)}, u32[]{:S(2)}, u32[]{:S(2)}) %collective-permute-start.10) | collective-permute-done | bytes 327712 | tf_op jit(solution)/shard_map/ppermute | solution.py:21
  92.8 4.2 %collective-permute-done.8.h1 = bf16[640,256]{1,0:T(8,128)(2,1)S(1)} collective-permute-done((bf16[640,256]{1,0:T(8,128)(2,1)}, bf16[640,256]{1,0:T(8,128)(2,1)S(1)}, u32[]{:S(2)}, u32[]{:S(2)}) %collective-permute-start.8) | collective-permute-done | bytes 327712 | tf_op jit(solution)/shard_map/ppermute | solution.py:21
  97.8 4.6 %shard_map.159 = (f32[2,640,256]{2,1,0:T(8,128)}, bf16[2,640,256]{2,1,0:T(8,128)(2,1)}) custom-call(s32[4]{0:T(128)} %pad_add_fusion.refs_0_.g_ref, bf16[640,256]{1,0:T(8,128)(2,1)} %shard_map.158.h0, bf16[640,256]{1,0:T(8,128)(2,1)} %copy-done.3, bf16[640,256]{1,0:T(8,128)(2,1)} %copy-done.4, bf16[640,256]{1,0:T(8,128)(2,1)} %copy-done.2, ...), custom_call_target="tpu_custom_call" | custom-call | tf_op jit(solution)/shard_map/pallas_call | solution.py:259
  102.4 2.3 %collective-permute-done.12 = bf16[2,640,256]{2,1,0:T(8,128)(2,1)S(1)} collective-permute-done((bf16[2,640,256]{2,1,0:T(8,128)(2,1)}, bf16[2,640,256]{2,1,0:T(8,128)(2,1)S(1)}, u32[]{:S(2)}, u32[]{:S(2)}) %collective-permute-start.12) | collective-permute-done | bytes 655392 | tf_op jit(solution)/shard_map/ppermute | solution.py:21
  106.2 1.6 %collective-permute-start.13 = (bf16[640,256]{1,0:T(8,128)(2,1)S(1)}, bf16[640,256]{1,0:T(8,128)(2,1)S(1)}, u32[]{:S(2)}, u32[]{:S(2)}) collective-permute-start(bf16[640,256]{1,0:T(8,128)(2,1)S(1)} %fusion.2), channel_id=1, source_target_pairs={{0,2},{1,3},{2,0},{3,1},{4,6},{5,7},{6,4},{7,5},{8,10},{9,11},{10,... | collective-permute-start | bytes 983048 | tf_op jit(solution)/shard_map/ppermute | solution.py:21
  107.8 8.2 %collective-permute-done.13 = bf16[640,256]{1,0:T(8,128)(2,1)S(1)} collective-permute-done((bf16[640,256]{1,0:T(8,128)(2,1)S(1)}, bf16[640,256]{1,0:T(8,128)(2,1)S(1)}, u32[]{:S(2)}, u32[]{:S(2)}) %collective-permute-start.13) | collective-permute-done | bytes 327712 | tf_op jit(solution)/shard_map/ppermute | solution.py:21
  116.1 1.8 %collective-permute-start.14 = (bf16[160,256]{1,0:T(8,128)(2,1)S(1)}, bf16[160,256]{1,0:T(8,128)(2,1)S(1)}, u32[]{:S(2)}, u32[]{:S(2)}) collective-permute-start(bf16[160,256]{1,0:T(8,128)(2,1)S(1)} %constant_dynamic-slice_fusion.2), channel_id=1, source_target_pairs={{0,8},{1,9},{2,10},{3,11},{4,12},{5,13},{6,14},{7,15},{8,0},{9,1},... | collective-permute-start | bytes 245768 | tf_op jit(solution)/shard_map/ppermute | solution.py:21
  117.9 2.7 %collective-permute-done.14 = bf16[160,256]{1,0:T(8,128)(2,1)S(1)} collective-permute-done((bf16[160,256]{1,0:T(8,128)(2,1)S(1)}, bf16[160,256]{1,0:T(8,128)(2,1)S(1)}, u32[]{:S(2)}, u32[]{:S(2)}) %collective-permute-start.14) | collective-permute-done | bytes 81952 | tf_op jit(solution)/shard_map/ppermute | solution.py:21
  121.3 2.6 %collective-permute-start.16 = (bf16[160,256]{1,0:T(8,128)(2,1)S(1)}, bf16[160,256]{1,0:T(8,128)(2,1)S(1)}, u32[]{:S(2)}, u32[]{:S(2)}) collective-permute-start(bf16[160,256]{1,0:T(8,128)(2,1)S(1)} %get-tuple-element.46), channel_id=1, source_target_pairs={{0,12},{1,13},{2,14},{3,15},{4,8},{5,9},{6,10},{7,11},{8,4},{9,5},... | collective-permute-start | bytes 245768 | tf_op jit(solution)/shard_map/ppermute | solution.py:21
  (66 shorter events, 21.5 us)
Async XLA Ops:
  0.0 16.7 %copy-start = (f32[128,1024]{1,0:T(8,128)S(1)}, f32[128,1024]{1,0:T(8,128)}, u32[]{:S(2)}) copy-start(f32[128,1024]{1,0:T(8,128)} %param.18) | copy-start | bytes 1572868
  0.0 6.8 %copy-start.1 = (bf16[1024,512]{1,0:T(8,128)(2,1)S(1)}, bf16[1024,512]{1,0:T(8,128)(2,1)}, u32[]{:S(2)}) copy-start(bf16[1024,512]{1,0:T(8,128)(2,1)} %wa_ref.1) | copy-start | bytes 3145732
  0.0 9.8 %slice-start.1 = ((bf16[160,3,1024]{2,0,1:T(8,128)(2,1)}), bf16[160,1,1024]{2,0,1:T(8,128)(2,1)S(1)}, s32[]{:S(2)}) async-start(bf16[160,3,1024]{2,0,1:T(8,128)(2,1)} %param.16), calls=%async_computation.1 | async-start | bytes 655360 | tf_op jit(solution)/shard_map/slice | solution.py:284
  2.3 15.0 %collective-permute-start = (bf16[2,160,256]{2,1,0:T(8,128)(2,1)S(1)}, bf16[2,160,256]{2,1,0:T(8,128)(2,1)S(1)}, u32[]{:S(2)}, u32[]{:S(2)}) collective-permute-start(bf16[2,160,256]{2,1,0:T(8,128)(2,1)S(1)} %get-tuple-element.40), channel_id=1, source_target_pairs={{0,4},{1,5},{2,6},{3,7},{4,0},{5,1},{6,2},{7,3},{8,12},{9,13},{10,... | collective-permute-start | bytes 491528 | tf_op jit(solution)/shard_map/ppermute | solution.py:21
  5.2 13.9 %collective-permute-start.1 = (bf16[2,160,256]{2,1,0:T(8,128)(2,1)S(1)}, bf16[2,160,256]{2,1,0:T(8,128)(2,1)S(1)}, u32[]{:S(2)}, u32[]{:S(2)}) collective-permute-start(bf16[2,160,256]{2,1,0:T(8,128)(2,1)S(1)} %get-tuple-element.39), channel_id=1, source_target_pairs={{0,8},{1,9},{2,10},{3,11},{4,12},{5,13},{6,14},{7,15},{8,0},{9,1},... | collective-permute-start | bytes 491528 | tf_op jit(solution)/shard_map/ppermute | solution.py:21
  6.8 14.3 %collective-permute-start.2 = (bf16[2,160,256]{2,1,0:T(8,128)(2,1)S(1)}, bf16[2,160,256]{2,1,0:T(8,128)(2,1)S(1)}, u32[]{:S(2)}, u32[]{:S(2)}) collective-permute-start(bf16[2,160,256]{2,1,0:T(8,128)(2,1)S(1)} %get-tuple-element.38), channel_id=1, source_target_pairs={{0,12},{1,13},{2,14},{3,15},{4,8},{5,9},{6,10},{7,11},{8,4},{9,5},... | collective-permute-start | bytes 491528 | tf_op jit(solution)/shard_map/ppermute | solution.py:21
  6.8 90.1 %collective-permute-start.11 = (bf16[1024,512]{1,0:T(8,128)(2,1)S(1)}, bf16[1024,512]{1,0:T(8,128)(2,1)}, u32[]{:S(2)}, u32[]{:S(2)}) collective-permute-start(bf16[1024,512]{1,0:T(8,128)(2,1)S(1)} %copy-done.1), channel_id=1, source_target_pairs={{0,16},{1,17},{2,18},{3,19},{4,20},{5,21},{6,22},{7,23},{8,24},{9,... | collective-permute-start | bytes 3145736 | tf_op jit(solution)/shard_map/ppermute | solution.py:21
  10.5 22.5 %collective-permute-start.4 = (bf16[160,256]{1,0:T(8,128)(2,1)S(1)}, bf16[160,256]{1,0:T(8,128)(2,1)S(1)}, u32[]{:S(2)}, u32[]{:S(2)}) collective-permute-start(bf16[160,256]{1,0:T(8,128)(2,1)S(1)} %get-tuple-element.50), channel_id=1, source_target_pairs={{0,4},{1,5},{2,6},{3,7},{4,0},{5,1},{6,2},{7,3},{8,12},{9,13},{10,... | collective-permute-start | bytes 245768 | tf_op jit(solution)/shard_map/ppermute | solution.py:21
  17.3 21.9 %collective-permute-start.5 = (bf16[160,256]{1,0:T(8,128)(2,1)S(1)}, bf16[160,256]{1,0:T(8,128)(2,1)S(1)}, u32[]{:S(2)}, u32[]{:S(2)}) collective-permute-start(bf16[160,256]{1,0:T(8,128)(2,1)S(1)} %get-tuple-element.49), channel_id=1, source_target_pairs={{0,8},{1,9},{2,10},{3,11},{4,12},{5,13},{6,14},{7,15},{8,0},{9,1},... | collective-permute-start | bytes 245768 | tf_op jit(solution)/shard_map/ppermute | solution.py:21
  19.2 21.1 %collective-permute-start.6 = (bf16[160,256]{1,0:T(8,128)(2,1)S(1)}, bf16[160,256]{1,0:T(8,128)(2,1)S(1)}, u32[]{:S(2)}, u32[]{:S(2)}) collective-permute-start(bf16[160,256]{1,0:T(8,128)(2,1)S(1)} %get-tuple-element.48), channel_id=1, source_target_pairs={{0,12},{1,13},{2,14},{3,15},{4,8},{5,9},{6,10},{7,11},{8,4},{9,5},... | collective-permute-start | bytes 245768 | tf_op jit(solution)/shard_map/ppermute | solution.py:21
  25.4 32.4 %collective-permute-start.3 = (bf16[144,256]{1,0:T(8,128)(2,1)}, bf16[144,256]{1,0:T(8,128)(2,1)S(1)}, u32[]{:S(2)}, u32[]{:S(2)}) collective-permute-start(bf16[144,256]{1,0:T(8,128)(2,1)} %get-tuple-element.21), channel_id=1, source_target_pairs={{0,16},{1,17},{2,18},{3,19},{4,20},{5,21},{6,22},{7,23},{8,24},{9,... | collective-permute-start | bytes 221192 | tf_op jit(solution)/shard_map/ppermute | solution.py:21
  33.0 24.9 %copy-start.5 = (bf16[160,256]{1,0:T(8,128)(2,1)}, bf16[160,256]{1,0:T(8,128)(2,1)S(1)}, u32[]{:S(2)}) copy-start(bf16[160,256]{1,0:T(8,128)(2,1)S(1)} %collective-permute-done.4.refs_14_.refs_9_) | copy-start | bytes 245764
  39.2 18.6 %copy-start.6 = (bf16[160,256]{1,0:T(8,128)(2,1)}, bf16[160,256]{1,0:T(8,128)(2,1)S(1)}, u32[]{:S(2)}) copy-start(bf16[160,256]{1,0:T(8,128)(2,1)S(1)} %collective-permute-done.5.refs_15_.refs_10_) | copy-start | bytes 245764
  40.3 17.5 %copy-start.7 = (bf16[160,256]{1,0:T(8,128)(2,1)}, bf16[160,256]{1,0:T(8,128)(2,1)S(1)}, u32[]{:S(2)}) copy-start(bf16[160,256]{1,0:T(8,128)(2,1)S(1)} %collective-permute-done.6.refs_16_.refs_11_) | copy-start | bytes 245764
  67.4 5.1 %collective-permute-start.7 = (f32[40,256]{1,0:T(8,128)}, f32[40,256]{1,0:T(8,128)S(1)}, u32[]{:S(2)}, u32[]{:S(2)}) collective-permute-start(f32[40,256]{1,0:T(8,128)} %get-tuple-element.27), channel_id=1, source_target_pairs={{0,16},{1,17},{2,18},{3,19},{4,20},{5,21},{6,22},{7,23},{8,24},{9,... | collective-permute-start | bytes 122888 | tf_op jit(solution)/shard_map/ppermute | solution.py:21
  79.1 13.7 %collective-permute-start.10 = (bf16[640,256]{1,0:T(8,128)(2,1)}, bf16[640,256]{1,0:T(8,128)(2,1)S(1)}, u32[]{:S(2)}, u32[]{:S(2)}) collective-permute-start(bf16[640,256]{1,0:T(8,128)(2,1)} %shard_map.158.h0), channel_id=1, source_target_pairs={{0,12},{1,13},{2,14},{3,15},{4,8},{5,9},{6,10},{7,11},{8,4},{9,5},... | collective-permute-start | bytes 983048 | tf_op jit(solution)/shard_map/ppermute | solution.py:21
  83.9 13.0 %collective-permute-start.8 = (bf16[640,256]{1,0:T(8,128)(2,1)}, bf16[640,256]{1,0:T(8,128)(2,1)S(1)}, u32[]{:S(2)}, u32[]{:S(2)}) collective-permute-start(bf16[640,256]{1,0:T(8,128)(2,1)} %shard_map.158.h0), channel_id=1, source_target_pairs={{0,4},{1,5},{2,6},{3,7},{4,0},{5,1},{6,2},{7,3},{8,12},{9,13},{10,... | collective-permute-start | bytes 983048 | tf_op jit(solution)/shard_map/ppermute | solution.py:21
  84.4 12.5 %collective-permute-start.9 = (bf16[640,256]{1,0:T(8,128)(2,1)}, bf16[640,256]{1,0:T(8,128)(2,1)S(1)}, u32[]{:S(2)}, u32[]{:S(2)}) collective-permute-start(bf16[640,256]{1,0:T(8,128)(2,1)} %shard_map.158.h0), channel_id=1, source_target_pairs={{0,8},{1,9},{2,10},{3,11},{4,12},{5,13},{6,14},{7,15},{8,0},{9,1},... | collective-permute-start | bytes 983048 | tf_op jit(solution)/shard_map/ppermute | solution.py:21
  102.4 2.3 %collective-permute-start.12 = (bf16[2,640,256]{2,1,0:T(8,128)(2,1)}, bf16[2,640,256]{2,1,0:T(8,128)(2,1)S(1)}, u32[]{:S(2)}, u32[]{:S(2)}) collective-permute-start(bf16[2,640,256]{2,1,0:T(8,128)(2,1)} %get-tuple-element.34), channel_id=1, source_target_pairs={{0,1},{1,0},{2,3},{3,2},{4,5},{5,4},{6,7},{7,6},{8,9},{9,8},{10,11... | collective-permute-start | bytes 1966088 | tf_op jit(solution)/shard_map/ppermute | solution.py:21
  106.2 9.8 %collective-permute-start.13 = (bf16[640,256]{1,0:T(8,128)(2,1)S(1)}, bf16[640,256]{1,0:T(8,128)(2,1)S(1)}, u32[]{:S(2)}, u32[]{:S(2)}) collective-permute-start(bf16[640,256]{1,0:T(8,128)(2,1)S(1)} %fusion.2), channel_id=1, source_target_pairs={{0,2},{1,3},{2,0},{3,1},{4,6},{5,7},{6,4},{7,5},{8,10},{9,11},{10,... | collective-permute-start | bytes 983048 | tf_op jit(solution)/shard_map/ppermute | solution.py:21
  116.1 4.5 %collective-permute-start.14 = (bf16[160,256]{1,0:T(8,128)(2,1)S(1)}, bf16[160,256]{1,0:T(8,128)(2,1)S(1)}, u32[]{:S(2)}, u32[]{:S(2)}) collective-permute-start(bf16[160,256]{1,0:T(8,128)(2,1)S(1)} %constant_dynamic-slice_fusion.2), channel_id=1, source_target_pairs={{0,8},{1,9},{2,10},{3,11},{4,12},{5,13},{6,14},{7,15},{8,0},{9,1},... | collective-permute-start | bytes 245768 | tf_op jit(solution)/shard_map/ppermute | solution.py:21
  120.7 4.5 %collective-permute-start.15 = (bf16[160,256]{1,0:T(8,128)(2,1)S(1)}, bf16[160,256]{1,0:T(8,128)(2,1)S(1)}, u32[]{:S(2)}, u32[]{:S(2)}) collective-permute-start(bf16[160,256]{1,0:T(8,128)(2,1)S(1)} %get-tuple-element.47), channel_id=1, source_target_pairs={{0,4},{1,5},{2,6},{3,7},{4,0},{5,1},{6,2},{7,3},{8,12},{9,13},{10,... | collective-permute-start | bytes 245768 | tf_op jit(solution)/shard_map/ppermute | solution.py:21
  121.3 5.3 %collective-permute-start.16 = (bf16[160,256]{1,0:T(8,128)(2,1)S(1)}, bf16[160,256]{1,0:T(8,128)(2,1)S(1)}, u32[]{:S(2)}, u32[]{:S(2)}) collective-permute-start(bf16[160,256]{1,0:T(8,128)(2,1)S(1)} %get-tuple-element.46), channel_id=1, source_target_pairs={{0,12},{1,13},{2,14},{3,15},{4,8},{5,9},{6,10},{7,11},{8,4},{9,5},... | collective-permute-start | bytes 245768 | tf_op jit(solution)/shard_map/ppermute | solution.py:21
  126.7 1.5 %collective-permute-start.17 = (bf16[2,160,256]{2,1,0:T(8,128)(2,1)S(1)}, bf16[2,160,256]{2,1,0:T(8,128)(2,1)S(1)}, u32[]{:S(2)}, u32[]{:S(2)}) collective-permute-start(bf16[2,160,256]{2,1,0:T(8,128)(2,1)S(1)} %pad_maximum_fusion.1), channel_id=1, source_target_pairs={{0,1},{1,0},{2,3},{3,2},{4,5},{5,4},{6,7},{7,6},{8,9},{9,8},{10,11... | collective-permute-start | bytes 491528 | tf_op jit(solution)/shard_map/ppermute | solution.py:21
  (9 other events, 14.9 us)
where the time goes:
time: 129 us
  waiting for transfers between devices  57.1 us (44%)
  Pallas kernels  33.2 us (26%)
  starting transfers between devices  23.7 us (18%)
  local copies, waits for them, and re-layouts  11.8 us (9%)
  other arithmetic  3.05 us (2%)
    ppermute x18, waiting for transfers between devices, swap(): return lax.ppermute(block, AXES, [(i, i ^ bits) for i in range(32)])  57.1 us
    pallas_call x5, Pallas kernels, call(): pl.pallas_call(kernel, out_shape=tuple((jax.ShapeDtypeStruct(s, d) for s,...  27.9 us
    ppermute x18, starting transfers between devices, swap(): return lax.ppermute(block, AXES, [(i, i ^ bits) for i in range(32)])  23.7 us
    dynamic_slice x5, local copies, waits for them, and re-layouts, columns(): lax.dynamic_slice_in_dim(x, (g ^ slot) * quarter, quarter, x.ndim - 1)  5.41 us
    pallas_call x1, Pallas kernels, fast_body(): pl.pallas_call(lambda *refs: filters_kernel(rows, modes, *refs), out_shap...  5.24 us
    unnamed x26, local copies, waits for them, and re-layouts  2.73 us
  transfers between devices with their start and end apart: 18, of which 14 were waited for; matrix products, arithmetic and copies ran while one was open for 6% of the time, Pallas kernels for 22%

commit v1 on v0

v1 whole, which is shorter than its diff:
```python
import jax
import jax.numpy as jnp
import ml_dtypes
import numpy as np
from jax import lax
from jax.experimental import pallas as pl
from jax.experimental.pallas import tpu as pltpu
from jax.sharding import PartitionSpec as P

F32 = jnp.float32
BF16 = jnp.bfloat16
AXES = ("ctx", "tp")
GROUP = 4
BIT_CORE, BIT_PART = 1, 16
EARLY = 6
SLOT_BITS = (0, 4, 8, 12)
VMEM = pl.BlockSpec(memory_space=pltpu.VMEM)
SMEM = pl.BlockSpec(memory_space=pltpu.SMEM)


def swap(block, bits):
    return lax.ppermute(block, AXES, [(i, i ^ bits) for i in range(32)])


def homeward(a, b, c):
    route = []
    for i in range(32):
        high, low, y, core = i >> 3 & 1, i >> 2 & 1, i >> 1 & 1, i & 1
        route.append((i, (i & 16) + (core ^ a) * 8 + (low ^ b) * 4 + (y ^ c) * 2 + high))
    return route


def split_const(mat):
    hi = mat.astype(ml_dtypes.bfloat16)
    lo = (mat - hi.astype(np.float64)).astype(ml_dtypes.bfloat16)
    return hi, lo


def odd_dft(size, rows_in):
    freq = 2 * np.pi * (np.arange(size // 2) + 0.5) / size
    ang = freq[:, None] * np.arange(rows_in)
    return np.concatenate([np.cos(ang), -np.sin(ang)], 0)


def odd_idft(size, rows_out):
    freq = 2 * np.pi * (np.arange(size // 2) + 0.5) / size
    ang = np.asarray(rows_out)[:, None] * freq
    return np.concatenate([np.cos(ang), -np.sin(ang)], 1) * (2.0 / size)


def mm(a, b):
    return jnp.dot(a, b, preferred_element_type=F32)


def split(x):
    hi = x.astype(BF16)
    return hi, (x - hi.astype(F32)).astype(BF16)


def mm3(hi, lo, x):
    xh, xl = split(x)
    return mm(hi, xh) + mm(lo, xh) + mm(hi, xl)


def cmul(spec, filt):
    half = spec.shape[0] // 2
    a, b, c, d = spec[:half], spec[half:], filt[:half], filt[half:]
    return jnp.concatenate([a * c - b * d, a * d + b * c], 0)


class View:
    def __init__(self, ref, top, high, wide):
        self.ref, self.top, self.high, self.wide = ref, top, high, wide

    def __getitem__(self, key):
        wide = self.wide if key is Ellipsis else key[1].stop
        return self.ref[self.top:self.top + self.high, :wide]


def views(consts, rows, size):
    out, top = [], 0
    for high, wide in ((size, size), (2 * rows, size), (2 * rows, rows), (rows, 2 * rows)):
        for _ in range(2):
            out.append(View(consts, top, high, wide))
            top += high
    return out


def params(**kw):
    return pltpu.CompilerParams(vmem_limit_bytes=16 * 1024 * 1024, **kw)


def filters_kernel(rows, modes, g_ref, taps_ref, rate_all, angle_all, res_all, skip_all, short_all, consts,
                   spec_ref, lspec_ref, qre_ref, qim_ref, par_ref, short_ref):
    width = spec_ref.shape[1]
    ntap = taps_ref.shape[0]
    cmh, cml, _, _, clh, cll, _, _ = views(consts, rows, spec_ref.shape[0])
    at = pl.ds(pl.multiple_of(g_ref[0] * width, width), width)
    spec_ref[...] = mm3(cmh[:, :ntap], cml[:, :ntap], taps_ref[:, at])
    short_ref[...] = short_all[:, :, at]
    rate_ref, angle_ref, res_ref, skip_ref = rate_all[:, at], angle_all[:, at], res_all[:, :, at], skip_all[:, at]
    rate, angle = rate_ref[...], angle_ref[...]
    amp = jnp.sqrt(1.0 - jnp.exp(-2.0 * rate))
    rre, rim = res_ref[0] * amp, res_ref[1] * amp

    def power(n):
        mag = jnp.exp(-rate * n)
        return mag * jnp.cos(angle * n), mag * jnp.sin(angle * n)

    p1, p8, pend = power(1.0), power(8.0), power(float(rows))
    par_ref[0], par_ref[1] = rre * p1[0] - rim * p1[1], rre * p1[1] + rim * p1[0]
    par_ref[2], par_ref[3] = pend
    steps = lax.broadcasted_iota(jnp.int32, (8, width), 0).astype(F32)
    filt = [jnp.zeros((8, width), F32) for _ in range(rows // 8)]
    for m in range(modes):
        ang = angle[m:m + 1] * steps
        mag = jnp.exp(-rate[m:m + 1] * steps)
        cre, cim = mag * jnp.cos(ang), mag * jnp.sin(ang)
        sre, sim = p8[0][m:m + 1], p8[1][m:m + 1]
        wre, wim = rre[m:m + 1], rim[m:m + 1]
        for j in range(rows // 8):
            qre_ref[m, j * 8:j * 8 + 8] = cre
            qim_ref[m, j * 8:j * 8 + 8] = cim
            filt[j] = filt[j] + wre * cre - wim * cim
            cre, cim = cre * sre - cim * sim, cre * sim + cim * sre
    first = lax.broadcasted_iota(jnp.int32, (8, width), 0) == 0
    filt[0] = filt[0] + jnp.where(first, skip_ref[...], 0.0)
    lspec_ref[...] = mm3(clh[...], cll[...], jnp.concatenate(filt, 0))


def prepare_kernel(rows, g_ref, x_ref, t_ref, o0, o1, o2, o3, kx, vx, gate):
    outs = (o0, o1, o2, o3)
    g = g_ref[0]
    quarter = o0.shape[1]
    for lt in range(x_ref.shape[2] // 128):
        ls = slice(lt * 128, lt * 128 + 128)
        for src, ext in ((1, kx), (2, vx)):
            ext[lt, :8] = jnp.zeros((8, 128), F32)
            ext[lt, 8:] = x_ref[src, :, ls].astype(F32)
        tk = [jnp.broadcast_to(t_ref[1, j:j + 1, ls], (8, 128)) for j in range(7)]
        tv = [jnp.broadcast_to(t_ref[2, j:j + 1, ls], (8, 128)) for j in range(7)]
        for r in range(0, rows, 16):
            both = []
            for h in (0, 8):
                sk, sv = tk[0] * kx[lt, 8 + r + h:16 + r + h], tv[0] * vx[lt, 8 + r + h:16 + r + h]
                for j in range(1, 7):
                    o = 8 + r + h - j
                    sk, sv = sk + tk[j] * kx[lt, o:o + 8], sv + tv[j] * vx[lt, o:o + 8]
                both.append(sk * sv)
            gate[r:r + 16, ls] = jnp.concatenate(both, 0).astype(BF16)
    for m, out in enumerate(outs):
        at = pl.ds(pl.multiple_of((g ^ m) * quarter, quarter), quarter)
        out[:rows] = gate[:, at]
        out[rows:2 * rows] = x_ref[0, :, at]
        for i in (1, 2):
            ends = [x_ref[i, :16, at].astype(F32)[:8], x_ref[i, rows - 16:, at].astype(F32)[8:]]
            row = 2 * rows + 16 * (i - 1)
            out[row:row + 16] = jnp.concatenate(ends, 0).astype(BF16)


def first_gates(before, ends, taps):
    out = []
    for i in (0, 1):
        ext = jnp.concatenate([before[16 * i + 8:16 * i + 16], ends[16 * i:16 * i + 8]], 0)
        t = taps[1 + i]
        acc = t[0:1] * ext[8:16]
        for j in range(1, 7):
            acc = acc + t[j:j + 1] * ext[8 - j:16 - j]
        out.append(acc)
    return out[0] * out[1]


def tail_part(tail, taps):
    ext = jnp.concatenate([tail, jnp.zeros_like(tail)], 0)
    out = taps[1:2] * ext[7:15]
    for lag in range(2, 7):
        out = out + taps[lag:lag + 1] * ext[8 - lag:16 - lag]
    return out


def end_states(rows, modes, per, flip, blocks, qre_ref, qim_ref, er, ei, width):
    for lt in range(width // 128):
        ls = slice(lt * 128, lt * 128 + 128)
        for m0 in range(0, modes, per):
            def step(j, acc):
                at = pl.ds(pl.multiple_of(j * 8, 8), 8)
                x = [flip[b, at, ls] for b in blocks]
                out = []
                for i in range(per):
                    qr, qi = qre_ref[m0 + i, at, ls], qim_ref[m0 + i, at, ls]
                    for b in range(len(blocks)):
                        k = (i * len(blocks) + b) * 2
                        out += [acc[k] + x[b] * qr, acc[k + 1] + x[b] * qi]
                return tuple(out)
            acc = lax.fori_loop(0, rows // 8, step, (jnp.zeros((8, 128), F32),) * (2 * len(blocks) * per), unroll=4)
            for i in range(per):
                for b in range(len(blocks)):
                    k = (i * len(blocks) + b) * 2
                    er[b, m0 + i:m0 + i + 1, ls] = jnp.sum(acc[k], 0, keepdims=True)
                    ei[b, m0 + i:m0 + i + 1, ls] = jnp.sum(acc[k + 1], 0, keepdims=True)


def medium_of(gates, spec, cmh, cml, imh, iml):
    return mm3(imh[...], iml[...], cmul(mm(cmh[...], gates) + mm(cml[...], gates), spec))


def medium_kernel(rows, modes, g_ref, t_ref, spec_ref, qre_ref, qim_ref, par_ref,
                  consts, q0, q1, q2, q3,
                  med_ref, st_ref, out_ref, rim_ref, gate_ref, ends_ref, gx, flip, er, ei, ends):
    g = g_ref[0]
    cmh, cml, imh, iml = views(consts, rows, spec_ref.shape[0])[:4]
    width = gate_ref.shape[1]
    gx[:128] = jnp.zeros_like(gx[:128])
    for m, msg in enumerate((q0, q1, q2, q3)):
        gx[pl.ds(pl.multiple_of(128 + (g ^ m) * rows, 16), rows), :] = msg[:rows]
        ends[g ^ m] = msg[2 * rows:2 * rows + 32].astype(F32)
    gate_ref[...] = gx[128:128 + rows]
    ends_ref[...] = ends[0]
    rim_ref[:128] = gx[GROUP * rows:]
    rim_ref[128:160] = ends[GROUP - 1].astype(BF16)
    for b in range(1, GROUP):
        top = 128 + b * rows
        head = first_gates(ends[b - 1], ends[b], t_ref)
        gx[top:top + 16] = jnp.concatenate([head, gx[top:top + 16].astype(F32)[8:]], 0).astype(BF16)
    for b in range(GROUP):
        both = medium_of(gx[b * rows:b * rows + rows + 128], spec_ref[...], cmh, cml, imh, iml)
        med_ref[b] = both[:rows]
        flip[b] = both[rows:]
    end_states(rows, modes, 4, flip, range(GROUP), qre_ref, qim_ref, er, ei, width)
    dre, dim = par_ref[2], par_ref[3]
    sre = jnp.zeros((modes, width), F32)
    sim = sre
    for b in range(GROUP):
        st_ref[b, 0], st_ref[b, 1] = er[b], ei[b]
        sre, sim = dre * sre - dim * sim + er[b], dre * sim + dim * sre + ei[b]
    out_ref[:modes] = sre
    out_ref[modes:2 * modes] = sim
    for m, q in enumerate((q0, q1, q2, q3)):
        @pl.when((g ^ m) == GROUP - 1)
        def _():
            out_ref[2 * modes:] = q[2 * rows - 16:2 * rows].astype(F32)[8:]


def intra_kernel(rows, g_ref, t_ref, med_ref, lspec_ref, consts, q0, q1, q2, q3, intra_ref, query_ref, qx):
    g = g_ref[0]
    _, _, _, _, clh, cll, ilh, ill = views(consts, rows, med_ref.shape[1] + 128)
    for b in range(1, GROUP):
        intra_ref[b - 1] = mm3(ilh[...], ill[...], cmul(mm3(clh[...], cll[...], med_ref[b]), lspec_ref[...]))
    total = GROUP * rows
    for lt in range(query_ref.shape[1] // 128):
        ls = slice(lt * 128, lt * 128 + 128)
        qx[lt, :8] = jnp.zeros((8, 128), F32)
        for m, q in enumerate((q0, q1, q2, q3)):
            qx[lt, pl.ds(pl.multiple_of((g ^ m) * rows + 8, 8), rows), :] = q[rows:2 * rows, ls].astype(F32)
        t = [jnp.broadcast_to(t_ref[0, j:j + 1, ls], (8, 128)) for j in range(7)]
        for r in range(0, total, 8):
            acc = t[0] * qx[lt, 8 + r:16 + r]
            for j in range(1, 7):
                acc = acc + t[j] * qx[lt, 8 + r - j:16 + r - j]
            query_ref[r:r + 8, ls] = acc


def hidden_kernel(rows, modes, g_ref, t_ref, in_ref, rim_ref, gate_ref, ends_ref, spec_ref, lspec_ref, st_ref, par_ref,
                  qre_ref, qim_ref, later_ref, query_ref, consts,
                  hid_ref, amp, gx, flip, er, ei, intra):
    part = g_ref[1]
    live = (part > 0).astype(F32)
    width = query_ref.shape[1]
    cmh, cml, imh, iml, clh, cll, ilh, ill = views(consts, rows, gx.shape[0])
    gx[:128] = (rim_ref[:128].astype(F32) * live).astype(BF16)
    head = first_gates(rim_ref[128:160].astype(F32) * live, ends_ref[...], t_ref)
    gx[128:] = gate_ref[...]
    gx[128:144] = jnp.concatenate([head, gate_ref[:16].astype(F32)[8:]], 0).astype(BF16)
    both = medium_of(gx[...], spec_ref[...], cmh, cml, imh, iml)
    flip[0] = both[rows:]
    intra[0] = mm3(ilh[...], ill[...], cmul(mm3(clh[...], cll[...], both[:rows]), lspec_ref[...]))
    end_states(rows, modes, 8, flip, range(1), qre_ref, qim_ref, er, ei, width)
    sre, sim = in_ref[:modes] * live, in_ref[modes:2 * modes] * live
    rre, rim, dre, dim = par_ref[0], par_ref[1], par_ref[2], par_ref[3]
    for b in range(GROUP):
        are, aim = rre * sre - rim * sim, rre * sim + rim * sre
        for m in range(modes):
            amp[b, m, 0] = jnp.broadcast_to(are[m:m + 1], (8, width))
            amp[b, m, 1] = jnp.broadcast_to(aim[m:m + 1], (8, width))
        ere, eim = (er[0], ei[0]) if b == 0 else (st_ref[b, 0], st_ref[b, 1])
        sre, sim = dre * sre - dim * sim + ere, dre * sim + dim * sre + eim
    query_ref[:8] = query_ref[:8] + tail_part(in_ref[2 * modes:] * live, t_ref[0])
    for lt in range(width // 128):
        ls = slice(lt * 128, lt * 128 + 128)

        def step(j, carry):
            at = [pl.ds(pl.multiple_of(j * 16 + 8 * i, 8), 8) for i in range(2)]
            acc = [[intra[0, at[i], ls] for i in range(2)]]
            acc += [[later_ref[b, at[i], ls] for i in range(2)] for b in range(GROUP - 1)]
            for m in range(modes):
                qr = [qre_ref[m, at[i], ls] for i in range(2)]
                qi = [qim_ref[m, at[i], ls] for i in range(2)]
                for b in range(GROUP):
                    ar, ai = amp[b, m, 0, :, ls], amp[b, m, 1, :, ls]
                    for i in range(2):
                        acc[b][i] = acc[b][i] + ar * qr[i] - ai * qi[i]
            for b in range(GROUP):
                row = pl.multiple_of(b * rows + j * 16, 16)
                long = jnp.concatenate(acc[b], 0)
                hid_ref[pl.ds(row, 16), ls] = (query_ref[pl.ds(row, 16), ls] * long).astype(BF16)
            return carry

        lax.fori_loop(0, rows // 16, step, 0)


def project_kernel(g_ref, h0, h1, h2, h3, wa_ref, *rest):
    far, (keep_ref, send_ref, wb_ref) = rest[:-3], rest[-3:]
    g, same, core = g_ref[0], g_ref[2], g_ref[3]
    quarter = h0.shape[1]
    half = wa_ref.shape[1] // 2
    top = 0
    for part in far:
        wb_ref[top:top + part.shape[0]] = part[...]
        top += part.shape[0]
    mine = pl.ds(pl.multiple_of(core * half, half), half)
    other = pl.ds(pl.multiple_of((1 - core) * half, half), half)
    accs = [None] * 4
    for m, h in enumerate((h0, h1, h2, h3)):
        at = pl.ds(pl.multiple_of((g ^ m) * quarter, quarter), quarter)
        x = h[...]
        for n, cols in enumerate((mine, other)):
            a, b = wa_ref[at, cols], wb_ref[at, cols]
            for k, w in enumerate((a, b)):
                d = mm(x, w)
                accs[2 * k + n] = d if m == 0 else accs[2 * k + n] + d
    own = same > 0
    keep_ref[0] = jnp.where(own, accs[0], accs[2])
    keep_ref[1] = jnp.where(own, accs[2], accs[0])
    send_ref[0] = jnp.where(own, accs[1], accs[3]).astype(BF16)
    send_ref[1] = jnp.where(own, accs[3], accs[1]).astype(BF16)


def sort_kernel(rows, g_ref, keep_ref, got_ref, *outs):
    low, core = g_ref[4], g_ref[3]
    for n, out in enumerate(outs):
        a, b, c = n >> 2 & 1, n >> 1 & 1, n & 1
        block = 2 * (core ^ a) + (low ^ b)
        at = pl.ds(pl.multiple_of(block * rows, rows), rows)
        out[...] = (keep_ref[c, at, :] + got_ref[c, at, :].astype(F32)).astype(BF16)


def gather_kernel(g_ref, *refs):
    out_ref = refs[-1]
    low, high = g_ref[4], g_ref[5]
    width = refs[0].shape[1]
    for n in range(4):
        a, b = n >> 1, n & 1
        at = pl.ds(pl.multiple_of((2 * (low ^ b) + (high ^ a)) * width, width), width)
        out_ref[:, at] = (refs[2 * n][...].astype(F32) + refs[2 * n + 1][...].astype(F32)).astype(BF16)


def call(us, kernel, outs, args, scratch=()):
    return pl.pallas_call(
        kernel,
        out_shape=tuple(jax.ShapeDtypeStruct(s, d) for s, d in outs),
        in_specs=[SMEM] + [VMEM] * (len(args) - 1),
        out_specs=(VMEM,) * len(outs),
        scratch_shapes=[pltpu.VMEM(s, d) for s, d in scratch],
        compiler_params=params(),
        cost_estimate=pl.CostEstimate(flops=int(us * 1.15e9), bytes_accessed=int(us * 3.69e6), transcendentals=0),
    )(*args)


def fast_body(streams, short_taps, mix_taps, pole_rate, pole_angle, residue, skip, out_weight):
    rows, _, width = streams.shape
    modes = pole_rate.shape[0]
    ntap = mix_taps.shape[0]
    quarter = width // GROUP
    total = GROUP * rows
    ctx, tp = lax.axis_index("ctx"), lax.axis_index("tp")
    g, part = ctx % GROUP, ctx // GROUP
    core, y = tp % 2, tp // 2
    scal = jnp.stack([g, part, (y == part).astype(jnp.int32), core, g % 2, g // 2]).astype(jnp.int32)

    cut = width * EARLY // 16
    size_m = rows + ntap
    back = np.concatenate([np.arange(ntap, size_m), np.arange(ntap, size_m)[::-1]])
    mats = [odd_dft(size_m, size_m), odd_idft(size_m, back), odd_dft(2 * rows, rows), odd_idft(2 * rows, np.arange(rows))]
    consts = np.concatenate([
        np.pad(half, ((0, 0), (0, 2 * rows - half.shape[1]))) for mat in mats for half in split_const(mat)], 0)

    short_taps = short_taps.transpose(1, 0, 2)
    msgs = call(
        1.5,
        lambda *refs: prepare_kernel(rows, *refs),
        [((2 * rows + 32, quarter), BF16)] * GROUP,
        (scal, streams.transpose(1, 0, 2), short_taps),
        [((width // 128, rows + 8, 128), F32)] * 2 + [((rows, width), BF16)],
    )
    ahead, msgs = lax.optimization_barrier((out_weight[:cut], msgs))
    early = swap(ahead, BIT_PART)
    msgs = [msgs[0]] + [swap(msgs[m], SLOT_BITS[m]) for m in (1, 2, 3)]
    spec, lspec, qre, qim, par, taps = call(
        2.5,
        lambda *refs: filters_kernel(rows, modes, *refs),
        [(s, F32) for s in ((size_m, quarter), (2 * rows, quarter), (modes, rows, quarter), (modes, rows, quarter),
                            (4, modes, quarter), (3, 7, quarter))],
        (scal, mix_taps, pole_rate, pole_angle, residue, skip[None], short_taps, consts),
    )
    med, st, out, rim, gate, ends = call(
        5.4,
        lambda *refs: medium_kernel(rows, modes, *refs),
        [((GROUP, rows, quarter), F32), ((GROUP, 2, modes, quarter), F32), ((2 * modes + 8, quarter), F32),
         ((160, quarter), BF16), ((rows, quarter), BF16), ((32, quarter), F32)],
        (scal, taps, spec, qre, qim, par, consts, *msgs),
        [((total + 128, quarter), BF16), ((GROUP, rows, quarter), F32), ((GROUP, modes, quarter), F32), ((GROUP, modes, quarter), F32),
         ((GROUP, 32, quarter), F32)],
    )
    out, rim, early = lax.optimization_barrier((out, rim, early))
    state_in, rim_in = swap(out, BIT_PART), swap(rim, BIT_PART)
    late, state_in, rim_in = lax.optimization_barrier((out_weight[cut:], state_in, rim_in))
    far_weight = [early, swap(late, BIT_PART)]
    later, query = call(
        3.1,
        lambda *refs: intra_kernel(rows, *refs),
        [((GROUP - 1, rows, quarter), F32), ((total, quarter), F32)],
        (scal, taps, med, lspec, consts, *msgs),
        [((quarter // 128, total + 8, 128), F32)],
    )
    (hidden,) = call(
        5.2,
        lambda *refs: hidden_kernel(rows, modes, *refs),
        [((total, quarter), BF16)],
        (scal, taps, state_in, rim_in, gate, ends, spec, lspec, st, par, qre, qim, later, query, consts),
        [((GROUP, modes, 2, 8, quarter), F32), ((rows + 128, quarter), BF16), ((1, rows, quarter), F32),
         ((1, modes, quarter), F32), ((1, modes, quarter), F32), ((1, rows, quarter), F32)],
    )
    hid = [hidden] + [swap(hidden, SLOT_BITS[m]) for m in (1, 2, 3)]
    half = out_weight.shape[1] // 2
    keep, send = call(
        2.2,
        project_kernel,
        [((2, total, half), F32), ((2, total, half), BF16)],
        (scal, *hid, out_weight, *far_weight),
        [((width, 2 * half), BF16)],
    )
    blocks = call(
        0.7,
        lambda *refs: sort_kernel(rows, *refs),
        [((rows, half), BF16)] * 8,
        (scal, keep, swap(send, BIT_CORE)),
    )
    blocks = [lax.ppermute(block, AXES, homeward(n >> 2 & 1, n >> 1 & 1, n & 1)) for n, block in enumerate(blocks)]
    (mixed,) = call(1.3, gather_kernel, [((rows, 4 * half), BF16)], (scal, *blocks))
    return mixed


def from_behind(block, axis, distance):
    devices = range(lax.axis_size(axis))
    route = [(i - distance, i) for i in devices if i - distance in devices]
    return lax.ppermute(block, axis, route)


def depthwise(ext, taps):
    width = taps.shape[1]
    kernel = taps[::-1][:, None, :]
    out = lax.conv_general_dilated(
        ext[None],
        kernel,
        (1,),
        "VALID",
        dimension_numbers=("NWC", "WIO", "NWC"),
        feature_group_count=width,
        precision=lax.Precision.HIGHEST,
    )
    return out[0]


def general_body(streams, short_taps, mix_taps, pole_rate, pole_angle, residue, skip, out_weight):
    rows, three, width = streams.shape
    modes = pole_rate.shape[0]
    short = short_taps.reshape(7, three * width)
    rim = from_behind(streams[rows - 6 :], "ctx", 1)
    ext = jnp.concatenate([rim, streams], 0).astype(jnp.float32).reshape(rows + 6, three * width)
    conv = depthwise(ext, short).reshape(rows, three, width)
    gate = (conv[:, 1] * conv[:, 2]).astype(jnp.bfloat16)
    gate_rim = from_behind(gate[rows - 127 :], "ctx", 1)
    gate_ext = jnp.concatenate([gate_rim, gate], 0)
    query = conv[:, 0]
    medium = depthwise(gate_ext.astype(jnp.float32), mix_taps)
    amp = jnp.sqrt(1.0 - jnp.exp(-2.0 * pole_rate))
    res_re = residue[0] * amp
    res_im = residue[1] * amp
    steps = jnp.arange(rows).astype(jnp.float32)[:, None]
    flipped = medium[::-1]

    def first_pass(mode, carry):
        filt, end_re, end_im = carry
        rate = pole_rate[mode][None]
        angle = pole_angle[mode][None]
        mag = jnp.exp(-rate * steps)
        cosk = mag * jnp.cos(angle * steps)
        sink = mag * jnp.sin(angle * steps)
        filt = filt + res_re[mode][None] * cosk - res_im[mode][None] * sink
        end_re = end_re.at[mode].set(jnp.sum(flipped * cosk, 0))
        end_im = end_im.at[mode].set(jnp.sum(flipped * sink, 0))
        return (filt, end_re, end_im)

    zero_state = jnp.zeros((modes, width), jnp.float32)
    filt, end_re, end_im = lax.fori_loop(
        0, modes, first_pass, (jnp.zeros((rows, width), jnp.float32), zero_state, zero_state)
    )
    dec_mag = jnp.exp(-pole_rate * rows)
    dec_re = dec_mag * jnp.cos(pole_angle * rows)
    dec_im = dec_mag * jnp.sin(pole_angle * rows)

    def relay_step(turn, received):
        in_re, in_im = received
        out_re = dec_re * in_re - dec_im * in_im + end_re
        out_im = dec_re * in_im + dec_im * in_re + end_im
        return from_behind((out_re, out_im), "ctx", 1)

    st_re, st_im = lax.fori_loop(0, lax.axis_size("ctx") - 1, relay_step, (zero_state, zero_state))
    later = steps + 1.0

    def second_pass(mode, inflow):
        rate = pole_rate[mode][None]
        angle = pole_angle[mode][None]
        mag = jnp.exp(-rate * later)
        cos1 = mag * jnp.cos(angle * later)
        sin1 = mag * jnp.sin(angle * later)
        are = res_re[mode] * st_re[mode] - res_im[mode] * st_im[mode]
        aim = res_re[mode] * st_im[mode] + res_im[mode] * st_re[mode]
        return inflow + are[None] * cos1 - aim[None] * sin1

    inflow = lax.fori_loop(0, modes, second_pass, jnp.zeros((rows, width), jnp.float32))
    padded = jnp.concatenate([jnp.zeros((rows - 1, width), jnp.float32), medium], 0)
    intra = depthwise(padded, filt)
    longf = intra + inflow + skip[None] * medium
    hidden = (query * longf).astype(jnp.bfloat16)
    partial_out = jnp.dot(
        hidden,
        lax.all_gather(out_weight, "ctx", axis=1, tiled=True),
        preferred_element_type=jnp.float32,
    )
    return lax.psum_scatter(partial_out, "tp", scatter_dimension=1, tiled=True).astype(jnp.bfloat16)


def solution(mesh):
    fast = dict(mesh.shape) == {"ctx": 8, "tp": 4}
    return jax.shard_map(
        fast_body if fast else general_body,
        mesh=mesh,
        in_specs=(
            P("ctx", None, "tp"),
            P(None, None, "tp"),
            P(None, "tp"),
            P(None, "tp"),
            P(None, "tp"),
            P(None, None, "tp"),
            P("tp"),
            P("tp", "ctx"),
        ),
        out_specs=P("ctx", "tp"),
        check_vma=False,
    )
```

time: 129 us -> 95.3 us (0.74)
  waiting for transfers between devices: 57.1 us -> 43.6 us
  Pallas kernels: 33.2 us -> 21 us
  local copies, waits for them, and re-layouts: 11.8 us -> 3.28 us
  starting transfers between devices: 23.7 us -> 27 us
  other arithmetic: 3.05 us -> 0 us
    ppermute x18 -> x11, waiting for transfers between devices: 57.1 us -> 38.6 us  [swap(): return lax.ppermute(block, AXES, [(i, i ^ bits) for i in range(32)])]
    ppermute x0 -> x8, starting transfers between devices: none -> 11.4 us  [fast_body(): lax.ppermute(block, AXES, homeward(n >> 2 & 1, n >> 1 & 1, n & 1))]
    ppermute x18 -> x11, starting transfers between devices: 23.7 us -> 15.6 us  [swap(): return lax.ppermute(block, AXES, [(i, i ^ bits) for i in range(32)])]
    pallas_call x5 -> x8, Pallas kernels: 27.9 us -> 21 us  [call(): pl.pallas_call(kernel, out_shape=tuple((jax.ShapeDtypeStruct(s, d) for s,...]
    dynamic_slice x6 -> x0, local copies, waits for them, and re-layouts: 5.42 us -> none  [the longest x5 5.41 us: columns(): lax.dynamic_slice_in_dim(x, (g ^ slot) * quarter, quarter, x.ndim - 1)]
    pallas_call x1 -> x0, Pallas kernels: 5.24 us -> none  [fast_body(): pl.pallas_call(lambda *refs: filters_kernel(rows, modes, *refs), out_shap...]
    ppermute x0 -> x8, waiting for transfers between devices: none -> 5.01 us  [fast_body(): lax.ppermute(block, AXES, homeward(n >> 2 & 1, n >> 1 & 1, n & 1))]
    transpose x2 -> x0, local copies, waits for them, and re-layouts: 2.09 us -> none  [the longest x1 1.35 us: fast_body(): taps = columns(short_taps).transpose(1, 0, 2)]
  transfers between devices with their start and end apart: 18 -> 19, of which waited for: 14 -> 10; matrix products, arithmetic and copies ran while one was open for 6% -> 0% of each run, Pallas kernels for 22% -> 16%
where the time goes in v1:
time: 95.3 us; the launch traced here: 95.1 us
  waiting for transfers between devices  43.6 us (46%)
  starting transfers between devices  27 us (28%)
  Pallas kernels  21 us (22%)
  local copies, waits for them, and re-layouts  3.28 us (3%)
    ppermute x11, waiting for transfers between devices, swap(): return lax.ppermute(block, AXES, [(i, i ^ bits) for i in range(32)])  38.6 us
    pallas_call x8, Pallas kernels, call(): pl.pallas_call(kernel, out_shape=tuple((jax.ShapeDtypeStruct(s, d) for s,...  21 us
    ppermute x11, starting transfers between devices, swap(): return lax.ppermute(block, AXES, [(i, i ^ bits) for i in range(32)])  15.6 us
    ppermute x8, starting transfers between devices, fast_body(): lax.ppermute(block, AXES, homeward(n >> 2 & 1, n >> 1 & 1, n & 1))  11.4 us
    ppermute x8, waiting for transfers between devices, fast_body(): lax.ppermute(block, AXES, homeward(n >> 2 & 1, n >> 1 & 1, n & 1))  5.01 us
    unnamed x18, local copies, waits for them, and re-layouts  2.13 us
  transfers between devices with their start and end apart: 19, of which 10 were waited for; matrix products, arithmetic and copies ran while one was open for 0% of the time, Pallas kernels for 16%

profile of v1, /device:TPU:0, one launch (start us, length us, event | category | flops | bytes accessed | tf_op | source)
XLA Modules:
  0.0 95.1 jit_solution(4700081277657980143)
XLA Ops:
  3.3 1.4 %shard_map.92 = (bf16[352,256]{1,0:T(8,128)(2,1)S(1)}, bf16[352,256]{1,0:T(8,128)(2,1)S(1)}, bf16[352,256]{1,0:T(8,128)(2,1)S(1)}, bf16[352,256]{1,0:T(8,128)(2,1)S(1)}) custom-call(s32[6]{0:T(128)S(1)} %stack.31.refs_0_.g_ref, bf16[3,160,1024]{2,1,0:T(8,128)(2,1)S(1)} %bitcast.9, f32[3,7,1024]{2,1,0:T(8,128)S(1)} %bitcast.10), custom_call_target="tpu_custom_call" | custom-call | flops 1724999936 | bytes 5535000 | tf_op jit(solution)/shard_map/pallas_call | solution.py:358
  4.7 3.0 %collective-permute-start = (bf16[352,256]{1,0:T(8,128)(2,1)S(1)}, bf16[352,256]{1,0:T(8,128)(2,1)S(1)}, u32[]{:S(2)}, u32[]{:S(2)}) collective-permute-start(bf16[352,256]{1,0:T(8,128)(2,1)S(1)} %get-tuple-element.54), channel_id=1, source_target_pairs={{0,4},{1,5},{2,6},{3,7},{4,0},{5,1},{6,2},{7,3},{8,12},{9,13},{10,... | collective-permute-start | bytes 540680 | tf_op jit(solution)/shard_map/ppermute | solution.py:22
  7.7 1.6 %collective-permute-start.1 = (bf16[352,256]{1,0:T(8,128)(2,1)S(1)}, bf16[352,256]{1,0:T(8,128)(2,1)S(1)}, u32[]{:S(2)}, u32[]{:S(2)}) collective-permute-start(bf16[352,256]{1,0:T(8,128)(2,1)S(1)} %get-tuple-element.55), channel_id=1, source_target_pairs={{0,8},{1,9},{2,10},{3,11},{4,12},{5,13},{6,14},{7,15},{8,0},{9,1},... | collective-permute-start | bytes 540680 | tf_op jit(solution)/shard_map/ppermute | solution.py:22
  9.3 3.0 %collective-permute-start.3 = (bf16[384,512]{1,0:T(8,128)(2,1)S(1)}, bf16[384,512]{1,0:T(8,128)(2,1)S(1)}, u32[]{:S(2)}, u32[]{:S(2)}) collective-permute-start(bf16[384,512]{1,0:T(8,128)(2,1)S(1)} %slice.7), channel_id=1, source_target_pairs={{0,16},{1,17},{2,18},{3,19},{4,20},{5,21},{6,22},{7,23},{8,24},{9,... | collective-permute-start | bytes 1179656 | tf_op jit(solution)/shard_map/ppermute | solution.py:22
  12.4 2.6 %shard_map.91 = (f32[288,256]{1,0:T(8,128)S(1)}, f32[320,256]{1,0:T(8,128)S(1)}, f32[16,160,256]{2,1,0:T(8,128)S(1)}, f32[16,160,256]{2,1,0:T(8,128)S(1)}, f32[4...) custom-call(s32[6]{0:T(128)S(1)} %stack.31.refs_0_.g_ref, f32[128,1024]{1,0:T(8,128)S(1)} %copy-done.2, ...), custom_call_target="tpu_custom_call" | custom-call | flops 2875000064 | bytes 9225000 | tf_op jit(solution)/shard_map/pallas_call | solution.py:358
  15.0 7.7 %collective-permute-done.1.refs_9_.refs_7_ = bf16[352,256]{1,0:T(8,128)(2,1)S(1)} collective-permute-done((bf16[352,256]{1,0:T(8,128)(2,1)S(1)}, bf16[352,256]{1,0:T(8,128)(2,1)S(1)}, u32[]{:S(2)}, u32[]{:S(2)}) %collective-permute-start.1) | collective-permute-done | bytes 180256 | tf_op jit(solution)/shard_map/ppermute | solution.py:22
  23.9 5.4 %shard_map.93 = (f32[4,160,256]{2,1,0:T(8,128)S(1)}, f32[4,2,16,256]{3,2,1,0:T(8,128)S(1)}, f32[40,256]{1,0:T(8,128)S(1)}, bf16[160,256]{1,0:T(8,128)(2,1)S(1)},...) custom-call(s32[6]{0:T(128)S(1)} %stack.31.refs_0_.g_ref, f32[3,7,256]{2,1,0:T(8,128)S(1)} %get-tuple-element.44.refs_1_, ...), custom_call_target="tpu_custom_call" | custom-call | flops 6209999872 | bytes 19926000 | tf_op jit(solution)/shard_map/pallas_call | solution.py:358
  30.0 2.3 %collective-permute-start.4 = (f32[40,256]{1,0:T(8,128)S(1)}, f32[40,256]{1,0:T(8,128)S(1)}, u32[]{:S(2)}, u32[]{:S(2)}) collective-permute-start(f32[40,256]{1,0:T(8,128)S(1)} %get-tuple-element.60), channel_id=1, source_target_pairs={{0,16},{1,17},{2,18},{3,19},{4,20},{5,21},{6,22},{7,23},{8,24},{9,... | collective-permute-start | bytes 122888 | tf_op jit(solution)/shard_map/ppermute | solution.py:22
  32.3 2.2 %shard_map.94 = (f32[3,160,256]{2,1,0:T(8,128)S(1)}, f32[640,256]{1,0:T(8,128)S(1)}) custom-call(s32[6]{0:T(128)S(1)} %stack.31.refs_0_.g_ref, f32[3,7,256]{2,1,0:T(8,128)S(1)} %get-tuple-element.44.refs_1_, f32[4,160,256]{2,1,0:T(8,128)S(1)} %get-tuple-element.68.refs_2_, f32[320,256]{1,0:T(8,128)S(1)} %get-tuple-element.66.refs_3_.refs_7_, ...), custom_call_target="tpu_custom_call" | custom-call | flops 3564999936 | bytes 11439000 | tf_op jit(solution)/shard_map/pallas_call | solution.py:358
  34.5 2.0 %collective-permute-done.4.refs_2_ = f32[40,256]{1,0:T(8,128)S(1)} collective-permute-done((f32[40,256]{1,0:T(8,128)S(1)}, f32[40,256]{1,0:T(8,128)S(1)}, u32[]{:S(2)}, u32[]{:S(2)}) %collective-permute-start.4) | collective-permute-done | bytes 40992 | tf_op jit(solution)/shard_map/ppermute | solution.py:22
  37.4 5.3 %shard_map.95.h0 = bf16[640,256]{1,0:T(8,128)(2,1)S(1)} custom-call(s32[6]{0:T(128)S(1)} %stack.31.refs_0_.g_ref, f32[3,7,256]{2,1,0:T(8,128)S(1)} %get-tuple-element.44.refs_1_, f32[40,256]{1,0:T(8,128)S(1)} %collective-permute-done.4.refs_2_, bf16[160,256]{1,0:T(8,128)(2,1)S(1)} %collective-permute-done.5.refs_3_, ...), custom_call_target="tpu_custom_call" | custom-call | flops 5980000256 | bytes 19188000 | tf_op jit(solution)/shard_map/pallas_call | solution.py:358
  42.6 2.6 %collective-permute-start.6 = (bf16[640,256]{1,0:T(8,128)(2,1)S(1)}, bf16[640,256]{1,0:T(8,128)(2,1)S(1)}, u32[]{:S(2)}, u32[]{:S(2)}) collective-permute-start(bf16[640,256]{1,0:T(8,128)(2,1)S(1)} %shard_map.95.h0), channel_id=1, source_target_pairs={{0,4},{1,5},{2,6},{3,7},{4,0},{5,1},{6,2},{7,3},{8,12},{9,13},{10,... | collective-permute-start | bytes 983048 | tf_op jit(solution)/shard_map/ppermute | solution.py:22
  46.8 5.0 %collective-permute-done.6.h1 = bf16[640,256]{1,0:T(8,128)(2,1)S(1)} collective-permute-done((bf16[640,256]{1,0:T(8,128)(2,1)S(1)}, bf16[640,256]{1,0:T(8,128)(2,1)S(1)}, u32[]{:S(2)}, u32[]{:S(2)}) %collective-permute-start.6) | collective-permute-done | bytes 327712 | tf_op jit(solution)/shard_map/ppermute | solution.py:22
  51.8 17.2 %collective-permute-done.7.h2 = bf16[640,256]{1,0:T(8,128)(2,1)S(1)} collective-permute-done((bf16[640,256]{1,0:T(8,128)(2,1)S(1)}, bf16[640,256]{1,0:T(8,128)(2,1)S(1)}, u32[]{:S(2)}, u32[]{:S(2)}) %collective-permute-start.7) | collective-permute-done | bytes 327712 | tf_op jit(solution)/shard_map/ppermute | solution.py:22
  69.0 3.3 %collective-permute-done.8.h3 = bf16[640,256]{1,0:T(8,128)(2,1)S(1)} collective-permute-done((bf16[640,256]{1,0:T(8,128)(2,1)S(1)}, bf16[640,256]{1,0:T(8,128)(2,1)S(1)}, u32[]{:S(2)}, u32[]{:S(2)}) %collective-permute-start.8) | collective-permute-done | bytes 327712 | tf_op jit(solution)/shard_map/ppermute | solution.py:22
  72.4 2.1 %shard_map.96 = (f32[2,640,256]{2,1,0:T(8,128)S(1)}, bf16[2,640,256]{2,1,0:T(8,128)(2,1)S(1)}) custom-call(s32[6]{0:T(128)S(1)} %stack.31.refs_0_.g_ref, bf16[640,256]{1,0:T(8,128)(2,1)S(1)} %shard_map.95.h0, bf16[640,256]{1,0:T(8,128)(2,1)S(1)} %collective-permute-done.6.h1, bf16[640,256]{1,0:T(8,128)(2,1)S(1)} %collective-permute-done.7.h2, ...), custom_call_target="tpu_custom_call" | custom-call | flops 2529999872 | bytes 8118000 | tf_op jit(solution)/shard_map/pallas_call | solution.py:358
  74.6 2.1 %collective-permute-done.10.refs_2_ = bf16[2,640,256]{2,1,0:T(8,128)(2,1)S(1)} collective-permute-done((bf16[2,640,256]{2,1,0:T(8,128)(2,1)S(1)}, bf16[2,640,256]{2,1,0:T(8,128)(2,1)S(1)}, u32[]{:S(2)}, u32[]{:S(2)}) %collective-permute-start.10) | collective-permute-done | bytes 655392 | tf_op jit(solution)/shard_map/ppermute | solution.py:22
  78.0 1.5 %collective-permute-start.12 = (bf16[160,256]{1,0:T(8,128)(2,1)S(1)}, bf16[160,256]{1,0:T(8,128)(2,1)S(1)}, u32[]{:S(2)}, u32[]{:S(2)}) collective-permute-start(bf16[160,256]{1,0:T(8,128)(2,1)S(1)} %get-tuple-element.76), channel_id=1, source_target_pairs={{0,2},{1,10},{2,0},{3,8},{4,6},{5,14},{6,4},{7,12},{8,3},{9,11},{1... | collective-permute-start | bytes 245768 | tf_op jit(solution)/shard_map/ppermute | solution.py:448
  79.5 1.7 %collective-permute-start.13 = (bf16[160,256]{1,0:T(8,128)(2,1)S(1)}, bf16[160,256]{1,0:T(8,128)(2,1)S(1)}, u32[]{:S(2)}, u32[]{:S(2)}) collective-permute-start(bf16[160,256]{1,0:T(8,128)(2,1)S(1)} %get-tuple-element.77), channel_id=1, source_target_pairs={{0,4},{1,12},{2,6},{3,14},{4,0},{5,8},{6,2},{7,10},{8,5},{9,13},{1... | collective-permute-start | bytes 245768 | tf_op jit(solution)/shard_map/ppermute | solution.py:448
  81.5 3.3 %collective-permute-start.15 = (bf16[160,256]{1,0:T(8,128)(2,1)S(1)}, bf16[160,256]{1,0:T(8,128)(2,1)S(1)}, u32[]{:S(2)}, u32[]{:S(2)}) collective-permute-start(bf16[160,256]{1,0:T(8,128)(2,1)S(1)} %get-tuple-element.79), channel_id=1, source_target_pairs={{0,8},{1,0},{2,10},{3,2},{4,12},{5,4},{6,14},{7,6},{8,9},{9,1},{10... | collective-permute-start | bytes 245768 | tf_op jit(solution)/shard_map/ppermute | solution.py:448
  85.7 2.9 %collective-permute-start.17 = (bf16[160,256]{1,0:T(8,128)(2,1)S(1)}, bf16[160,256]{1,0:T(8,128)(2,1)S(1)}, u32[]{:S(2)}, u32[]{:S(2)}) collective-permute-start(bf16[160,256]{1,0:T(8,128)(2,1)S(1)} %get-tuple-element.81), channel_id=1, source_target_pairs={{0,12},{1,4},{2,14},{3,6},{4,8},{5,0},{6,10},{7,2},{8,13},{9,5},{1... | collective-permute-start | bytes 245768 | tf_op jit(solution)/shard_map/ppermute | solution.py:448
  88.7 1.7 %collective-permute-done.16.refs_5_ = bf16[160,256]{1,0:T(8,128)(2,1)S(1)} collective-permute-done((bf16[160,256]{1,0:T(8,128)(2,1)S(1)}, bf16[160,256]{1,0:T(8,128)(2,1)S(1)}, u32[]{:S(2)}, u32[]{:S(2)}) %collective-permute-start.16) | collective-permute-done | bytes 81952 | tf_op jit(solution)/shard_map/ppermute | solution.py:448
  90.7 3.0 %collective-permute-done.18.refs_7_ = bf16[160,256]{1,0:T(8,128)(2,1)S(1)} collective-permute-done((bf16[160,256]{1,0:T(8,128)(2,1)S(1)}, bf16[160,256]{1,0:T(8,128)(2,1)S(1)}, u32[]{:S(2)}, u32[]{:S(2)}) %collective-permute-start.18) | collective-permute-done | bytes 81952 | tf_op jit(solution)/shard_map/ppermute | solution.py:448
  93.7 1.3 %shard_map.98 = bf16[160,1024]{1,0:T(8,128)(2,1)} custom-call(s32[6]{0:T(128)S(1)} %stack.31.refs_0_.g_ref, bf16[160,256]{1,0:T(8,128)(2,1)S(1)} %collective-permute-done.11.refs_0_, bf16[160,256]{1,0:T(8,128)(2,1)S(1)} %collective-permute-done.12.refs_1_, bf16[160,256]{1,0:T(8,128)(2,1)S(1)} %collective-permute-done.13.refs_2_, ...), custom_call_target="tpu_custom_call" | custom-call | flops 1495000064 | bytes 4797000 | tf_op jit(solution)/shard_map/pallas_call | solution.py:358
  (43 shorter events, 10.5 us)
Async XLA Ops:
  3.2 9.1 %copy-start.3 = (f32[2,16,1024]{2,1,0:T(8,128)S(1)}, f32[2,16,1024]{2,1,0:T(8,128)}, u32[]{:S(2)}) copy-start(f32[2,16,1024]{2,1,0:T(8,128)} %refs_4_.2) | copy-start | bytes 393220
  3.2 9.1 %copy-start.5 = (f32[16,1024]{1,0:T(8,128)S(1)}, f32[16,1024]{1,0:T(8,128)}, u32[]{:S(2)}) copy-start(f32[16,1024]{1,0:T(8,128)} %refs_2_.1) | copy-start | bytes 196612
  3.2 9.2 %copy-start.6 = (f32[16,1024]{1,0:T(8,128)S(1)}, f32[16,1024]{1,0:T(8,128)}, u32[]{:S(2)}) copy-start(f32[16,1024]{1,0:T(8,128)} %refs_3_.1) | copy-start | bytes 196612
  3.3 9.2 %copy-start.7 = (f32[1024]{0:T(1024)S(1)}, f32[1024]{0:T(1024)}, u32[]{:S(2)}) copy-start(f32[1024]{0:T(1024)} %param.15) | copy-start | bytes 12292
  3.3 9.1 %copy-start.8 = (bf16[2176,320]{1,0:T(8,128)(2,1)S(1)}, bf16[2176,320]{1,0:T(8,128)(2,1)}, u32[]{:S(2)}) copy-start(bf16[2176,320]{1,0:T(8,128)(2,1)} %constant.64.clone.refs_7_.refs_6_.refs_4_.refs_14_) | copy-start | bytes 4177924
  4.7 10.3 %collective-permute-start = (bf16[352,256]{1,0:T(8,128)(2,1)S(1)}, bf16[352,256]{1,0:T(8,128)(2,1)S(1)}, u32[]{:S(2)}, u32[]{:S(2)}) collective-permute-start(bf16[352,256]{1,0:T(8,128)(2,1)S(1)} %get-tuple-element.54), channel_id=1, source_target_pairs={{0,4},{1,5},{2,6},{3,7},{4,0},{5,1},{6,2},{7,3},{8,12},{9,13},{10,... | collective-permute-start | bytes 540680 | tf_op jit(solution)/shard_map/ppermute | solution.py:22
  7.7 15.0 %collective-permute-start.1 = (bf16[352,256]{1,0:T(8,128)(2,1)S(1)}, bf16[352,256]{1,0:T(8,128)(2,1)S(1)}, u32[]{:S(2)}, u32[]{:S(2)}) collective-permute-start(bf16[352,256]{1,0:T(8,128)(2,1)S(1)} %get-tuple-element.55), channel_id=1, source_target_pairs={{0,8},{1,9},{2,10},{3,11},{4,12},{5,13},{6,14},{7,15},{8,0},{9,1},... | collective-permute-start | bytes 540680 | tf_op jit(solution)/shard_map/ppermute | solution.py:22
  9.3 14.6 %collective-permute-start.2 = (bf16[352,256]{1,0:T(8,128)(2,1)S(1)}, bf16[352,256]{1,0:T(8,128)(2,1)S(1)}, u32[]{:S(2)}, u32[]{:S(2)}) collective-permute-start(bf16[352,256]{1,0:T(8,128)(2,1)S(1)} %get-tuple-element.56), channel_id=1, source_target_pairs={{0,12},{1,13},{2,14},{3,15},{4,8},{5,9},{6,10},{7,11},{8,4},{9,5},... | collective-permute-start | bytes 540680 | tf_op jit(solution)/shard_map/ppermute | solution.py:22
  9.3 20.0 %collective-permute-start.3 = (bf16[384,512]{1,0:T(8,128)(2,1)S(1)}, bf16[384,512]{1,0:T(8,128)(2,1)S(1)}, u32[]{:S(2)}, u32[]{:S(2)}) collective-permute-start(bf16[384,512]{1,0:T(8,128)(2,1)S(1)} %slice.7), channel_id=1, source_target_pairs={{0,16},{1,17},{2,18},{3,19},{4,20},{5,21},{6,22},{7,23},{8,24},{9,... | collective-permute-start | bytes 1179656 | tf_op jit(solution)/shard_map/ppermute | solution.py:22
  29.4 7.2 %collective-permute-start.5 = (bf16[160,256]{1,0:T(8,128)(2,1)S(1)}, bf16[160,256]{1,0:T(8,128)(2,1)S(1)}, u32[]{:S(2)}, u32[]{:S(2)}) collective-permute-start(bf16[160,256]{1,0:T(8,128)(2,1)S(1)} %get-tuple-element.61), channel_id=1, source_target_pairs={{0,16},{1,17},{2,18},{3,19},{4,20},{5,21},{6,22},{7,23},{8,24},{9,... | collective-permute-start | bytes 245768 | tf_op jit(solution)/shard_map/ppermute | solution.py:22
  30.0 6.6 %collective-permute-start.4 = (f32[40,256]{1,0:T(8,128)S(1)}, f32[40,256]{1,0:T(8,128)S(1)}, u32[]{:S(2)}, u32[]{:S(2)}) collective-permute-start(f32[40,256]{1,0:T(8,128)S(1)} %get-tuple-element.60), channel_id=1, source_target_pairs={{0,16},{1,17},{2,18},{3,19},{4,20},{5,21},{6,22},{7,23},{8,24},{9,... | collective-permute-start | bytes 122888 | tf_op jit(solution)/shard_map/ppermute | solution.py:22
  36.6 35.8 %collective-permute-start.9 = (bf16[640,512]{1,0:T(8,128)(2,1)S(1)}, bf16[640,512]{1,0:T(8,128)(2,1)S(1)}, u32[]{:S(2)}, u32[]{:S(2)}) collective-permute-start(bf16[640,512]{1,0:T(8,128)(2,1)S(1)} %slice.6), channel_id=1, source_target_pairs={{0,16},{1,17},{2,18},{3,19},{4,20},{5,21},{6,22},{7,23},{8,24},{9,... | collective-permute-start | bytes 1966088 | tf_op jit(solution)/shard_map/ppermute | solution.py:22
  42.6 9.2 %collective-permute-start.6 = (bf16[640,256]{1,0:T(8,128)(2,1)S(1)}, bf16[640,256]{1,0:T(8,128)(2,1)S(1)}, u32[]{:S(2)}, u32[]{:S(2)}) collective-permute-start(bf16[640,256]{1,0:T(8,128)(2,1)S(1)} %shard_map.95.h0), channel_id=1, source_target_pairs={{0,4},{1,5},{2,6},{3,7},{4,0},{5,1},{6,2},{7,3},{8,12},{9,13},{10,... | collective-permute-start | bytes 983048 | tf_op jit(solution)/shard_map/ppermute | solution.py:22
  45.2 23.8 %collective-permute-start.7 = (bf16[640,256]{1,0:T(8,128)(2,1)S(1)}, bf16[640,256]{1,0:T(8,128)(2,1)S(1)}, u32[]{:S(2)}, u32[]{:S(2)}) collective-permute-start(bf16[640,256]{1,0:T(8,128)(2,1)S(1)} %shard_map.95.h0), channel_id=1, source_target_pairs={{0,8},{1,9},{2,10},{3,11},{4,12},{5,13},{6,14},{7,15},{8,0},{9,1},... | collective-permute-start | bytes 983048 | tf_op jit(solution)/shard_map/ppermute | solution.py:22
  46.1 26.2 %collective-permute-start.8 = (bf16[640,256]{1,0:T(8,128)(2,1)S(1)}, bf16[640,256]{1,0:T(8,128)(2,1)S(1)}, u32[]{:S(2)}, u32[]{:S(2)}) collective-permute-start(bf16[640,256]{1,0:T(8,128)(2,1)S(1)} %shard_map.95.h0), channel_id=1, source_target_pairs={{0,12},{1,13},{2,14},{3,15},{4,8},{5,9},{6,10},{7,11},{8,4},{9,5},... | collective-permute-start | bytes 983048 | tf_op jit(solution)/shard_map/ppermute | solution.py:22
  74.5 2.2 %collective-permute-start.10 = (bf16[2,640,256]{2,1,0:T(8,128)(2,1)S(1)}, bf16[2,640,256]{2,1,0:T(8,128)(2,1)S(1)}, u32[]{:S(2)}, u32[]{:S(2)}) collective-permute-start(bf16[2,640,256]{2,1,0:T(8,128)(2,1)S(1)} %get-tuple-element.74), channel_id=1, source_target_pairs={{0,1},{1,0},{2,3},{3,2},{4,5},{5,4},{6,7},{7,6},{8,9},{9,8},{10,11... | collective-permute-start | bytes 1966088 | tf_op jit(solution)/shard_map/ppermute | solution.py:22
  77.3 7.5 %collective-permute-start.11 = (bf16[160,256]{1,0:T(8,128)(2,1)S(1)}, bf16[160,256]{1,0:T(8,128)(2,1)S(1)}, u32[]{:S(2)}, u32[]{:S(2)}) collective-permute-start(bf16[160,256]{1,0:T(8,128)(2,1)S(1)} %get-tuple-element.75), channel_id=1, source_target_pairs={{0,0},{1,8},{2,2},{3,10},{4,4},{5,12},{6,6},{7,14},{8,1},{9,9},{10... | collective-permute-start | bytes 245768 | tf_op jit(solution)/shard_map/ppermute | solution.py:448
  78.0 7.7 %collective-permute-start.12 = (bf16[160,256]{1,0:T(8,128)(2,1)S(1)}, bf16[160,256]{1,0:T(8,128)(2,1)S(1)}, u32[]{:S(2)}, u32[]{:S(2)}) collective-permute-start(bf16[160,256]{1,0:T(8,128)(2,1)S(1)} %get-tuple-element.76), channel_id=1, source_target_pairs={{0,2},{1,10},{2,0},{3,8},{4,6},{5,14},{6,4},{7,12},{8,3},{9,11},{1... | collective-permute-start | bytes 245768 | tf_op jit(solution)/shard_map/ppermute | solution.py:448
  79.5 9.1 %collective-permute-start.13 = (bf16[160,256]{1,0:T(8,128)(2,1)S(1)}, bf16[160,256]{1,0:T(8,128)(2,1)S(1)}, u32[]{:S(2)}, u32[]{:S(2)}) collective-permute-start(bf16[160,256]{1,0:T(8,128)(2,1)S(1)} %get-tuple-element.77), channel_id=1, source_target_pairs={{0,4},{1,12},{2,6},{3,14},{4,0},{5,8},{6,2},{7,10},{8,5},{9,13},{1... | collective-permute-start | bytes 245768 | tf_op jit(solution)/shard_map/ppermute | solution.py:448
  81.2 7.5 %collective-permute-start.14 = (bf16[160,256]{1,0:T(8,128)(2,1)S(1)}, bf16[160,256]{1,0:T(8,128)(2,1)S(1)}, u32[]{:S(2)}, u32[]{:S(2)}) collective-permute-start(bf16[160,256]{1,0:T(8,128)(2,1)S(1)} %get-tuple-element.78), channel_id=1, source_target_pairs={{0,6},{1,14},{2,4},{3,12},{4,2},{5,10},{6,0},{7,8},{8,7},{9,15},{1... | collective-permute-start | bytes 245768 | tf_op jit(solution)/shard_map/ppermute | solution.py:448
  81.5 7.2 %collective-permute-start.15 = (bf16[160,256]{1,0:T(8,128)(2,1)S(1)}, bf16[160,256]{1,0:T(8,128)(2,1)S(1)}, u32[]{:S(2)}, u32[]{:S(2)}) collective-permute-start(bf16[160,256]{1,0:T(8,128)(2,1)S(1)} %get-tuple-element.79), channel_id=1, source_target_pairs={{0,8},{1,0},{2,10},{3,2},{4,12},{5,4},{6,14},{7,6},{8,9},{9,1},{10... | collective-permute-start | bytes 245768 | tf_op jit(solution)/shard_map/ppermute | solution.py:448
  84.8 5.6 %collective-permute-start.16 = (bf16[160,256]{1,0:T(8,128)(2,1)S(1)}, bf16[160,256]{1,0:T(8,128)(2,1)S(1)}, u32[]{:S(2)}, u32[]{:S(2)}) collective-permute-start(bf16[160,256]{1,0:T(8,128)(2,1)S(1)} %get-tuple-element.80), channel_id=1, source_target_pairs={{0,10},{1,2},{2,8},{3,0},{4,14},{5,6},{6,12},{7,4},{8,11},{9,3},{1... | collective-permute-start | bytes 245768 | tf_op jit(solution)/shard_map/ppermute | solution.py:448
  85.7 5.0 %collective-permute-start.17 = (bf16[160,256]{1,0:T(8,128)(2,1)S(1)}, bf16[160,256]{1,0:T(8,128)(2,1)S(1)}, u32[]{:S(2)}, u32[]{:S(2)}) collective-permute-start(bf16[160,256]{1,0:T(8,128)(2,1)S(1)} %get-tuple-element.81), channel_id=1, source_target_pairs={{0,12},{1,4},{2,14},{3,6},{4,8},{5,0},{6,10},{7,2},{8,13},{9,5},{1... | collective-permute-start | bytes 245768 | tf_op jit(solution)/shard_map/ppermute | solution.py:448
  88.7 5.1 %collective-permute-start.18 = (bf16[160,256]{1,0:T(8,128)(2,1)S(1)}, bf16[160,256]{1,0:T(8,128)(2,1)S(1)}, u32[]{:S(2)}, u32[]{:S(2)}) collective-permute-start(bf16[160,256]{1,0:T(8,128)(2,1)S(1)} %get-tuple-element.82), channel_id=1, source_target_pairs={{0,14},{1,6},{2,12},{3,4},{4,10},{5,2},{6,8},{7,0},{8,15},{9,7},{1... | collective-permute-start | bytes 245768 | tf_op jit(solution)/shard_map/ppermute | solution.py:448
  (4 other events, 20.3 us)

commit v2 on v1

--- a/solution.py
+++ b/solution.py
@@ -11,8 +11,8 @@
 BF16 = jnp.bfloat16
 AXES = ("ctx", "tp")
 GROUP = 4
-BIT_CORE, BIT_PART = 1, 16
-EARLY = 6
+BIT_CORE, BIT_PART, BITS_FAR = 1, 16, 24
+EARLY = 9
 SLOT_BITS = (0, 4, 8, 12)
 VMEM = pl.BlockSpec(memory_space=pltpu.VMEM)
 SMEM = pl.BlockSpec(memory_space=pltpu.SMEM)
@@ -26,8 +26,17 @@
     route = []
     for i in range(32):
         high, low, y, core = i >> 3 & 1, i >> 2 & 1, i >> 1 & 1, i & 1
-        route.append((i, (i & 16) + (core ^ a) * 8 + (low ^ b) * 4 + (y ^ c) * 2 + high))
+        part, row = i >> 4, y ^ c
+        route.append((i, part * 16 + (core ^ a) * 8 + (low ^ b) * 4 + row * 2 + (high ^ part ^ row)))
     return route
+
+
+def outer(i):
+    return (i >> 4) == (i >> 3 & 1)
+
+
+def far_swap(block, ends):
+    return lax.ppermute(block, AXES, [(i, i ^ BITS_FAR) for i in range(32) if outer(i) == ends])
 
 
 def split_const(mat):
@@ -128,12 +137,22 @@
     lspec_ref[...] = mm3(clh[...], cll[...], jnp.concatenate(filt, 0))
 
 
-def prepare_kernel(rows, g_ref, x_ref, t_ref, o0, o1, o2, o3, kx, vx, gate):
-    outs = (o0, o1, o2, o3)
+def prepare_kernel(rows, g_ref, x_hbm, t_hbm, o0, o1, o2, o3, p0, p1, p2, p3, x_ref, t_ref, kx, vx, gate, sems):
+    outs, queries = (o0, o1, o2, o3), (p0, p1, p2, p3)
     g = g_ref[0]
     quarter = o0.shape[1]
-    for lt in range(x_ref.shape[2] // 128):
+    tiles = x_ref.shape[2] // 128
+    short = pltpu.make_async_copy(t_hbm, t_ref, sems.at[tiles])
+    short.start()
+    loads = []
+    for lt in range(tiles):
         ls = slice(lt * 128, lt * 128 + 128)
+        loads.append(pltpu.make_async_copy(x_hbm.at[:, :, ls], x_ref.at[:, :, ls], sems.at[lt]))
+        loads[-1].start()
+    short.wait()
+    for lt in range(tiles):
+        ls = slice(lt * 128, lt * 128 + 128)
+        loads[lt].wait()
         for src, ext in ((1, kx), (2, vx)):
             ext[lt, :8] = jnp.zeros((8, 128), F32)
             ext[lt, 8:] = x_ref[src, :, ls].astype(F32)
@@ -148,14 +167,15 @@
                     sk, sv = sk + tk[j] * kx[lt, o:o + 8], sv + tv[j] * vx[lt, o:o + 8]
                 both.append(sk * sv)
             gate[r:r + 16, ls] = jnp.concatenate(both, 0).astype(BF16)
-    for m, out in enumerate(outs):
+    for m, (out, query) in enumerate(zip(outs, queries)):
         at = pl.ds(pl.multiple_of((g ^ m) * quarter, quarter), quarter)
         out[:rows] = gate[:, at]
-        out[rows:2 * rows] = x_ref[0, :, at]
         for i in (1, 2):
             ends = [x_ref[i, :16, at].astype(F32)[:8], x_ref[i, rows - 16:, at].astype(F32)[8:]]
-            row = 2 * rows + 16 * (i - 1)
+            row = rows + 16 * (i - 1)
             out[row:row + 16] = jnp.concatenate(ends, 0).astype(BF16)
+        out[rows + 32:rows + 48] = x_ref[0, rows - 16:, at]
+        query[...] = x_ref[0, :, at]
 
 
 def first_gates(before, ends, taps):
@@ -192,7 +212,7 @@
                         k = (i * len(blocks) + b) * 2
                         out += [acc[k] + x[b] * qr, acc[k + 1] + x[b] * qi]
                 return tuple(out)
-            acc = lax.fori_loop(0, rows // 8, step, (jnp.zeros((8, 128), F32),) * (2 * len(blocks) * per), unroll=4)
+            acc = lax.fori_loop(0, rows // 8, step, (jnp.zeros((8, 128), F32),) * (2 * len(blocks) * per), unroll=10 if len(blocks) > 1 else 20)
             for i in range(per):
                 for b in range(len(blocks)):
                     k = (i * len(blocks) + b) * 2
@@ -213,7 +233,7 @@
     gx[:128] = jnp.zeros_like(gx[:128])
     for m, msg in enumerate((q0, q1, q2, q3)):
         gx[pl.ds(pl.multiple_of(128 + (g ^ m) * rows, 16), rows), :] = msg[:rows]
-        ends[g ^ m] = msg[2 * rows:2 * rows + 32].astype(F32)
+        ends[g ^ m] = msg[rows:rows + 32].astype(F32)
     gate_ref[...] = gx[128:128 + rows]
     ends_ref[...] = ends[0]
     rim_ref[:128] = gx[GROUP * rows:]
@@ -222,10 +242,11 @@
         top = 128 + b * rows
         head = first_gates(ends[b - 1], ends[b], t_ref)
         gx[top:top + 16] = jnp.concatenate([head, gx[top:top + 16].astype(F32)[8:]], 0).astype(BF16)
+    ext = jnp.concatenate([gx[b * rows:b * rows + rows + 128] for b in range(GROUP)], 1)
+    both = medium_of(ext, jnp.concatenate([spec_ref[...]] * GROUP, 1), cmh, cml, imh, iml)
     for b in range(GROUP):
-        both = medium_of(gx[b * rows:b * rows + rows + 128], spec_ref[...], cmh, cml, imh, iml)
-        med_ref[b] = both[:rows]
-        flip[b] = both[rows:]
+        med_ref[b] = both[:rows, b * width:(b + 1) * width]
+        flip[b] = both[rows:, b * width:(b + 1) * width]
     end_states(rows, modes, 4, flip, range(GROUP), qre_ref, qim_ref, er, ei, width)
     dre, dim = par_ref[2], par_ref[3]
     sre = jnp.zeros((modes, width), F32)
@@ -238,7 +259,7 @@
     for m, q in enumerate((q0, q1, q2, q3)):
         @pl.when((g ^ m) == GROUP - 1)
         def _():
-            out_ref[2 * modes:] = q[2 * rows - 16:2 * rows].astype(F32)[8:]
+            out_ref[2 * modes:] = q[rows + 32:].astype(F32)[8:]
 
 
 def intra_kernel(rows, g_ref, t_ref, med_ref, lspec_ref, consts, q0, q1, q2, q3, intra_ref, query_ref, qx):
@@ -251,7 +272,7 @@
         ls = slice(lt * 128, lt * 128 + 128)
         qx[lt, :8] = jnp.zeros((8, 128), F32)
         for m, q in enumerate((q0, q1, q2, q3)):
-            qx[lt, pl.ds(pl.multiple_of((g ^ m) * rows + 8, 8), rows), :] = q[rows:2 * rows, ls].astype(F32)
+            qx[lt, pl.ds(pl.multiple_of((g ^ m) * rows + 8, 8), rows), :] = q[:, ls].astype(F32)
         t = [jnp.broadcast_to(t_ref[0, j:j + 1, ls], (8, 128)) for j in range(7)]
         for r in range(0, total, 8):
             acc = t[0] * qx[lt, 8 + r:16 + r]
@@ -308,40 +329,48 @@
         lax.fori_loop(0, rows // 16, step, 0)
 
 
-def project_kernel(g_ref, h0, h1, h2, h3, wa_ref, *rest):
-    far, (keep_ref, send_ref, wb_ref) = rest[:-3], rest[-3:]
-    g, same, core = g_ref[0], g_ref[2], g_ref[3]
+def project_kernel(c, g_ref, h0, h1, h2, h3, wa_ref, early, out_late, in_late, keep_ref, send_ref, wb_ref):
+    g, own, core, at_end, cut = g_ref[0], g_ref[2] != c, g_ref[3], g_ref[6], early.shape[0]
     quarter = h0.shape[1]
     half = wa_ref.shape[1] // 2
-    top = 0
-    for part in far:
-        wb_ref[top:top + part.shape[0]] = part[...]
-        top += part.shape[0]
     mine = pl.ds(pl.multiple_of(core * half, half), half)
     other = pl.ds(pl.multiple_of((1 - core) * half, half), half)
-    accs = [None] * 4
-    for m, h in enumerate((h0, h1, h2, h3)):
-        at = pl.ds(pl.multiple_of((g ^ m) * quarter, quarter), quarter)
-        x = h[...]
-        for n, cols in enumerate((mine, other)):
-            a, b = wa_ref[at, cols], wb_ref[at, cols]
-            for k, w in enumerate((a, b)):
-                d = mm(x, w)
-                accs[2 * k + n] = d if m == 0 else accs[2 * k + n] + d
-    own = same > 0
-    keep_ref[0] = jnp.where(own, accs[0], accs[2])
-    keep_ref[1] = jnp.where(own, accs[2], accs[0])
-    send_ref[0] = jnp.where(own, accs[1], accs[3]).astype(BF16)
-    send_ref[1] = jnp.where(own, accs[3], accs[1]).astype(BF16)
+
+    def run(weight):
+        keep = send = None
+        for m, h in enumerate((h0, h1, h2, h3)):
+            at = pl.ds(pl.multiple_of((g ^ m) * quarter, quarter), quarter)
+            x = h[...]
+            a, b = mm(x, weight[at, mine]), mm(x, weight[at, other])
+            keep, send = (a, b) if m == 0 else (keep + a, send + b)
+        keep_ref[...] = keep
+        send_ref[...] = send.astype(BF16)
+
+    @pl.when(own)
+    def _():
+        run(wa_ref)
+
+    @pl.when(jnp.logical_not(own))
+    def _():
+        wb_ref[:cut] = early[...]
+
+        @pl.when(at_end > 0)
+        def _():
+            wb_ref[cut:] = out_late[...]
+
+        @pl.when(at_end == 0)
+        def _():
+            wb_ref[cut:] = in_late[...]
+
+        run(wb_ref)
 
 
 def sort_kernel(rows, g_ref, keep_ref, got_ref, *outs):
     low, core = g_ref[4], g_ref[3]
     for n, out in enumerate(outs):
-        a, b, c = n >> 2 & 1, n >> 1 & 1, n & 1
-        block = 2 * (core ^ a) + (low ^ b)
+        block = 2 * (core ^ (n >> 1)) + (low ^ (n & 1))
         at = pl.ds(pl.multiple_of(block * rows, rows), rows)
-        out[...] = (keep_ref[c, at, :] + got_ref[c, at, :].astype(F32)).astype(BF16)
+        out[...] = (keep_ref[at, :] + got_ref[at, :].astype(F32)).astype(BF16)
 
 
 def gather_kernel(g_ref, *refs):
@@ -375,7 +404,7 @@
     ctx, tp = lax.axis_index("ctx"), lax.axis_index("tp")
     g, part = ctx % GROUP, ctx // GROUP
     core, y = tp % 2, tp // 2
-    scal = jnp.stack([g, part, (y == part).astype(jnp.int32), core, g % 2, g // 2]).astype(jnp.int32)
+    scal = jnp.stack([g, part, (y == part).astype(jnp.int32), core, g % 2, g // 2, (part == g // 2).astype(jnp.int32)]).astype(jnp.int32)
 
     cut = width * EARLY // 16
     size_m = rows + ntap
@@ -385,25 +414,32 @@
         np.pad(half, ((0, 0), (0, 2 * rows - half.shape[1]))) for mat in mats for half in split_const(mat)], 0)
 
     short_taps = short_taps.transpose(1, 0, 2)
-    msgs = call(
-        1.5,
+    anywhere = pl.BlockSpec(memory_space=pltpu.HBM)
+    sent = pl.pallas_call(
         lambda *refs: prepare_kernel(rows, *refs),
-        [((2 * rows + 32, quarter), BF16)] * GROUP,
-        (scal, streams.transpose(1, 0, 2), short_taps),
-        [((width // 128, rows + 8, 128), F32)] * 2 + [((rows, width), BF16)],
-    )
-    ahead, msgs = lax.optimization_barrier((out_weight[:cut], msgs))
-    early = swap(ahead, BIT_PART)
+        out_shape=tuple(jax.ShapeDtypeStruct((r, quarter), BF16) for r in (rows + 48,) * GROUP + (rows,) * GROUP),
+        in_specs=[SMEM, anywhere, anywhere],
+        out_specs=(VMEM,) * (2 * GROUP),
+        scratch_shapes=[pltpu.VMEM((3, rows, width), BF16), pltpu.VMEM((3, 7, width), F32)]
+        + [pltpu.VMEM((width // 128, rows + 8, 128), F32)] * 2
+        + [pltpu.VMEM((rows, width), BF16), pltpu.SemaphoreType.DMA((width // 128 + 1,))],
+        compiler_params=params(),
+        cost_estimate=pl.CostEstimate(flops=int(2e9), bytes_accessed=int(6e6), transcendentals=0),
+    )(scal, streams.transpose(1, 0, 2), short_taps)
+    msgs, qs = sent[:GROUP], sent[GROUP:]
+    early = swap(out_weight[:cut], BITS_FAR)
     msgs = [msgs[0]] + [swap(msgs[m], SLOT_BITS[m]) for m in (1, 2, 3)]
     spec, lspec, qre, qim, par, taps = call(
-        2.5,
+        0.3,
         lambda *refs: filters_kernel(rows, modes, *refs),
         [(s, F32) for s in ((size_m, quarter), (2 * rows, quarter), (modes, rows, quarter), (modes, rows, quarter),
                             (4, modes, quarter), (3, 7, quarter))],
         (scal, mix_taps, pole_rate, pole_angle, residue, skip[None], short_taps, consts),
     )
+    spec, qs = lax.optimization_barrier((spec, qs))
+    qs = [qs[0]] + [swap(qs[m], SLOT_BITS[m]) for m in (1, 2, 3)]
     med, st, out, rim, gate, ends = call(
-        5.4,
+        0.6,
         lambda *refs: medium_kernel(rows, modes, *refs),
         [((GROUP, rows, quarter), F32), ((GROUP, 2, modes, quarter), F32), ((2 * modes + 8, quarter), F32),
          ((160, quarter), BF16), ((rows, quarter), BF16), ((32, quarter), F32)],
@@ -413,15 +449,15 @@
     )
     out, rim, early = lax.optimization_barrier((out, rim, early))
     state_in, rim_in = swap(out, BIT_PART), swap(rim, BIT_PART)
-    late, state_in, rim_in = lax.optimization_barrier((out_weight[cut:], state_in, rim_in))
-    far_weight = [early, swap(late, BIT_PART)]
     later, query = call(
         3.1,
         lambda *refs: intra_kernel(rows, *refs),
         [((GROUP - 1, rows, quarter), F32), ((total, quarter), F32)],
-        (scal, taps, med, lspec, consts, *msgs),
+        (scal, taps, med, lspec, consts, *qs),
         [((quarter // 128, total + 8, 128), F32)],
     )
+    late, later = lax.optimization_barrier((out_weight[cut:], later))
+    out_late = far_swap(late, True)
     (hidden,) = call(
         5.2,
         lambda *refs: hidden_kernel(rows, modes, *refs),
@@ -430,22 +466,29 @@
         [((GROUP, modes, 2, 8, quarter), F32), ((rows + 128, quarter), BF16), ((1, rows, quarter), F32),
          ((1, modes, quarter), F32), ((1, modes, quarter), F32), ((1, rows, quarter), F32)],
     )
+    hidden, late = lax.optimization_barrier((hidden, out_weight[cut:]))
+    in_late = far_swap(late, False)
     hid = [hidden] + [swap(hidden, SLOT_BITS[m]) for m in (1, 2, 3)]
     half = out_weight.shape[1] // 2
-    keep, send = call(
-        2.2,
-        project_kernel,
-        [((2, total, half), F32), ((2, total, half), BF16)],
-        (scal, *hid, out_weight, *far_weight),
-        [((width, 2 * half), BF16)],
-    )
-    blocks = call(
-        0.7,
-        lambda *refs: sort_kernel(rows, *refs),
-        [((rows, half), BF16)] * 8,
-        (scal, keep, swap(send, BIT_CORE)),
-    )
-    blocks = [lax.ppermute(block, AXES, homeward(n >> 2 & 1, n >> 1 & 1, n & 1)) for n, block in enumerate(blocks)]
+    blocks = {}
+    for c in (1, 0):
+        keep, send = call(
+            1.2,
+            lambda *refs: project_kernel(c, *refs),
+            [((total, half), F32), ((total, half), BF16)],
+            (scal, *hid, out_weight, early, out_late, in_late),
+            [((width, 2 * half), BF16)],
+        )
+        send, hid = lax.optimization_barrier((send, hid))
+        parts = call(
+            0.4,
+            lambda *refs: sort_kernel(rows, *refs),
+            [((rows, half), BF16)] * GROUP,
+            (scal, keep, swap(send, BIT_CORE)),
+        )
+        for n, part in enumerate(parts):
+            blocks[n, c] = lax.ppermute(part, AXES, homeward(n >> 1, n & 1, c))
+    blocks = [blocks[n, c] for n in range(GROUP) for c in (0, 1)]
     (mixed,) = call(1.3, gather_kernel, [((rows, 4 * half), BF16)], (scal, *blocks))
     return mixed
 

time: 95.3 us -> 88.3 us (0.927)
  waiting for transfers between devices: 43.6 us -> 24.3 us
  starting transfers between devices: 27 us -> 38.8 us
    ppermute x11 -> x14, waiting for transfers between devices: 38.6 us -> 17.7 us  [swap(): return lax.ppermute(block, AXES, [(i, i ^ bits) for i in range(32)])]
    ppermute x8 -> x10, starting transfers between devices: 11.4 us -> 18 us  [the longest x8 12.4 us: fast_body(): blocks[n, c] = lax.ppermute(part, AXES, homeward(n >> 1, n & 1, c))]
    ppermute x11 -> x14, starting transfers between devices: 15.6 us -> 20.8 us  [swap(): return lax.ppermute(block, AXES, [(i, i ^ bits) for i in range(32)])]
    pallas_call x0 -> x1, Pallas kernels: none -> 1.94 us  [fast_body(): pl.pallas_call(lambda *refs: prepare_kernel(rows, *refs), out_shape=tuple...]
    ppermute x8 -> x10, waiting for transfers between devices: 5.01 us -> 6.58 us  [the longest x8 4.55 us: fast_body(): blocks[n, c] = lax.ppermute(part, AXES, homeward(n >> 1, n & 1, c))]
    pallas_call x8 -> x9, Pallas kernels: 21 us -> 19.4 us  [call(): pl.pallas_call(kernel, out_shape=tuple((jax.ShapeDtypeStruct(s, d) for s,...]
    unnamed x18 -> x20, local copies, waits for them, and re-layouts: 2.13 us -> 2.13 us
  transfers between devices with their start and end apart: 19 -> 24, of which waited for: 10 -> 6; matrix products, arithmetic and copies ran while one was open for 0% -> 0% of each run, Pallas kernels for 16% -> 21%
where the time goes in v2:
time: 88.3 us; the launch traced here: 88.1 us
  starting transfers between devices  38.8 us (44%)
  waiting for transfers between devices  24.3 us (28%)
  Pallas kernels  21.3 us (24%)
  local copies, waits for them, and re-layouts  3.35 us (4%)
    ppermute x14, starting transfers between devices, swap(): return lax.ppermute(block, AXES, [(i, i ^ bits) for i in range(32)])  20.8 us
    pallas_call x9, Pallas kernels, call(): pl.pallas_call(kernel, out_shape=tuple((jax.ShapeDtypeStruct(s, d) for s,...  19.4 us
    ppermute x14, waiting for transfers between devices, swap(): return lax.ppermute(block, AXES, [(i, i ^ bits) for i in range(32)])  17.7 us
    ppermute x8, starting transfers between devices, fast_body(): blocks[n, c] = lax.ppermute(part, AXES, homeward(n >> 1, n & 1, c))  12.4 us
    ppermute x2, starting transfers between devices, far_swap(): lax.ppermute(block, AXES, [(i, i ^ BITS_FAR) for i in range(32) if outer(...  5.62 us
    ppermute x8, waiting for transfers between devices, fast_body(): blocks[n, c] = lax.ppermute(part, AXES, homeward(n >> 1, n & 1, c))  4.55 us
    unnamed x20, local copies, waits for them, and re-layouts  2.13 us
    ppermute x2, waiting for transfers between devices, far_swap(): lax.ppermute(block, AXES, [(i, i ^ BITS_FAR) for i in range(32) if outer(...  2.04 us
  transfers between devices with their start and end apart: 24, of which 6 were waited for; matrix products, arithmetic and copies ran while one was open for 0% of the time, Pallas kernels for 21%

profile of v2, /device:TPU:0, one launch (start us, length us, event | category | flops | bytes accessed | tf_op | source)
XLA Modules:
  0.0 88.1 jit_solution(16326292260994389292)
XLA Ops:
  1.1 5.1 %collective-permute-start.3 = (bf16[576,512]{1,0:T(8,128)(2,1)S(1)}, bf16[576,512]{1,0:T(8,128)(2,1)S(1)}, u32[]{:S(2)}, u32[]{:S(2)}) collective-permute-start(bf16[576,512]{1,0:T(8,128)(2,1)S(1)} %slice.7), channel_id=1, source_target_pairs={{0,24},{1,25},{2,26},{3,27},{4,28},{5,29},{6,30},{7,31},{8,16},{9,... | collective-permute-start | bytes 1769480 | tf_op jit(solution)/shard_map/ppermute | solution.py:22
  8.4 1.9 %shard_map.92 = (bf16[208,256]{1,0:T(8,128)(2,1)S(1)}, bf16[208,256]{1,0:T(8,128)(2,1)S(1)}, bf16[208,256]{1,0:T(8,128)(2,1)S(1)}, bf16[208,256]{1,0:T(8,128)(2,...) custom-call(s32[7]{0:T(128)S(1)} %stack.39.refs_0_.g_ref, ...), custom_call_target="tpu_custom_call" | custom-call | flops 2000000000 | bytes 6000000 | tf_op jit(solution)/shard_map/pallas_call | solution.py:418
  10.4 1.6 %collective-permute-start = (bf16[208,256]{1,0:T(8,128)(2,1)S(1)}, bf16[208,256]{1,0:T(8,128)(2,1)S(1)}, u32[]{:S(2)}, u32[]{:S(2)}) collective-permute-start(bf16[208,256]{1,0:T(8,128)(2,1)S(1)} %get-tuple-element.68), channel_id=1, source_target_pairs={{0,4},{1,5},{2,6},{3,7},{4,0},{5,1},{6,2},{7,3},{8,12},{9,13},{10,... | collective-permute-start | bytes 319496 | tf_op jit(solution)/shard_map/ppermute | solution.py:22
  12.0 2.0 %collective-permute-start.2 = (bf16[208,256]{1,0:T(8,128)(2,1)S(1)}, bf16[208,256]{1,0:T(8,128)(2,1)S(1)}, u32[]{:S(2)}, u32[]{:S(2)}) collective-permute-start(bf16[208,256]{1,0:T(8,128)(2,1)S(1)} %get-tuple-element.70), channel_id=1, source_target_pairs={{0,12},{1,13},{2,14},{3,15},{4,8},{5,9},{6,10},{7,11},{8,4},{9,5},... | collective-permute-start | bytes 319496 | tf_op jit(solution)/shard_map/ppermute | solution.py:22
  14.0 2.6 %shard_map.91 = (f32[288,256]{1,0:T(8,128)S(1)}, f32[320,256]{1,0:T(8,128)S(1)}, f32[16,160,256]{2,1,0:T(8,128)S(1)}, f32[16,160,256]{2,1,0:T(8,128)S(1)}, f32[4...) custom-call(s32[7]{0:T(128)S(1)} %stack.39.refs_0_.g_ref, f32[128,1024]{1,0:T(8,128)S(1)} %copy-done.2, ...), custom_call_target="tpu_custom_call" | custom-call | flops 345000000 | bytes 1107000 | tf_op jit(solution)/shard_map/pallas_call | solution.py:387
  16.6 1.6 %collective-permute-start.6 = (bf16[160,256]{1,0:T(8,128)(2,1)S(1)}, bf16[160,256]{1,0:T(8,128)(2,1)S(1)}, u32[]{:S(2)}, u32[]{:S(2)}) collective-permute-start(bf16[160,256]{1,0:T(8,128)(2,1)S(1)} %get-tuple-element.81), channel_id=1, source_target_pairs={{0,4},{1,5},{2,6},{3,7},{4,0},{5,1},{6,2},{7,3},{8,12},{9,13},{10,... | collective-permute-start | bytes 245768 | tf_op jit(solution)/shard_map/ppermute | solution.py:22
  18.2 4.1 %collective-permute-done.1.refs_9_ = bf16[208,256]{1,0:T(8,128)(2,1)S(1)} collective-permute-done((bf16[208,256]{1,0:T(8,128)(2,1)S(1)}, bf16[208,256]{1,0:T(8,128)(2,1)S(1)}, u32[]{:S(2)}, u32[]{:S(2)}) %collective-permute-start.1) | collective-permute-done | bytes 106528 | tf_op jit(solution)/shard_map/ppermute | solution.py:22
  22.3 3.4 %collective-permute-start.8 = (bf16[160,256]{1,0:T(8,128)(2,1)S(1)}, bf16[160,256]{1,0:T(8,128)(2,1)S(1)}, u32[]{:S(2)}, u32[]{:S(2)}) collective-permute-start(bf16[160,256]{1,0:T(8,128)(2,1)S(1)} %get-tuple-element.83), channel_id=1, source_target_pairs={{0,12},{1,13},{2,14},{3,15},{4,8},{5,9},{6,10},{7,11},{8,4},{9,5},... | collective-permute-start | bytes 245768 | tf_op jit(solution)/shard_map/ppermute | solution.py:22
  25.7 4.3 %shard_map.93 = (f32[4,160,256]{2,1,0:T(8,128)S(1)}, f32[4,2,16,256]{3,2,1,0:T(8,128)S(1)}, f32[40,256]{1,0:T(8,128)S(1)}, bf16[160,256]{1,0:T(8,128)(2,1)S(1)},...) custom-call(s32[7]{0:T(128)S(1)} %stack.39.refs_0_.g_ref, f32[3,7,256]{2,1,0:T(8,128)S(1)} %get-tuple-element.57.refs_1_, ...), custom_call_target="tpu_custom_call" | custom-call | flops 690000000 | bytes 2214000 | tf_op jit(solution)/shard_map/pallas_call | solution.py:387
  30.0 2.9 %collective-permute-start.5 = (bf16[160,256]{1,0:T(8,128)(2,1)S(1)}, bf16[160,256]{1,0:T(8,128)(2,1)S(1)}, u32[]{:S(2)}, u32[]{:S(2)}) collective-permute-start(bf16[160,256]{1,0:T(8,128)(2,1)S(1)} %get-tuple-element.74), channel_id=1, source_target_pairs={{0,16},{1,17},{2,18},{3,19},{4,20},{5,21},{6,22},{7,23},{8,24},{9,... | collective-permute-start | bytes 245768 | tf_op jit(solution)/shard_map/ppermute | solution.py:22
  33.0 2.2 %shard_map.94 = (f32[3,160,256]{2,1,0:T(8,128)S(1)}, f32[640,256]{1,0:T(8,128)S(1)}) custom-call(s32[7]{0:T(128)S(1)} %stack.39.refs_0_.g_ref, f32[3,7,256]{2,1,0:T(8,128)S(1)} %get-tuple-element.57.refs_1_, f32[4,160,256]{2,1,0:T(8,128)S(1)} %get-tuple-element.79.refs_2_, f32[320,256]{1,0:T(8,128)S(1)} %get-tuple-element.77.refs_3_.refs_7_, ...), custom_call_target="tpu_custom_call" | custom-call | flops 3564999936 | bytes 11439000 | tf_op jit(solution)/shard_map/pallas_call | solution.py:387
  35.2 4.9 %collective-permute-start.12 = (bf16[448,512]{1,0:T(8,128)(2,1)S(1)}, bf16[448,512]{1,0:T(8,128)(2,1)S(1)}, u32[]{:S(2)}, u32[]{:S(2)}) collective-permute-start(bf16[448,512]{1,0:T(8,128)(2,1)S(1)} %slice.8), channel_id=1, source_target_pairs={{0,24},{1,25},{2,26},{3,27},{4,28},{5,29},{6,30},{7,31},{24,0},{25... | collective-permute-start | bytes 1376264 | tf_op jit(solution)/shard_map/ppermute | solution.py:39
  40.2 5.0 %shard_map.95.refs_1_ = bf16[640,256]{1,0:T(8,128)(2,1)S(1)} custom-call(s32[7]{0:T(128)S(1)} %stack.39.refs_0_.g_ref, f32[3,7,256]{2,1,0:T(8,128)S(1)} %get-tuple-element.57.refs_1_, f32[40,256]{1,0:T(8,128)S(1)} %collective-permute-done.4.refs_2_, bf16[160,256]{1,0:T(8,128)(2,1)S(1)} %collective-permute-done.5.refs_3_, ...), custom_call_target="tpu_custom_call" | custom-call | flops 5980000256 | bytes 19188000 | tf_op jit(solution)/shard_map/pallas_call | solution.py:387
  46.3 1.6 %collective-permute-start.11 = (bf16[640,256]{1,0:T(8,128)(2,1)S(1)}, bf16[640,256]{1,0:T(8,128)(2,1)S(1)}, u32[]{:S(2)}, u32[]{:S(2)}) collective-permute-start(bf16[640,256]{1,0:T(8,128)(2,1)S(1)} %shard_map.95.refs_1_), channel_id=1, source_target_pairs={{0,12},{1,13},{2,14},{3,15},{4,8},{5,9},{6,10},{7,11},{8,4},{9,5},... | collective-permute-start | bytes 983048 | tf_op jit(solution)/shard_map/ppermute | solution.py:22
  47.9 1.5 %collective-permute-start.9 = (bf16[640,256]{1,0:T(8,128)(2,1)S(1)}, bf16[640,256]{1,0:T(8,128)(2,1)S(1)}, u32[]{:S(2)}, u32[]{:S(2)}) collective-permute-start(bf16[640,256]{1,0:T(8,128)(2,1)S(1)} %shard_map.95.refs_1_), channel_id=1, source_target_pairs={{0,4},{1,5},{2,6},{3,7},{4,0},{5,1},{6,2},{7,3},{8,12},{9,13},{10,... | collective-permute-start | bytes 983048 | tf_op jit(solution)/shard_map/ppermute | solution.py:22
  49.4 2.0 %collective-permute-done.12.refs_7_ = bf16[448,512]{1,0:T(8,128)(2,1)S(1)} collective-permute-done((bf16[448,512]{1,0:T(8,128)(2,1)S(1)}, bf16[448,512]{1,0:T(8,128)(2,1)S(1)}, u32[]{:S(2)}, u32[]{:S(2)}) %collective-permute-start.12) | collective-permute-done | bytes 458784 | tf_op jit(solution)/shard_map/ppermute | solution.py:39
  51.5 6.7 %collective-permute-done.10.refs_3_ = bf16[640,256]{1,0:T(8,128)(2,1)S(1)} collective-permute-done((bf16[640,256]{1,0:T(8,128)(2,1)S(1)}, bf16[640,256]{1,0:T(8,128)(2,1)S(1)}, u32[]{:S(2)}, u32[]{:S(2)}) %collective-permute-start.10) | collective-permute-done | bytes 327712 | tf_op jit(solution)/shard_map/ppermute | solution.py:22
  58.2 6.8 %collective-permute-done.11.refs_4_ = bf16[640,256]{1,0:T(8,128)(2,1)S(1)} collective-permute-done((bf16[640,256]{1,0:T(8,128)(2,1)S(1)}, bf16[640,256]{1,0:T(8,128)(2,1)S(1)}, u32[]{:S(2)}, u32[]{:S(2)}) %collective-permute-start.11) | collective-permute-done | bytes 327712 | tf_op jit(solution)/shard_map/ppermute | solution.py:22
  65.0 1.5 %shard_map.96 = (f32[640,256]{1,0:T(8,128)S(1)}, bf16[640,256]{1,0:T(8,128)(2,1)S(1)}) custom-call(s32[7]{0:T(128)S(1)} %stack.39.refs_0_.g_ref, bf16[640,256]{1,0:T(8,128)(2,1)S(1)} %shard_map.95.refs_1_, bf16[640,256]{1,0:T(8,128)(2,1)S(1)} %collective-permute-done.9.refs_2_, bf16[640,256]{1,0:T(8,128)(2,1)S(1)} %collective-permute-done.10.refs_3_, ...), custom_call_target="tpu_custom_call" | custom-call | flops 1380000000 | bytes 4428000 | tf_op jit(solution)/shard_map/pallas_call | solution.py:387
  70.3 2.0 %collective-permute-start.19 = (bf16[160,256]{1,0:T(8,128)(2,1)S(1)}, bf16[160,256]{1,0:T(8,128)(2,1)S(1)}, u32[]{:S(2)}, u32[]{:S(2)}) collective-permute-start(bf16[160,256]{1,0:T(8,128)(2,1)S(1)} %get-tuple-element.104), channel_id=1, source_target_pairs={{0,7},{1,15},{2,4},{3,12},{4,3},{5,11},{6,0},{7,8},{8,6},{9,14},{1... | collective-permute-start | bytes 245768 | tf_op jit(solution)/shard_map/ppermute | solution.py:490
  75.6 1.5 %collective-permute-start.18 = (bf16[160,256]{1,0:T(8,128)(2,1)S(1)}, bf16[160,256]{1,0:T(8,128)(2,1)S(1)}, u32[]{:S(2)}, u32[]{:S(2)}) collective-permute-start(bf16[160,256]{1,0:T(8,128)(2,1)S(1)} %get-tuple-element.103), channel_id=1, source_target_pairs={{0,4},{1,12},{2,7},{3,15},{4,0},{5,8},{6,3},{7,11},{8,5},{9,13},{1... | collective-permute-start | bytes 245768 | tf_op jit(solution)/shard_map/ppermute | solution.py:490
  77.1 4.9 %collective-permute-start.20 = (bf16[160,256]{1,0:T(8,128)(2,1)S(1)}, bf16[160,256]{1,0:T(8,128)(2,1)S(1)}, u32[]{:S(2)}, u32[]{:S(2)}) collective-permute-start(bf16[160,256]{1,0:T(8,128)(2,1)S(1)} %get-tuple-element.105), channel_id=1, source_target_pairs={{0,8},{1,0},{2,11},{3,3},{4,12},{5,4},{6,15},{7,7},{8,9},{9,1},{10... | collective-permute-start | bytes 245768 | tf_op jit(solution)/shard_map/ppermute | solution.py:490
  82.2 1.9 %collective-permute-done.20.refs_4_ = bf16[160,256]{1,0:T(8,128)(2,1)S(1)} collective-permute-done((bf16[160,256]{1,0:T(8,128)(2,1)S(1)}, bf16[160,256]{1,0:T(8,128)(2,1)S(1)}, u32[]{:S(2)}, u32[]{:S(2)}) %collective-permute-start.20) | collective-permute-done | bytes 81952 | tf_op jit(solution)/shard_map/ppermute | solution.py:490
  84.1 2.6 %collective-permute-done.22.refs_6_ = bf16[160,256]{1,0:T(8,128)(2,1)S(1)} collective-permute-done((bf16[160,256]{1,0:T(8,128)(2,1)S(1)}, bf16[160,256]{1,0:T(8,128)(2,1)S(1)}, u32[]{:S(2)}, u32[]{:S(2)}) %collective-permute-start.22) | collective-permute-done | bytes 81952 | tf_op jit(solution)/shard_map/ppermute | solution.py:490
  (57 shorter events, 13.1 us)
Async XLA Ops:
  1.1 28.9 %collective-permute-start.3 = (bf16[576,512]{1,0:T(8,128)(2,1)S(1)}, bf16[576,512]{1,0:T(8,128)(2,1)S(1)}, u32[]{:S(2)}, u32[]{:S(2)}) collective-permute-start(bf16[576,512]{1,0:T(8,128)(2,1)S(1)} %slice.7), channel_id=1, source_target_pairs={{0,24},{1,25},{2,26},{3,27},{4,28},{5,29},{6,30},{7,31},{8,16},{9,... | collective-permute-start | bytes 1769480 | tf_op jit(solution)/shard_map/ppermute | solution.py:22
  10.4 7.7 %collective-permute-start = (bf16[208,256]{1,0:T(8,128)(2,1)S(1)}, bf16[208,256]{1,0:T(8,128)(2,1)S(1)}, u32[]{:S(2)}, u32[]{:S(2)}) collective-permute-start(bf16[208,256]{1,0:T(8,128)(2,1)S(1)} %get-tuple-element.68), channel_id=1, source_target_pairs={{0,4},{1,5},{2,6},{3,7},{4,0},{5,1},{6,2},{7,3},{8,12},{9,13},{10,... | collective-permute-start | bytes 319496 | tf_op jit(solution)/shard_map/ppermute | solution.py:22
  12.0 10.3 %collective-permute-start.1 = (bf16[208,256]{1,0:T(8,128)(2,1)S(1)}, bf16[208,256]{1,0:T(8,128)(2,1)S(1)}, u32[]{:S(2)}, u32[]{:S(2)}) collective-permute-start(bf16[208,256]{1,0:T(8,128)(2,1)S(1)} %get-tuple-element.69), channel_id=1, source_target_pairs={{0,8},{1,9},{2,10},{3,11},{4,12},{5,13},{6,14},{7,15},{8,0},{9,1},... | collective-permute-start | bytes 319496 | tf_op jit(solution)/shard_map/ppermute | solution.py:22
  12.0 13.8 %collective-permute-start.2 = (bf16[208,256]{1,0:T(8,128)(2,1)S(1)}, bf16[208,256]{1,0:T(8,128)(2,1)S(1)}, u32[]{:S(2)}, u32[]{:S(2)}) collective-permute-start(bf16[208,256]{1,0:T(8,128)(2,1)S(1)} %get-tuple-element.70), channel_id=1, source_target_pairs={{0,12},{1,13},{2,14},{3,15},{4,8},{5,9},{6,10},{7,11},{8,4},{9,5},... | collective-permute-start | bytes 319496 | tf_op jit(solution)/shard_map/ppermute | solution.py:22
  16.6 16.5 %collective-permute-start.6 = (bf16[160,256]{1,0:T(8,128)(2,1)S(1)}, bf16[160,256]{1,0:T(8,128)(2,1)S(1)}, u32[]{:S(2)}, u32[]{:S(2)}) collective-permute-start(bf16[160,256]{1,0:T(8,128)(2,1)S(1)} %get-tuple-element.81), channel_id=1, source_target_pairs={{0,4},{1,5},{2,6},{3,7},{4,0},{5,1},{6,2},{7,3},{8,12},{9,13},{10,... | collective-permute-start | bytes 245768 | tf_op jit(solution)/shard_map/ppermute | solution.py:22
  18.1 14.9 %collective-permute-start.7 = (bf16[160,256]{1,0:T(8,128)(2,1)S(1)}, bf16[160,256]{1,0:T(8,128)(2,1)S(1)}, u32[]{:S(2)}, u32[]{:S(2)}) collective-permute-start(bf16[160,256]{1,0:T(8,128)(2,1)S(1)} %get-tuple-element.82), channel_id=1, source_target_pairs={{0,8},{1,9},{2,10},{3,11},{4,12},{5,13},{6,14},{7,15},{8,0},{9,1},... | collective-permute-start | bytes 245768 | tf_op jit(solution)/shard_map/ppermute | solution.py:22
  22.3 10.8 %collective-permute-start.8 = (bf16[160,256]{1,0:T(8,128)(2,1)S(1)}, bf16[160,256]{1,0:T(8,128)(2,1)S(1)}, u32[]{:S(2)}, u32[]{:S(2)}) collective-permute-start(bf16[160,256]{1,0:T(8,128)(2,1)S(1)} %get-tuple-element.83), channel_id=1, source_target_pairs={{0,12},{1,13},{2,14},{3,15},{4,8},{5,9},{6,10},{7,11},{8,4},{9,5},... | collective-permute-start | bytes 245768 | tf_op jit(solution)/shard_map/ppermute | solution.py:22
  30.0 10.2 %collective-permute-start.5 = (bf16[160,256]{1,0:T(8,128)(2,1)S(1)}, bf16[160,256]{1,0:T(8,128)(2,1)S(1)}, u32[]{:S(2)}, u32[]{:S(2)}) collective-permute-start(bf16[160,256]{1,0:T(8,128)(2,1)S(1)} %get-tuple-element.74), channel_id=1, source_target_pairs={{0,16},{1,17},{2,18},{3,19},{4,20},{5,21},{6,22},{7,23},{8,24},{9,... | collective-permute-start | bytes 245768 | tf_op jit(solution)/shard_map/ppermute | solution.py:22
  32.9 7.3 %collective-permute-start.4 = (f32[40,256]{1,0:T(8,128)S(1)}, f32[40,256]{1,0:T(8,128)S(1)}, u32[]{:S(2)}, u32[]{:S(2)}) collective-permute-start(f32[40,256]{1,0:T(8,128)S(1)} %get-tuple-element.73), channel_id=1, source_target_pairs={{0,16},{1,17},{2,18},{3,19},{4,20},{5,21},{6,22},{7,23},{8,24},{9,... | collective-permute-start | bytes 122888 | tf_op jit(solution)/shard_map/ppermute | solution.py:22
  35.2 16.2 %collective-permute-start.12 = (bf16[448,512]{1,0:T(8,128)(2,1)S(1)}, bf16[448,512]{1,0:T(8,128)(2,1)S(1)}, u32[]{:S(2)}, u32[]{:S(2)}) collective-permute-start(bf16[448,512]{1,0:T(8,128)(2,1)S(1)} %slice.8), channel_id=1, source_target_pairs={{0,24},{1,25},{2,26},{3,27},{4,28},{5,29},{6,30},{7,31},{24,0},{25... | collective-permute-start | bytes 1376264 | tf_op jit(solution)/shard_map/ppermute | solution.py:39
  45.2 19.8 %collective-permute-start.13 = (bf16[448,512]{1,0:T(8,128)(2,1)S(1)}, bf16[448,512]{1,0:T(8,128)(2,1)S(1)}, u32[]{:S(2)}, u32[]{:S(2)}) collective-permute-start(bf16[448,512]{1,0:T(8,128)(2,1)S(1)} %slice.8), channel_id=1, source_target_pairs={{8,16},{9,17},{10,18},{11,19},{12,20},{13,21},{14,22},{15,23},{16,... | collective-permute-start | bytes 1376264 | tf_op jit(solution)/shard_map/ppermute | solution.py:39
  45.9 12.3 %collective-permute-start.10 = (bf16[640,256]{1,0:T(8,128)(2,1)S(1)}, bf16[640,256]{1,0:T(8,128)(2,1)S(1)}, u32[]{:S(2)}, u32[]{:S(2)}) collective-permute-start(bf16[640,256]{1,0:T(8,128)(2,1)S(1)} %shard_map.95.refs_1_), channel_id=1, source_target_pairs={{0,8},{1,9},{2,10},{3,11},{4,12},{5,13},{6,14},{7,15},{8,0},{9,1},... | collective-permute-start | bytes 983048 | tf_op jit(solution)/shard_map/ppermute | solution.py:22
  46.3 18.7 %collective-permute-start.11 = (bf16[640,256]{1,0:T(8,128)(2,1)S(1)}, bf16[640,256]{1,0:T(8,128)(2,1)S(1)}, u32[]{:S(2)}, u32[]{:S(2)}) collective-permute-start(bf16[640,256]{1,0:T(8,128)(2,1)S(1)} %shard_map.95.refs_1_), channel_id=1, source_target_pairs={{0,12},{1,13},{2,14},{3,15},{4,8},{5,9},{6,10},{7,11},{8,4},{9,5},... | collective-permute-start | bytes 983048 | tf_op jit(solution)/shard_map/ppermute | solution.py:22
  47.9 17.1 %collective-permute-start.9 = (bf16[640,256]{1,0:T(8,128)(2,1)S(1)}, bf16[640,256]{1,0:T(8,128)(2,1)S(1)}, u32[]{:S(2)}, u32[]{:S(2)}) collective-permute-start(bf16[640,256]{1,0:T(8,128)(2,1)S(1)} %shard_map.95.refs_1_), channel_id=1, source_target_pairs={{0,4},{1,5},{2,6},{3,7},{4,0},{5,1},{6,2},{7,3},{8,12},{9,13},{10,... | collective-permute-start | bytes 983048 | tf_op jit(solution)/shard_map/ppermute | solution.py:22
  66.5 2.0 %collective-permute-start.16 = (bf16[640,256]{1,0:T(8,128)(2,1)S(1)}, bf16[640,256]{1,0:T(8,128)(2,1)S(1)}, u32[]{:S(2)}, u32[]{:S(2)}) collective-permute-start(bf16[640,256]{1,0:T(8,128)(2,1)S(1)} %get-tuple-element.101), channel_id=1, source_target_pairs={{0,1},{1,0},{2,3},{3,2},{4,5},{5,4},{6,7},{7,6},{8,9},{9,8},{10,11... | collective-permute-start | bytes 983048 | tf_op jit(solution)/shard_map/ppermute | solution.py:22
  67.9 6.3 %collective-permute-start.14 = (bf16[640,256]{1,0:T(8,128)(2,1)S(1)}, bf16[640,256]{1,0:T(8,128)(2,1)S(1)}, u32[]{:S(2)}, u32[]{:S(2)}) collective-permute-start(bf16[640,256]{1,0:T(8,128)(2,1)S(1)} %get-tuple-element.98), channel_id=1, source_target_pairs={{0,1},{1,0},{2,3},{3,2},{4,5},{5,4},{6,7},{7,6},{8,9},{9,8},{10,11... | collective-permute-start | bytes 983048 | tf_op jit(solution)/shard_map/ppermute | solution.py:22
  69.1 6.5 %collective-permute-start.17 = (bf16[160,256]{1,0:T(8,128)(2,1)S(1)}, bf16[160,256]{1,0:T(8,128)(2,1)S(1)}, u32[]{:S(2)}, u32[]{:S(2)}) collective-permute-start(bf16[160,256]{1,0:T(8,128)(2,1)S(1)} %get-tuple-element.102), channel_id=1, source_target_pairs={{0,3},{1,11},{2,0},{3,8},{4,7},{5,15},{6,4},{7,12},{8,2},{9,10},{1... | collective-permute-start | bytes 245768 | tf_op jit(solution)/shard_map/ppermute | solution.py:490
  70.3 6.8 %collective-permute-start.19 = (bf16[160,256]{1,0:T(8,128)(2,1)S(1)}, bf16[160,256]{1,0:T(8,128)(2,1)S(1)}, u32[]{:S(2)}, u32[]{:S(2)}) collective-permute-start(bf16[160,256]{1,0:T(8,128)(2,1)S(1)} %get-tuple-element.104), channel_id=1, source_target_pairs={{0,7},{1,15},{2,4},{3,12},{4,3},{5,11},{6,0},{7,8},{8,6},{9,14},{1... | collective-permute-start | bytes 245768 | tf_op jit(solution)/shard_map/ppermute | solution.py:490
  72.3 9.8 %collective-permute-start.21 = (bf16[160,256]{1,0:T(8,128)(2,1)S(1)}, bf16[160,256]{1,0:T(8,128)(2,1)S(1)}, u32[]{:S(2)}, u32[]{:S(2)}) collective-permute-start(bf16[160,256]{1,0:T(8,128)(2,1)S(1)} %get-tuple-element.106), channel_id=1, source_target_pairs={{0,11},{1,3},{2,8},{3,0},{4,15},{5,7},{6,12},{7,4},{8,10},{9,2},{1... | collective-permute-start | bytes 245768 | tf_op jit(solution)/shard_map/ppermute | solution.py:490
  73.5 8.6 %collective-permute-start.23 = (bf16[160,256]{1,0:T(8,128)(2,1)S(1)}, bf16[160,256]{1,0:T(8,128)(2,1)S(1)}, u32[]{:S(2)}, u32[]{:S(2)}) collective-permute-start(bf16[160,256]{1,0:T(8,128)(2,1)S(1)} %get-tuple-element.108), channel_id=1, source_target_pairs={{0,15},{1,7},{2,12},{3,4},{4,11},{5,3},{6,8},{7,0},{8,14},{9,6},{1... | collective-permute-start | bytes 245768 | tf_op jit(solution)/shard_map/ppermute | solution.py:490
  74.9 7.3 %collective-permute-start.15 = (bf16[160,256]{1,0:T(8,128)(2,1)S(1)}, bf16[160,256]{1,0:T(8,128)(2,1)S(1)}, u32[]{:S(2)}, u32[]{:S(2)}) collective-permute-start(bf16[160,256]{1,0:T(8,128)(2,1)S(1)} %get-tuple-element.99), channel_id=1, source_target_pairs={{0,0},{1,8},{2,3},{3,11},{4,4},{5,12},{6,7},{7,15},{8,1},{9,9},{10... | collective-permute-start | bytes 245768 | tf_op jit(solution)/shard_map/ppermute | solution.py:490
  75.6 6.6 %collective-permute-start.18 = (bf16[160,256]{1,0:T(8,128)(2,1)S(1)}, bf16[160,256]{1,0:T(8,128)(2,1)S(1)}, u32[]{:S(2)}, u32[]{:S(2)}) collective-permute-start(bf16[160,256]{1,0:T(8,128)(2,1)S(1)} %get-tuple-element.103), channel_id=1, source_target_pairs={{0,4},{1,12},{2,7},{3,15},{4,0},{5,8},{6,3},{7,11},{8,5},{9,13},{1... | collective-permute-start | bytes 245768 | tf_op jit(solution)/shard_map/ppermute | solution.py:490
  77.1 7.0 %collective-permute-start.20 = (bf16[160,256]{1,0:T(8,128)(2,1)S(1)}, bf16[160,256]{1,0:T(8,128)(2,1)S(1)}, u32[]{:S(2)}, u32[]{:S(2)}) collective-permute-start(bf16[160,256]{1,0:T(8,128)(2,1)S(1)} %get-tuple-element.105), channel_id=1, source_target_pairs={{0,8},{1,0},{2,11},{3,3},{4,12},{5,4},{6,15},{7,7},{8,9},{9,1},{10... | collective-permute-start | bytes 245768 | tf_op jit(solution)/shard_map/ppermute | solution.py:490
  82.1 4.6 %collective-permute-start.22 = (bf16[160,256]{1,0:T(8,128)(2,1)S(1)}, bf16[160,256]{1,0:T(8,128)(2,1)S(1)}, u32[]{:S(2)}, u32[]{:S(2)}) collective-permute-start(bf16[160,256]{1,0:T(8,128)(2,1)S(1)} %get-tuple-element.107), channel_id=1, source_target_pairs={{0,12},{1,4},{2,15},{3,7},{4,8},{5,0},{6,11},{7,3},{8,13},{9,5},{1... | collective-permute-start | bytes 245768 | tf_op jit(solution)/shard_map/ppermute | solution.py:490
  (10 other events, 56.3 us)

commit v3 on v2

--- a/solution.py
+++ b/solution.py
@@ -329,7 +329,7 @@
         lax.fori_loop(0, rows // 16, step, 0)
 
 
-def project_kernel(c, g_ref, h0, h1, h2, h3, wa_ref, early, out_late, in_late, keep_ref, send_ref, wb_ref):
+def project_kernel(c, g_ref, h0, h1, h2, h3, h4, wa_ref, early, out_late, in_late, keep_ref, send_ref, wb_ref):
     g, own, core, at_end, cut = g_ref[0], g_ref[2] != c, g_ref[3], g_ref[6], early.shape[0]
     quarter = h0.shape[1]
     half = wa_ref.shape[1] // 2
@@ -338,9 +338,9 @@
 
     def run(weight):
         keep = send = None
-        for m, h in enumerate((h0, h1, h2, h3)):
+        for m, h in enumerate((h0, h1, h2, None)):
             at = pl.ds(pl.multiple_of((g ^ m) * quarter, quarter), quarter)
-            x = h[...]
+            x = h[...] if m < 3 else jnp.concatenate([h3[...], h4[...]], 0)
             a, b = mm(x, weight[at, mine]), mm(x, weight[at, other])
             keep, send = (a, b) if m == 0 else (keep + a, send + b)
         keep_ref[...] = keep
@@ -468,7 +468,9 @@
     )
     hidden, late = lax.optimization_barrier((hidden, out_weight[cut:]))
     in_late = far_swap(late, False)
-    hid = [hidden] + [swap(hidden, SLOT_BITS[m]) for m in (1, 2, 3)]
+    hid = [hidden] + [swap(hidden, SLOT_BITS[m]) for m in (1, 2)]
+    hid[1], hid[2], out_late = lax.optimization_barrier((hid[1], hid[2], out_late))
+    hid += [swap(hid[2][:total // 2], SLOT_BITS[1]), swap(hid[1][total // 2:], SLOT_BITS[2])]
     half = out_weight.shape[1] // 2
     blocks = {}
     for c in (1, 0):

time: 88.3 us -> 87.5 us (level)
  starting transfers between devices: 38.8 us -> 37.4 us
    ppermute x14 -> x15, waiting for transfers between devices: 17.7 us -> 13.8 us  [swap(): return lax.ppermute(block, AXES, [(i, i ^ bits) for i in range(32)])]
    ppermute x2, waiting for transfers between devices: 2.04 us -> 5.87 us  [far_swap(): lax.ppermute(block, AXES, [(i, i ^ BITS_FAR) for i in range(32) if outer(...]
    ppermute x8, starting transfers between devices: 12.4 us -> 11.5 us  [fast_body(): blocks[n, c] = lax.ppermute(part, AXES, homeward(n >> 1, n & 1, c))]
    ppermute x14 -> x15, starting transfers between devices: 20.8 us -> 20.3 us  [swap(): return lax.ppermute(block, AXES, [(i, i ^ bits) for i in range(32)])]
  transfers between devices with their start and end apart: 24 -> 25, of which waited for: 6 -> 8; matrix products, arithmetic and copies ran while one was open for 0% -> 0% of each run, Pallas kernels for 21% -> 21%
where the time goes in v3:
time: 87.5 us; the launch traced here: 87.2 us
  starting transfers between devices  37.4 us (43%)
  waiting for transfers between devices  24.8 us (28%)
  Pallas kernels  21.3 us (24%)
  local copies, waits for them, and re-layouts  3.37 us (4%)
    ppermute x15, starting transfers between devices, swap(): return lax.ppermute(block, AXES, [(i, i ^ bits) for i in range(32)])  20.3 us
    pallas_call x9, Pallas kernels, call(): pl.pallas_call(kernel, out_shape=tuple((jax.ShapeDtypeStruct(s, d) for s,...  19.4 us
    ppermute x15, waiting for transfers between devices, swap(): return lax.ppermute(block, AXES, [(i, i ^ bits) for i in range(32)])  13.8 us
    ppermute x8, starting transfers between devices, fast_body(): blocks[n, c] = lax.ppermute(part, AXES, homeward(n >> 1, n & 1, c))  11.5 us
    ppermute x2, waiting for transfers between devices, far_swap(): lax.ppermute(block, AXES, [(i, i ^ BITS_FAR) for i in range(32) if outer(...  5.87 us
    ppermute x2, starting transfers between devices, far_swap(): lax.ppermute(block, AXES, [(i, i ^ BITS_FAR) for i in range(32) if outer(...  5.61 us
    ppermute x8, waiting for transfers between devices, fast_body(): blocks[n, c] = lax.ppermute(part, AXES, homeward(n >> 1, n & 1, c))  5.12 us
    unnamed x20, local copies, waits for them, and re-layouts  2.13 us
  transfers between devices with their start and end apart: 25, of which 8 were waited for; matrix products, arithmetic and copies ran while one was open for 0% of the time, Pallas kernels for 21%

profile of v3, /device:TPU:0, one launch (start us, length us, event | category | flops | bytes accessed | tf_op | source)
XLA Modules:
  0.0 87.2 jit_solution(13785946056268994188)
XLA Ops:
  1.1 5.1 %collective-permute-start.3 = (bf16[576,512]{1,0:T(8,128)(2,1)S(1)}, bf16[576,512]{1,0:T(8,128)(2,1)S(1)}, u32[]{:S(2)}, u32[]{:S(2)}) collective-permute-start(bf16[576,512]{1,0:T(8,128)(2,1)S(1)} %slice.13), channel_id=1, source_target_pairs={{0,24},{1,25},{2,26},{3,27},{4,28},{5,29},{6,30},{7,31},{8,16},{9,... | collective-permute-start | bytes 1769480 | tf_op jit(solution)/shard_map/ppermute | solution.py:22
  8.4 1.9 %shard_map.92 = (bf16[208,256]{1,0:T(8,128)(2,1)S(1)}, bf16[208,256]{1,0:T(8,128)(2,1)S(1)}, bf16[208,256]{1,0:T(8,128)(2,1)S(1)}, bf16[208,256]{1,0:T(8,128)(2,...) custom-call(s32[7]{0:T(128)S(1)} %stack.39.refs_0_.g_ref, ...), custom_call_target="tpu_custom_call" | custom-call | flops 2000000000 | bytes 6000000 | tf_op jit(solution)/shard_map/pallas_call | solution.py:418
  10.4 1.6 %collective-permute-start = (bf16[208,256]{1,0:T(8,128)(2,1)S(1)}, bf16[208,256]{1,0:T(8,128)(2,1)S(1)}, u32[]{:S(2)}, u32[]{:S(2)}) collective-permute-start(bf16[208,256]{1,0:T(8,128)(2,1)S(1)} %get-tuple-element.72), channel_id=1, source_target_pairs={{0,4},{1,5},{2,6},{3,7},{4,0},{5,1},{6,2},{7,3},{8,12},{9,13},{10,... | collective-permute-start | bytes 319496 | tf_op jit(solution)/shard_map/ppermute | solution.py:22
  12.0 2.0 %collective-permute-start.2 = (bf16[208,256]{1,0:T(8,128)(2,1)S(1)}, bf16[208,256]{1,0:T(8,128)(2,1)S(1)}, u32[]{:S(2)}, u32[]{:S(2)}) collective-permute-start(bf16[208,256]{1,0:T(8,128)(2,1)S(1)} %get-tuple-element.74), channel_id=1, source_target_pairs={{0,12},{1,13},{2,14},{3,15},{4,8},{5,9},{6,10},{7,11},{8,4},{9,5},... | collective-permute-start | bytes 319496 | tf_op jit(solution)/shard_map/ppermute | solution.py:22
  14.0 2.6 %shard_map.91 = (f32[288,256]{1,0:T(8,128)S(1)}, f32[320,256]{1,0:T(8,128)S(1)}, f32[16,160,256]{2,1,0:T(8,128)S(1)}, f32[16,160,256]{2,1,0:T(8,128)S(1)}, f32[4...) custom-call(s32[7]{0:T(128)S(1)} %stack.39.refs_0_.g_ref, f32[128,1024]{1,0:T(8,128)S(1)} %copy-done.2, ...), custom_call_target="tpu_custom_call" | custom-call | flops 345000000 | bytes 1107000 | tf_op jit(solution)/shard_map/pallas_call | solution.py:387
  16.6 1.6 %collective-permute-start.6 = (bf16[160,256]{1,0:T(8,128)(2,1)S(1)}, bf16[160,256]{1,0:T(8,128)(2,1)S(1)}, u32[]{:S(2)}, u32[]{:S(2)}) collective-permute-start(bf16[160,256]{1,0:T(8,128)(2,1)S(1)} %get-tuple-element.85), channel_id=1, source_target_pairs={{0,4},{1,5},{2,6},{3,7},{4,0},{5,1},{6,2},{7,3},{8,12},{9,13},{10,... | collective-permute-start | bytes 245768 | tf_op jit(solution)/shard_map/ppermute | solution.py:22
  18.2 4.1 %collective-permute-done.1.refs_9_ = bf16[208,256]{1,0:T(8,128)(2,1)S(1)} collective-permute-done((bf16[208,256]{1,0:T(8,128)(2,1)S(1)}, bf16[208,256]{1,0:T(8,128)(2,1)S(1)}, u32[]{:S(2)}, u32[]{:S(2)}) %collective-permute-start.1) | collective-permute-done | bytes 106528 | tf_op jit(solution)/shard_map/ppermute | solution.py:22
  22.3 3.4 %collective-permute-start.8 = (bf16[160,256]{1,0:T(8,128)(2,1)S(1)}, bf16[160,256]{1,0:T(8,128)(2,1)S(1)}, u32[]{:S(2)}, u32[]{:S(2)}) collective-permute-start(bf16[160,256]{1,0:T(8,128)(2,1)S(1)} %get-tuple-element.87), channel_id=1, source_target_pairs={{0,12},{1,13},{2,14},{3,15},{4,8},{5,9},{6,10},{7,11},{8,4},{9,5},... | collective-permute-start | bytes 245768 | tf_op jit(solution)/shard_map/ppermute | solution.py:22
  25.7 4.3 %shard_map.93 = (f32[4,160,256]{2,1,0:T(8,128)S(1)}, f32[4,2,16,256]{3,2,1,0:T(8,128)S(1)}, f32[40,256]{1,0:T(8,128)S(1)}, bf16[160,256]{1,0:T(8,128)(2,1)S(1)},...) custom-call(s32[7]{0:T(128)S(1)} %stack.39.refs_0_.g_ref, f32[3,7,256]{2,1,0:T(8,128)S(1)} %get-tuple-element.61.refs_1_, ...), custom_call_target="tpu_custom_call" | custom-call | flops 690000000 | bytes 2214000 | tf_op jit(solution)/shard_map/pallas_call | solution.py:387
  30.0 2.9 %collective-permute-start.5 = (bf16[160,256]{1,0:T(8,128)(2,1)S(1)}, bf16[160,256]{1,0:T(8,128)(2,1)S(1)}, u32[]{:S(2)}, u32[]{:S(2)}) collective-permute-start(bf16[160,256]{1,0:T(8,128)(2,1)S(1)} %get-tuple-element.78), channel_id=1, source_target_pairs={{0,16},{1,17},{2,18},{3,19},{4,20},{5,21},{6,22},{7,23},{8,24},{9,... | collective-permute-start | bytes 245768 | tf_op jit(solution)/shard_map/ppermute | solution.py:22
  33.0 2.2 %shard_map.94 = (f32[3,160,256]{2,1,0:T(8,128)S(1)}, f32[640,256]{1,0:T(8,128)S(1)}) custom-call(s32[7]{0:T(128)S(1)} %stack.39.refs_0_.g_ref, f32[3,7,256]{2,1,0:T(8,128)S(1)} %get-tuple-element.61.refs_1_, f32[4,160,256]{2,1,0:T(8,128)S(1)} %get-tuple-element.83.refs_2_, f32[320,256]{1,0:T(8,128)S(1)} %get-tuple-element.81.refs_3_.refs_7_, ...), custom_call_target="tpu_custom_call" | custom-call | flops 3564999936 | bytes 11439000 | tf_op jit(solution)/shard_map/pallas_call | solution.py:387
  35.2 4.9 %collective-permute-start.11 = (bf16[448,512]{1,0:T(8,128)(2,1)S(1)}, bf16[448,512]{1,0:T(8,128)(2,1)S(1)}, u32[]{:S(2)}, u32[]{:S(2)}) collective-permute-start(bf16[448,512]{1,0:T(8,128)(2,1)S(1)} %slice.14), channel_id=1, source_target_pairs={{0,24},{1,25},{2,26},{3,27},{4,28},{5,29},{6,30},{7,31},{24,0},{25... | collective-permute-start | bytes 1376264 | tf_op jit(solution)/shard_map/ppermute | solution.py:39
  40.2 5.0 %shard_map.95.refs_1_ = bf16[640,256]{1,0:T(8,128)(2,1)S(1)} custom-call(s32[7]{0:T(128)S(1)} %stack.39.refs_0_.g_ref, f32[3,7,256]{2,1,0:T(8,128)S(1)} %get-tuple-element.61.refs_1_, f32[40,256]{1,0:T(8,128)S(1)} %collective-permute-done.4.refs_2_, bf16[160,256]{1,0:T(8,128)(2,1)S(1)} %collective-permute-done.5.refs_3_, ...), custom_call_target="tpu_custom_call" | custom-call | flops 5980000256 | bytes 19188000 | tf_op jit(solution)/shard_map/pallas_call | solution.py:387
  46.5 5.9 %collective-permute-done.11.refs_8_ = bf16[448,512]{1,0:T(8,128)(2,1)S(1)} collective-permute-done((bf16[448,512]{1,0:T(8,128)(2,1)S(1)}, bf16[448,512]{1,0:T(8,128)(2,1)S(1)}, u32[]{:S(2)}, u32[]{:S(2)}) %collective-permute-start.11) | collective-permute-done | bytes 458784 | tf_op jit(solution)/shard_map/ppermute | solution.py:39
  52.4 4.8 %collective-permute-done.10.refs_3_ = bf16[640,256]{1,0:T(8,128)(2,1)S(1)} collective-permute-done((bf16[640,256]{1,0:T(8,128)(2,1)S(1)}, bf16[640,256]{1,0:T(8,128)(2,1)S(1)}, u32[]{:S(2)}, u32[]{:S(2)}) %collective-permute-start.10) | collective-permute-done | bytes 327712 | tf_op jit(solution)/shard_map/ppermute | solution.py:22
  59.7 3.4 %collective-permute-done.12.refs_4_ = bf16[320,256]{1,0:T(8,128)(2,1)S(1)} collective-permute-done((bf16[320,256]{1,0:T(8,128)(2,1)S(1)}, bf16[320,256]{1,0:T(8,128)(2,1)S(1)}, u32[]{:S(2)}, u32[]{:S(2)}) %collective-permute-start.12) | collective-permute-done | bytes 163872 | tf_op jit(solution)/shard_map/ppermute | solution.py:22
  63.1 1.4 %collective-permute-done.13.refs_5_ = bf16[320,256]{1,0:T(8,128)(2,1)S(1)} collective-permute-done((bf16[320,256]{1,0:T(8,128)(2,1)S(1)}, bf16[320,256]{1,0:T(8,128)(2,1)S(1)}, u32[]{:S(2)}, u32[]{:S(2)}) %collective-permute-start.13) | collective-permute-done | bytes 163872 | tf_op jit(solution)/shard_map/ppermute | solution.py:22
  64.5 1.5 %shard_map.96 = (f32[640,256]{1,0:T(8,128)S(1)}, bf16[640,256]{1,0:T(8,128)(2,1)S(1)}) custom-call(s32[7]{0:T(128)S(1)} %stack.39.refs_0_.g_ref, bf16[640,256]{1,0:T(8,128)(2,1)S(1)} %shard_map.95.refs_1_, bf16[640,256]{1,0:T(8,128)(2,1)S(1)} %collective-permute-done.9.refs_2_, bf16[640,256]{1,0:T(8,128)(2,1)S(1)} %collective-permute-done.10.refs_3_, ...), custom_call_target="tpu_custom_call" | custom-call | flops 1380000000 | bytes 4428000 | tf_op jit(solution)/shard_map/pallas_call | solution.py:387
  66.0 1.4 %shard_map.97 = (f32[640,256]{1,0:T(8,128)S(1)}, bf16[640,256]{1,0:T(8,128)(2,1)S(1)}) custom-call(s32[7]{0:T(128)S(1)} %stack.39.refs_0_.g_ref, bf16[640,256]{1,0:T(8,128)(2,1)S(1)} %shard_map.95.refs_1_, bf16[640,256]{1,0:T(8,128)(2,1)S(1)} %collective-permute-done.9.refs_2_, bf16[640,256]{1,0:T(8,128)(2,1)S(1)} %collective-permute-done.10.refs_3_, ...), custom_call_target="tpu_custom_call" | custom-call | flops 1380000000 | bytes 4428000 | tf_op jit(solution)/shard_map/pallas_call | solution.py:387
  69.8 1.5 %collective-permute-start.20 = (bf16[160,256]{1,0:T(8,128)(2,1)S(1)}, bf16[160,256]{1,0:T(8,128)(2,1)S(1)}, u32[]{:S(2)}, u32[]{:S(2)}) collective-permute-start(bf16[160,256]{1,0:T(8,128)(2,1)S(1)} %get-tuple-element.112), channel_id=1, source_target_pairs={{0,7},{1,15},{2,4},{3,12},{4,3},{5,11},{6,0},{7,8},{8,6},{9,14},{1... | collective-permute-start | bytes 245768 | tf_op jit(solution)/shard_map/ppermute | solution.py:492
  74.5 1.5 %collective-permute-start.19 = (bf16[160,256]{1,0:T(8,128)(2,1)S(1)}, bf16[160,256]{1,0:T(8,128)(2,1)S(1)}, u32[]{:S(2)}, u32[]{:S(2)}) collective-permute-start(bf16[160,256]{1,0:T(8,128)(2,1)S(1)} %get-tuple-element.111), channel_id=1, source_target_pairs={{0,4},{1,12},{2,7},{3,15},{4,0},{5,8},{6,3},{7,11},{8,5},{9,13},{1... | collective-permute-start | bytes 245768 | tf_op jit(solution)/shard_map/ppermute | solution.py:492
  77.0 4.0 %collective-permute-start.21 = (bf16[160,256]{1,0:T(8,128)(2,1)S(1)}, bf16[160,256]{1,0:T(8,128)(2,1)S(1)}, u32[]{:S(2)}, u32[]{:S(2)}) collective-permute-start(bf16[160,256]{1,0:T(8,128)(2,1)S(1)} %get-tuple-element.113), channel_id=1, source_target_pairs={{0,8},{1,0},{2,11},{3,3},{4,12},{5,4},{6,15},{7,7},{8,9},{9,1},{10... | collective-permute-start | bytes 245768 | tf_op jit(solution)/shard_map/ppermute | solution.py:492
  81.7 1.4 %collective-permute-done.21.refs_4_ = bf16[160,256]{1,0:T(8,128)(2,1)S(1)} collective-permute-done((bf16[160,256]{1,0:T(8,128)(2,1)S(1)}, bf16[160,256]{1,0:T(8,128)(2,1)S(1)}, u32[]{:S(2)}, u32[]{:S(2)}) %collective-permute-start.21) | collective-permute-done | bytes 81952 | tf_op jit(solution)/shard_map/ppermute | solution.py:492
  83.1 2.8 %collective-permute-done.23.refs_6_ = bf16[160,256]{1,0:T(8,128)(2,1)S(1)} collective-permute-done((bf16[160,256]{1,0:T(8,128)(2,1)S(1)}, bf16[160,256]{1,0:T(8,128)(2,1)S(1)}, u32[]{:S(2)}, u32[]{:S(2)}) %collective-permute-start.23) | collective-permute-done | bytes 81952 | tf_op jit(solution)/shard_map/ppermute | solution.py:492
  (61 shorter events, 15.8 us)
Async XLA Ops:
  1.1 28.9 %collective-permute-start.3 = (bf16[576,512]{1,0:T(8,128)(2,1)S(1)}, bf16[576,512]{1,0:T(8,128)(2,1)S(1)}, u32[]{:S(2)}, u32[]{:S(2)}) collective-permute-start(bf16[576,512]{1,0:T(8,128)(2,1)S(1)} %slice.13), channel_id=1, source_target_pairs={{0,24},{1,25},{2,26},{3,27},{4,28},{5,29},{6,30},{7,31},{8,16},{9,... | collective-permute-start | bytes 1769480 | tf_op jit(solution)/shard_map/ppermute | solution.py:22
  10.4 7.7 %collective-permute-start = (bf16[208,256]{1,0:T(8,128)(2,1)S(1)}, bf16[208,256]{1,0:T(8,128)(2,1)S(1)}, u32[]{:S(2)}, u32[]{:S(2)}) collective-permute-start(bf16[208,256]{1,0:T(8,128)(2,1)S(1)} %get-tuple-element.72), channel_id=1, source_target_pairs={{0,4},{1,5},{2,6},{3,7},{4,0},{5,1},{6,2},{7,3},{8,12},{9,13},{10,... | collective-permute-start | bytes 319496 | tf_op jit(solution)/shard_map/ppermute | solution.py:22
  12.0 10.3 %collective-permute-start.1 = (bf16[208,256]{1,0:T(8,128)(2,1)S(1)}, bf16[208,256]{1,0:T(8,128)(2,1)S(1)}, u32[]{:S(2)}, u32[]{:S(2)}) collective-permute-start(bf16[208,256]{1,0:T(8,128)(2,1)S(1)} %get-tuple-element.73), channel_id=1, source_target_pairs={{0,8},{1,9},{2,10},{3,11},{4,12},{5,13},{6,14},{7,15},{8,0},{9,1},... | collective-permute-start | bytes 319496 | tf_op jit(solution)/shard_map/ppermute | solution.py:22
  12.0 13.8 %collective-permute-start.2 = (bf16[208,256]{1,0:T(8,128)(2,1)S(1)}, bf16[208,256]{1,0:T(8,128)(2,1)S(1)}, u32[]{:S(2)}, u32[]{:S(2)}) collective-permute-start(bf16[208,256]{1,0:T(8,128)(2,1)S(1)} %get-tuple-element.74), channel_id=1, source_target_pairs={{0,12},{1,13},{2,14},{3,15},{4,8},{5,9},{6,10},{7,11},{8,4},{9,5},... | collective-permute-start | bytes 319496 | tf_op jit(solution)/shard_map/ppermute | solution.py:22
  16.6 16.5 %collective-permute-start.6 = (bf16[160,256]{1,0:T(8,128)(2,1)S(1)}, bf16[160,256]{1,0:T(8,128)(2,1)S(1)}, u32[]{:S(2)}, u32[]{:S(2)}) collective-permute-start(bf16[160,256]{1,0:T(8,128)(2,1)S(1)} %get-tuple-element.85), channel_id=1, source_target_pairs={{0,4},{1,5},{2,6},{3,7},{4,0},{5,1},{6,2},{7,3},{8,12},{9,13},{10,... | collective-permute-start | bytes 245768 | tf_op jit(solution)/shard_map/ppermute | solution.py:22
  18.1 14.9 %collective-permute-start.7 = (bf16[160,256]{1,0:T(8,128)(2,1)S(1)}, bf16[160,256]{1,0:T(8,128)(2,1)S(1)}, u32[]{:S(2)}, u32[]{:S(2)}) collective-permute-start(bf16[160,256]{1,0:T(8,128)(2,1)S(1)} %get-tuple-element.86), channel_id=1, source_target_pairs={{0,8},{1,9},{2,10},{3,11},{4,12},{5,13},{6,14},{7,15},{8,0},{9,1},... | collective-permute-start | bytes 245768 | tf_op jit(solution)/shard_map/ppermute | solution.py:22
  22.3 10.8 %collective-permute-start.8 = (bf16[160,256]{1,0:T(8,128)(2,1)S(1)}, bf16[160,256]{1,0:T(8,128)(2,1)S(1)}, u32[]{:S(2)}, u32[]{:S(2)}) collective-permute-start(bf16[160,256]{1,0:T(8,128)(2,1)S(1)} %get-tuple-element.87), channel_id=1, source_target_pairs={{0,12},{1,13},{2,14},{3,15},{4,8},{5,9},{6,10},{7,11},{8,4},{9,5},... | collective-permute-start | bytes 245768 | tf_op jit(solution)/shard_map/ppermute | solution.py:22
  30.0 10.2 %collective-permute-start.5 = (bf16[160,256]{1,0:T(8,128)(2,1)S(1)}, bf16[160,256]{1,0:T(8,128)(2,1)S(1)}, u32[]{:S(2)}, u32[]{:S(2)}) collective-permute-start(bf16[160,256]{1,0:T(8,128)(2,1)S(1)} %get-tuple-element.78), channel_id=1, source_target_pairs={{0,16},{1,17},{2,18},{3,19},{4,20},{5,21},{6,22},{7,23},{8,24},{9,... | collective-permute-start | bytes 245768 | tf_op jit(solution)/shard_map/ppermute | solution.py:22
  32.9 7.3 %collective-permute-start.4 = (f32[40,256]{1,0:T(8,128)S(1)}, f32[40,256]{1,0:T(8,128)S(1)}, u32[]{:S(2)}, u32[]{:S(2)}) collective-permute-start(f32[40,256]{1,0:T(8,128)S(1)} %get-tuple-element.77), channel_id=1, source_target_pairs={{0,16},{1,17},{2,18},{3,19},{4,20},{5,21},{6,22},{7,23},{8,24},{9,... | collective-permute-start | bytes 122888 | tf_op jit(solution)/shard_map/ppermute | solution.py:22
  35.2 17.2 %collective-permute-start.11 = (bf16[448,512]{1,0:T(8,128)(2,1)S(1)}, bf16[448,512]{1,0:T(8,128)(2,1)S(1)}, u32[]{:S(2)}, u32[]{:S(2)}) collective-permute-start(bf16[448,512]{1,0:T(8,128)(2,1)S(1)} %slice.14), channel_id=1, source_target_pairs={{0,24},{1,25},{2,26},{3,27},{4,28},{5,29},{6,30},{7,31},{24,0},{25... | collective-permute-start | bytes 1376264 | tf_op jit(solution)/shard_map/ppermute | solution.py:39
  45.2 12.1 %collective-permute-start.10 = (bf16[640,256]{1,0:T(8,128)(2,1)S(1)}, bf16[640,256]{1,0:T(8,128)(2,1)S(1)}, u32[]{:S(2)}, u32[]{:S(2)}) collective-permute-start(bf16[640,256]{1,0:T(8,128)(2,1)S(1)} %shard_map.95.refs_1_), channel_id=1, source_target_pairs={{0,8},{1,9},{2,10},{3,11},{4,12},{5,13},{6,14},{7,15},{8,0},{9,1},... | collective-permute-start | bytes 983048 | tf_op jit(solution)/shard_map/ppermute | solution.py:22
  45.2 12.0 %collective-permute-start.9 = (bf16[640,256]{1,0:T(8,128)(2,1)S(1)}, bf16[640,256]{1,0:T(8,128)(2,1)S(1)}, u32[]{:S(2)}, u32[]{:S(2)}) collective-permute-start(bf16[640,256]{1,0:T(8,128)(2,1)S(1)} %shard_map.95.refs_1_), channel_id=1, source_target_pairs={{0,4},{1,5},{2,6},{3,7},{4,0},{5,1},{6,2},{7,3},{8,12},{9,13},{10,... | collective-permute-start | bytes 983048 | tf_op jit(solution)/shard_map/ppermute | solution.py:22
  45.8 13.8 %collective-permute-start.14 = (bf16[448,512]{1,0:T(8,128)(2,1)S(1)}, bf16[448,512]{1,0:T(8,128)(2,1)S(1)}, u32[]{:S(2)}, u32[]{:S(2)}) collective-permute-start(bf16[448,512]{1,0:T(8,128)(2,1)S(1)} %slice.14), channel_id=1, source_target_pairs={{8,16},{9,17},{10,18},{11,19},{12,20},{13,21},{14,22},{15,23},{16,... | collective-permute-start | bytes 1376264 | tf_op jit(solution)/shard_map/ppermute | solution.py:39
  57.2 5.8 %collective-permute-start.12 = (bf16[320,256]{1,0:T(8,128)(2,1)S(1)}, bf16[320,256]{1,0:T(8,128)(2,1)S(1)}, u32[]{:S(2)}, u32[]{:S(2)}) collective-permute-start(bf16[320,256]{1,0:T(8,128)(2,1)S(1)} %slice.15), channel_id=1, source_target_pairs={{0,4},{1,5},{2,6},{3,7},{4,0},{5,1},{6,2},{7,3},{8,12},{9,13},{10,... | collective-permute-start | bytes 491528 | tf_op jit(solution)/shard_map/ppermute | solution.py:22
  58.6 5.9 %collective-permute-start.13 = (bf16[320,256]{1,0:T(8,128)(2,1)S(1)}, bf16[320,256]{1,0:T(8,128)(2,1)S(1)}, u32[]{:S(2)}, u32[]{:S(2)}) collective-permute-start(bf16[320,256]{1,0:T(8,128)(2,1)S(1)} %slice.16), channel_id=1, source_target_pairs={{0,8},{1,9},{2,10},{3,11},{4,12},{5,13},{6,14},{7,15},{8,0},{9,1},... | collective-permute-start | bytes 491528 | tf_op jit(solution)/shard_map/ppermute | solution.py:22
  67.4 5.8 %collective-permute-start.15 = (bf16[640,256]{1,0:T(8,128)(2,1)S(1)}, bf16[640,256]{1,0:T(8,128)(2,1)S(1)}, u32[]{:S(2)}, u32[]{:S(2)}) collective-permute-start(bf16[640,256]{1,0:T(8,128)(2,1)S(1)} %get-tuple-element.106), channel_id=1, source_target_pairs={{0,1},{1,0},{2,3},{3,2},{4,5},{5,4},{6,7},{7,6},{8,9},{9,8},{10,11... | collective-permute-start | bytes 983048 | tf_op jit(solution)/shard_map/ppermute | solution.py:22
  68.6 5.9 %collective-permute-start.18 = (bf16[160,256]{1,0:T(8,128)(2,1)S(1)}, bf16[160,256]{1,0:T(8,128)(2,1)S(1)}, u32[]{:S(2)}, u32[]{:S(2)}) collective-permute-start(bf16[160,256]{1,0:T(8,128)(2,1)S(1)} %get-tuple-element.110), channel_id=1, source_target_pairs={{0,3},{1,11},{2,0},{3,8},{4,7},{5,15},{6,4},{7,12},{8,2},{9,10},{1... | collective-permute-start | bytes 245768 | tf_op jit(solution)/shard_map/ppermute | solution.py:492
  69.8 7.2 %collective-permute-start.20 = (bf16[160,256]{1,0:T(8,128)(2,1)S(1)}, bf16[160,256]{1,0:T(8,128)(2,1)S(1)}, u32[]{:S(2)}, u32[]{:S(2)}) collective-permute-start(bf16[160,256]{1,0:T(8,128)(2,1)S(1)} %get-tuple-element.112), channel_id=1, source_target_pairs={{0,7},{1,15},{2,4},{3,12},{4,3},{5,11},{6,0},{7,8},{8,6},{9,14},{1... | collective-permute-start | bytes 245768 | tf_op jit(solution)/shard_map/ppermute | solution.py:492
  71.3 9.8 %collective-permute-start.22 = (bf16[160,256]{1,0:T(8,128)(2,1)S(1)}, bf16[160,256]{1,0:T(8,128)(2,1)S(1)}, u32[]{:S(2)}, u32[]{:S(2)}) collective-permute-start(bf16[160,256]{1,0:T(8,128)(2,1)S(1)} %get-tuple-element.114), channel_id=1, source_target_pairs={{0,11},{1,3},{2,8},{3,0},{4,15},{5,7},{6,12},{7,4},{8,10},{9,2},{1... | collective-permute-start | bytes 245768 | tf_op jit(solution)/shard_map/ppermute | solution.py:492
  72.5 9.1 %collective-permute-start.24 = (bf16[160,256]{1,0:T(8,128)(2,1)S(1)}, bf16[160,256]{1,0:T(8,128)(2,1)S(1)}, u32[]{:S(2)}, u32[]{:S(2)}) collective-permute-start(bf16[160,256]{1,0:T(8,128)(2,1)S(1)} %get-tuple-element.116), channel_id=1, source_target_pairs={{0,15},{1,7},{2,12},{3,4},{4,11},{5,3},{6,8},{7,0},{8,14},{9,6},{1... | collective-permute-start | bytes 245768 | tf_op jit(solution)/shard_map/ppermute | solution.py:492
  73.9 7.8 %collective-permute-start.16 = (bf16[160,256]{1,0:T(8,128)(2,1)S(1)}, bf16[160,256]{1,0:T(8,128)(2,1)S(1)}, u32[]{:S(2)}, u32[]{:S(2)}) collective-permute-start(bf16[160,256]{1,0:T(8,128)(2,1)S(1)} %get-tuple-element.107), channel_id=1, source_target_pairs={{0,0},{1,8},{2,3},{3,11},{4,4},{5,12},{6,7},{7,15},{8,1},{9,9},{10... | collective-permute-start | bytes 245768 | tf_op jit(solution)/shard_map/ppermute | solution.py:492
  74.5 7.1 %collective-permute-start.19 = (bf16[160,256]{1,0:T(8,128)(2,1)S(1)}, bf16[160,256]{1,0:T(8,128)(2,1)S(1)}, u32[]{:S(2)}, u32[]{:S(2)}) collective-permute-start(bf16[160,256]{1,0:T(8,128)(2,1)S(1)} %get-tuple-element.111), channel_id=1, source_target_pairs={{0,4},{1,12},{2,7},{3,15},{4,0},{5,8},{6,3},{7,11},{8,5},{9,13},{1... | collective-permute-start | bytes 245768 | tf_op jit(solution)/shard_map/ppermute | solution.py:492
  77.0 6.1 %collective-permute-start.21 = (bf16[160,256]{1,0:T(8,128)(2,1)S(1)}, bf16[160,256]{1,0:T(8,128)(2,1)S(1)}, u32[]{:S(2)}, u32[]{:S(2)}) collective-permute-start(bf16[160,256]{1,0:T(8,128)(2,1)S(1)} %get-tuple-element.113), channel_id=1, source_target_pairs={{0,8},{1,0},{2,11},{3,3},{4,12},{5,4},{6,15},{7,7},{8,9},{9,1},{10... | collective-permute-start | bytes 245768 | tf_op jit(solution)/shard_map/ppermute | solution.py:492
  81.0 4.8 %collective-permute-start.23 = (bf16[160,256]{1,0:T(8,128)(2,1)S(1)}, bf16[160,256]{1,0:T(8,128)(2,1)S(1)}, u32[]{:S(2)}, u32[]{:S(2)}) collective-permute-start(bf16[160,256]{1,0:T(8,128)(2,1)S(1)} %get-tuple-element.115), channel_id=1, source_target_pairs={{0,12},{1,4},{2,15},{3,7},{4,8},{5,0},{6,11},{7,3},{8,13},{9,5},{1... | collective-permute-start | bytes 245768 | tf_op jit(solution)/shard_map/ppermute | solution.py:492
  (11 other events, 58.4 us)

commit v4 on v3

--- a/solution.py
+++ b/solution.py
@@ -329,40 +329,38 @@
         lax.fori_loop(0, rows // 16, step, 0)
 
 
-def project_kernel(c, g_ref, h0, h1, h2, h3, h4, wa_ref, early, out_late, in_late, keep_ref, send_ref, wb_ref):
-    g, own, core, at_end, cut = g_ref[0], g_ref[2] != c, g_ref[3], g_ref[6], early.shape[0]
+def halves(core, wide):
+    half = wide // 2
+    return [pl.ds(pl.multiple_of(k * half, half), half) for k in (core, 1 - core)]
+
+
+def project_kernel(g_ref, h0, h1, h2, wa_ref, early, out_late, in_late, acc_ref, wb_ref):
+    g, same, core, at_end, cut = g_ref[0], g_ref[2], g_ref[3], g_ref[6], early.shape[0]
     quarter = h0.shape[1]
-    half = wa_ref.shape[1] // 2
-    mine = pl.ds(pl.multiple_of(core * half, half), half)
-    other = pl.ds(pl.multiple_of((1 - core) * half, half), half)
-
-    def run(weight):
-        keep = send = None
-        for m, h in enumerate((h0, h1, h2, None)):
-            at = pl.ds(pl.multiple_of((g ^ m) * quarter, quarter), quarter)
-            x = h[...] if m < 3 else jnp.concatenate([h3[...], h4[...]], 0)
-            a, b = mm(x, weight[at, mine]), mm(x, weight[at, other])
-            keep, send = (a, b) if m == 0 else (keep + a, send + b)
-        keep_ref[...] = keep
-        send_ref[...] = send.astype(BF16)
-
-    @pl.when(own)
+    wb_ref[:cut] = early[...]
+
+    @pl.when(at_end > 0)
     def _():
-        run(wa_ref)
-
-    @pl.when(jnp.logical_not(own))
+        wb_ref[cut:] = out_late[...]
+
+    @pl.when(at_end == 0)
     def _():
-        wb_ref[:cut] = early[...]
-
-        @pl.when(at_end > 0)
-        def _():
-            wb_ref[cut:] = out_late[...]
-
-        @pl.when(at_end == 0)
-        def _():
-            wb_ref[cut:] = in_late[...]
-
-        run(wb_ref)
+        wb_ref[cut:] = in_late[...]
+
+    at = [pl.ds(pl.multiple_of((g ^ m) * quarter, quarter), quarter) for m in range(GROUP - 1)]
+    x = jnp.concatenate([h0[...], h1[...], h2[...]], 1)
+    for weight, c in ((wa_ref, 1 - same), (wb_ref, same)):
+        for k, cols in enumerate(halves(core, wa_ref.shape[1])):
+            acc_ref[c, k] = mm(x, jnp.concatenate([weight[a, cols] for a in at], 0))
+
+
+def finish_kernel(c, g_ref, acc_ref, top, low, wa_ref, wb_ref, keep_ref, send_ref):
+    own, quarter = g_ref[2] != c, top.shape[1]
+    at = pl.ds(pl.multiple_of((g_ref[0] ^ (GROUP - 1)) * quarter, quarter), quarter)
+    x = jnp.concatenate([top[...], low[...]], 0)
+    mine, other = [mm(x, jnp.where(own, wa_ref[at, cols], wb_ref[at, cols])) for cols in halves(g_ref[3], wa_ref.shape[1])]
+    send_ref[...] = (acc_ref[c, 1] + other).astype(BF16)
+    keep_ref[...] = acc_ref[c, 0] + mine
 
 
 def sort_kernel(rows, g_ref, keep_ref, got_ref, *outs):
@@ -469,19 +467,25 @@
     hidden, late = lax.optimization_barrier((hidden, out_weight[cut:]))
     in_late = far_swap(late, False)
     hid = [hidden] + [swap(hidden, SLOT_BITS[m]) for m in (1, 2)]
-    hid[1], hid[2], out_late = lax.optimization_barrier((hid[1], hid[2], out_late))
-    hid += [swap(hid[2][:total // 2], SLOT_BITS[1]), swap(hid[1][total // 2:], SLOT_BITS[2])]
+    hid[1], out_late = lax.optimization_barrier((hid[1], out_late))
+    passed = swap(hid[1][rows:], SLOT_BITS[2])
+    hid += [swap(hid[2][:rows], SLOT_BITS[1]), passed]
     half = out_weight.shape[1] // 2
-    blocks = {}
+    acc, far = call(
+        2.0,
+        project_kernel,
+        [((2, 2, total, half), F32), ((width, 2 * half), BF16)],
+        (scal, *hid[:3], out_weight, early, out_late, in_late),
+    )
+    blocks, last = {}, hid[3:]
     for c in (1, 0):
         keep, send = call(
-            1.2,
-            lambda *refs: project_kernel(c, *refs),
+            0.8,
+            lambda *refs: finish_kernel(c, *refs),
             [((total, half), F32), ((total, half), BF16)],
-            (scal, *hid, out_weight, early, out_late, in_late),
-            [((width, 2 * half), BF16)],
+            (scal, acc, *last, out_weight, far),
         )
-        send, hid = lax.optimization_barrier((send, hid))
+        send, last = lax.optimization_barrier((send, last))
         parts = call(
             0.4,
             lambda *refs: sort_kernel(rows, *refs),

time: 87.5 us -> 85.9 us (0.982)
  waiting for transfers between devices: 24.8 us -> 19.5 us
  starting transfers between devices: 37.4 us -> 40.3 us
  Pallas kernels: 21.3 us -> 22.3 us
    ppermute x8, starting transfers between devices: 11.5 us -> 13.9 us  [fast_body(): blocks[n, c] = lax.ppermute(part, AXES, homeward(n >> 1, n & 1, c))]
    ppermute x2, waiting for transfers between devices: 5.87 us -> 3.61 us  [far_swap(): lax.ppermute(block, AXES, [(i, i ^ BITS_FAR) for i in range(32) if outer(...]
    ppermute x15, waiting for transfers between devices: 13.8 us -> 12.1 us  [swap(): return lax.ppermute(block, AXES, [(i, i ^ bits) for i in range(32)])]
    ppermute x8, waiting for transfers between devices: 5.12 us -> 3.84 us  [fast_body(): blocks[n, c] = lax.ppermute(part, AXES, homeward(n >> 1, n & 1, c))]
    pallas_call x9 -> x10, Pallas kernels: 19.4 us -> 20.3 us  [call(): pl.pallas_call(kernel, out_shape=tuple((jax.ShapeDtypeStruct(s, d) for s,...]
    unnamed x20 -> x18, local copies, waits for them, and re-layouts: 2.13 us -> 2.13 us
  transfers between devices with their start and end apart: 25 -> 25, of which waited for: 8 -> 8; matrix products, arithmetic and copies ran while one was open for 0% -> 0% of each run, Pallas kernels for 21% -> 23%
where the time goes in v4:
time: 85.9 us; the launch traced here: 85.6 us
  starting transfers between devices  40.3 us (47%)
  Pallas kernels  22.3 us (26%)
  waiting for transfers between devices  19.5 us (23%)
  local copies, waits for them, and re-layouts  3.37 us (4%)
    ppermute x15, starting transfers between devices, swap(): return lax.ppermute(block, AXES, [(i, i ^ bits) for i in range(32)])  20.7 us
    pallas_call x10, Pallas kernels, call(): pl.pallas_call(kernel, out_shape=tuple((jax.ShapeDtypeStruct(s, d) for s,...  20.3 us
    ppermute x8, starting transfers between devices, fast_body(): blocks[n, c] = lax.ppermute(part, AXES, homeward(n >> 1, n & 1, c))  13.9 us
    ppermute x15, waiting for transfers between devices, swap(): return lax.ppermute(block, AXES, [(i, i ^ bits) for i in range(32)])  12.1 us
    ppermute x2, starting transfers between devices, far_swap(): lax.ppermute(block, AXES, [(i, i ^ BITS_FAR) for i in range(32) if outer(...  5.62 us
    ppermute x8, waiting for transfers between devices, fast_body(): blocks[n, c] = lax.ppermute(part, AXES, homeward(n >> 1, n & 1, c))  3.84 us
    ppermute x2, waiting for transfers between devices, far_swap(): lax.ppermute(block, AXES, [(i, i ^ BITS_FAR) for i in range(32) if outer(...  3.61 us
    unnamed x18, local copies, waits for them, and re-layouts  2.13 us
  transfers between devices with their start and end apart: 25, of which 8 were waited for; matrix products, arithmetic and copies ran while one was open for 0% of the time, Pallas kernels for 23%

profile of v4, /device:TPU:0, one launch (start us, length us, event | category | flops | bytes accessed | tf_op | source)
XLA Modules:
  0.0 85.6 jit_solution(7638322045316778575)
XLA Ops:
  1.1 5.1 %collective-permute-start.3 = (bf16[576,512]{1,0:T(8,128)(2,1)S(1)}, bf16[576,512]{1,0:T(8,128)(2,1)S(1)}, u32[]{:S(2)}, u32[]{:S(2)}) collective-permute-start(bf16[576,512]{1,0:T(8,128)(2,1)S(1)} %slice.13), channel_id=1, source_target_pairs={{0,24},{1,25},{2,26},{3,27},{4,28},{5,29},{6,30},{7,31},{8,16},{9,... | collective-permute-start | bytes 1769480 | tf_op jit(solution)/shard_map/ppermute | solution.py:22
  8.4 1.9 %shard_map.92 = (bf16[208,256]{1,0:T(8,128)(2,1)S(1)}, bf16[208,256]{1,0:T(8,128)(2,1)S(1)}, bf16[208,256]{1,0:T(8,128)(2,1)S(1)}, bf16[208,256]{1,0:T(8,128)(2,...) custom-call(s32[7]{0:T(128)S(1)} %stack.39.refs_0_.g_ref, ...), custom_call_target="tpu_custom_call" | custom-call | flops 2000000000 | bytes 6000000 | tf_op jit(solution)/shard_map/pallas_call | solution.py:416
  10.4 1.6 %collective-permute-start = (bf16[208,256]{1,0:T(8,128)(2,1)S(1)}, bf16[208,256]{1,0:T(8,128)(2,1)S(1)}, u32[]{:S(2)}, u32[]{:S(2)}) collective-permute-start(bf16[208,256]{1,0:T(8,128)(2,1)S(1)} %get-tuple-element.70), channel_id=1, source_target_pairs={{0,4},{1,5},{2,6},{3,7},{4,0},{5,1},{6,2},{7,3},{8,12},{9,13},{10,... | collective-permute-start | bytes 319496 | tf_op jit(solution)/shard_map/ppermute | solution.py:22
  12.0 2.0 %collective-permute-start.2 = (bf16[208,256]{1,0:T(8,128)(2,1)S(1)}, bf16[208,256]{1,0:T(8,128)(2,1)S(1)}, u32[]{:S(2)}, u32[]{:S(2)}) collective-permute-start(bf16[208,256]{1,0:T(8,128)(2,1)S(1)} %get-tuple-element.72), channel_id=1, source_target_pairs={{0,12},{1,13},{2,14},{3,15},{4,8},{5,9},{6,10},{7,11},{8,4},{9,5},... | collective-permute-start | bytes 319496 | tf_op jit(solution)/shard_map/ppermute | solution.py:22
  14.0 2.6 %shard_map.91 = (f32[288,256]{1,0:T(8,128)S(1)}, f32[320,256]{1,0:T(8,128)S(1)}, f32[16,160,256]{2,1,0:T(8,128)S(1)}, f32[16,160,256]{2,1,0:T(8,128)S(1)}, f32[4...) custom-call(s32[7]{0:T(128)S(1)} %stack.39.refs_0_.g_ref, f32[128,1024]{1,0:T(8,128)S(1)} %copy-done.2, ...), custom_call_target="tpu_custom_call" | custom-call | flops 345000000 | bytes 1107000 | tf_op jit(solution)/shard_map/pallas_call | solution.py:385
  16.6 1.6 %collective-permute-start.6 = (bf16[160,256]{1,0:T(8,128)(2,1)S(1)}, bf16[160,256]{1,0:T(8,128)(2,1)S(1)}, u32[]{:S(2)}, u32[]{:S(2)}) collective-permute-start(bf16[160,256]{1,0:T(8,128)(2,1)S(1)} %get-tuple-element.83), channel_id=1, source_target_pairs={{0,4},{1,5},{2,6},{3,7},{4,0},{5,1},{6,2},{7,3},{8,12},{9,13},{10,... | collective-permute-start | bytes 245768 | tf_op jit(solution)/shard_map/ppermute | solution.py:22
  18.1 4.2 %collective-permute-done.1.refs_9_ = bf16[208,256]{1,0:T(8,128)(2,1)S(1)} collective-permute-done((bf16[208,256]{1,0:T(8,128)(2,1)S(1)}, bf16[208,256]{1,0:T(8,128)(2,1)S(1)}, u32[]{:S(2)}, u32[]{:S(2)}) %collective-permute-start.1) | collective-permute-done | bytes 106528 | tf_op jit(solution)/shard_map/ppermute | solution.py:22
  22.3 3.4 %collective-permute-start.8 = (bf16[160,256]{1,0:T(8,128)(2,1)S(1)}, bf16[160,256]{1,0:T(8,128)(2,1)S(1)}, u32[]{:S(2)}, u32[]{:S(2)}) collective-permute-start(bf16[160,256]{1,0:T(8,128)(2,1)S(1)} %get-tuple-element.85), channel_id=1, source_target_pairs={{0,12},{1,13},{2,14},{3,15},{4,8},{5,9},{6,10},{7,11},{8,4},{9,5},... | collective-permute-start | bytes 245768 | tf_op jit(solution)/shard_map/ppermute | solution.py:22
  25.7 4.3 %shard_map.93 = (f32[4,160,256]{2,1,0:T(8,128)S(1)}, f32[4,2,16,256]{3,2,1,0:T(8,128)S(1)}, f32[40,256]{1,0:T(8,128)S(1)}, bf16[160,256]{1,0:T(8,128)(2,1)S(1)},...) custom-call(s32[7]{0:T(128)S(1)} %stack.39.refs_0_.g_ref, f32[3,7,256]{2,1,0:T(8,128)S(1)} %get-tuple-element.59.refs_1_, ...), custom_call_target="tpu_custom_call" | custom-call | flops 690000000 | bytes 2214000 | tf_op jit(solution)/shard_map/pallas_call | solution.py:385
  30.0 2.9 %collective-permute-start.5 = (bf16[160,256]{1,0:T(8,128)(2,1)S(1)}, bf16[160,256]{1,0:T(8,128)(2,1)S(1)}, u32[]{:S(2)}, u32[]{:S(2)}) collective-permute-start(bf16[160,256]{1,0:T(8,128)(2,1)S(1)} %get-tuple-element.76), channel_id=1, source_target_pairs={{0,16},{1,17},{2,18},{3,19},{4,20},{5,21},{6,22},{7,23},{8,24},{9,... | collective-permute-start | bytes 245768 | tf_op jit(solution)/shard_map/ppermute | solution.py:22
  33.0 2.2 %shard_map.94 = (f32[3,160,256]{2,1,0:T(8,128)S(1)}, f32[640,256]{1,0:T(8,128)S(1)}) custom-call(s32[7]{0:T(128)S(1)} %stack.39.refs_0_.g_ref, f32[3,7,256]{2,1,0:T(8,128)S(1)} %get-tuple-element.59.refs_1_, f32[4,160,256]{2,1,0:T(8,128)S(1)} %get-tuple-element.81.refs_2_, f32[320,256]{1,0:T(8,128)S(1)} %get-tuple-element.79.refs_3_.refs_7_, ...), custom_call_target="tpu_custom_call" | custom-call | flops 3564999936 | bytes 11439000 | tf_op jit(solution)/shard_map/pallas_call | solution.py:385
  35.2 4.9 %collective-permute-start.10 = (bf16[448,512]{1,0:T(8,128)(2,1)S(1)}, bf16[448,512]{1,0:T(8,128)(2,1)S(1)}, u32[]{:S(2)}, u32[]{:S(2)}) collective-permute-start(bf16[448,512]{1,0:T(8,128)(2,1)S(1)} %slice.14), channel_id=1, source_target_pairs={{0,24},{1,25},{2,26},{3,27},{4,28},{5,29},{6,30},{7,31},{24,0},{25... | collective-permute-start | bytes 1376264 | tf_op jit(solution)/shard_map/ppermute | solution.py:39
  40.2 4.9 %shard_map.95.h0 = bf16[640,256]{1,0:T(8,128)(2,1)S(1)} custom-call(s32[7]{0:T(128)S(1)} %stack.39.refs_0_.g_ref, f32[3,7,256]{2,1,0:T(8,128)S(1)} %get-tuple-element.59.refs_1_, f32[40,256]{1,0:T(8,128)S(1)} %collective-permute-done.4.refs_2_, bf16[160,256]{1,0:T(8,128)(2,1)S(1)} %collective-permute-done.5.refs_3_, ...), custom_call_target="tpu_custom_call" | custom-call | flops 5980000256 | bytes 19188000 | tf_op jit(solution)/shard_map/pallas_call | solution.py:385
  46.4 1.3 %collective-permute-start.11 = (bf16[640,256]{1,0:T(8,128)(2,1)S(1)}, bf16[640,256]{1,0:T(8,128)(2,1)S(1)}, u32[]{:S(2)}, u32[]{:S(2)}) collective-permute-start(bf16[640,256]{1,0:T(8,128)(2,1)S(1)} %shard_map.95.h0), channel_id=1, source_target_pairs={{0,8},{1,9},{2,10},{3,11},{4,12},{5,13},{6,14},{7,15},{8,0},{9,1},... | collective-permute-start | bytes 983048 | tf_op jit(solution)/shard_map/ppermute | solution.py:22
  47.8 3.6 %collective-permute-done.10.out_late = bf16[448,512]{1,0:T(8,128)(2,1)S(1)} collective-permute-done((bf16[448,512]{1,0:T(8,128)(2,1)S(1)}, bf16[448,512]{1,0:T(8,128)(2,1)S(1)}, u32[]{:S(2)}, u32[]{:S(2)}) %collective-permute-start.10) | collective-permute-done | bytes 458784 | tf_op jit(solution)/shard_map/ppermute | solution.py:39
  51.4 3.2 %collective-permute-done.9.h1 = bf16[640,256]{1,0:T(8,128)(2,1)S(1)} collective-permute-done((bf16[640,256]{1,0:T(8,128)(2,1)S(1)}, bf16[640,256]{1,0:T(8,128)(2,1)S(1)}, u32[]{:S(2)}, u32[]{:S(2)}) %collective-permute-start.9) | collective-permute-done | bytes 327712 | tf_op jit(solution)/shard_map/ppermute | solution.py:22
  55.4 2.8 %collective-permute-done.11.h2 = bf16[640,256]{1,0:T(8,128)(2,1)S(1)} collective-permute-done((bf16[640,256]{1,0:T(8,128)(2,1)S(1)}, bf16[640,256]{1,0:T(8,128)(2,1)S(1)}, u32[]{:S(2)}, u32[]{:S(2)}) %collective-permute-start.11) | collective-permute-done | bytes 327712 | tf_op jit(solution)/shard_map/ppermute | solution.py:22
  59.0 2.0 %shard_map.96 = (f32[2,2,640,256]{3,2,1,0:T(8,128)S(1)}, bf16[1024,512]{1,0:T(8,128)(2,1)S(1)}) custom-call(s32[7]{0:T(128)S(1)} %stack.39.refs_0_.g_ref, bf16[640,256]{1,0:T(8,128)(2,1)S(1)} %shard_map.95.h0, bf16[640,256]{1,0:T(8,128)(2,1)S(1)} %collective-permute-done.9.h1, bf16[640,256]{1,0:T(8,128)(2,1)S(1)} %collective-permute-done.11.h2, ...), custom_call_target="tpu_custom_call" | custom-call | flops 2300000000 | bytes 7380000 | tf_op jit(solution)/shard_map/pallas_call | solution.py:385
  61.0 1.7 %collective-permute-done.13.refs_2_ = bf16[160,256]{1,0:T(8,128)(2,1)S(1)} collective-permute-done((bf16[160,256]{1,0:T(8,128)(2,1)S(1)}, bf16[160,256]{1,0:T(8,128)(2,1)S(1)}, u32[]{:S(2)}, u32[]{:S(2)}) %collective-permute-start.13) | collective-permute-done | bytes 81952 | tf_op jit(solution)/shard_map/ppermute | solution.py:22
  67.2 2.4 %collective-permute-start.20 = (bf16[160,256]{1,0:T(8,128)(2,1)S(1)}, bf16[160,256]{1,0:T(8,128)(2,1)S(1)}, u32[]{:S(2)}, u32[]{:S(2)}) collective-permute-start(bf16[160,256]{1,0:T(8,128)(2,1)S(1)} %get-tuple-element.108), channel_id=1, source_target_pairs={{0,7},{1,15},{2,4},{3,12},{4,3},{5,11},{6,0},{7,8},{8,6},{9,14},{1... | collective-permute-start | bytes 245768 | tf_op jit(solution)/shard_map/ppermute | solution.py:496
  70.8 1.8 %collective-permute-start.24 = (bf16[160,256]{1,0:T(8,128)(2,1)S(1)}, bf16[160,256]{1,0:T(8,128)(2,1)S(1)}, u32[]{:S(2)}, u32[]{:S(2)}) collective-permute-start(bf16[160,256]{1,0:T(8,128)(2,1)S(1)} %get-tuple-element.112), channel_id=1, source_target_pairs={{0,15},{1,7},{2,12},{3,4},{4,11},{5,3},{6,8},{7,0},{8,14},{9,6},{1... | collective-permute-start | bytes 245768 | tf_op jit(solution)/shard_map/ppermute | solution.py:496
  74.5 5.0 %collective-permute-start.21 = (bf16[160,256]{1,0:T(8,128)(2,1)S(1)}, bf16[160,256]{1,0:T(8,128)(2,1)S(1)}, u32[]{:S(2)}, u32[]{:S(2)}) collective-permute-start(bf16[160,256]{1,0:T(8,128)(2,1)S(1)} %get-tuple-element.109), channel_id=1, source_target_pairs={{0,8},{1,0},{2,11},{3,3},{4,12},{5,4},{6,15},{7,7},{8,9},{9,1},{10... | collective-permute-start | bytes 245768 | tf_op jit(solution)/shard_map/ppermute | solution.py:496
  81.5 2.8 %collective-permute-done.23.refs_6_ = bf16[160,256]{1,0:T(8,128)(2,1)S(1)} collective-permute-done((bf16[160,256]{1,0:T(8,128)(2,1)S(1)}, bf16[160,256]{1,0:T(8,128)(2,1)S(1)}, u32[]{:S(2)}, u32[]{:S(2)}) %collective-permute-start.23) | collective-permute-done | bytes 81952 | tf_op jit(solution)/shard_map/ppermute | solution.py:496
  84.3 1.3 %shard_map.101 = bf16[160,1024]{1,0:T(8,128)(2,1)} custom-call(s32[7]{0:T(128)S(1)} %stack.39.refs_0_.g_ref, bf16[160,256]{1,0:T(8,128)(2,1)S(1)} %collective-permute-done.16.refs_0_, bf16[160,256]{1,0:T(8,128)(2,1)S(1)} %collective-permute-done.18.refs_1_, bf16[160,256]{1,0:T(8,128)(2,1)S(1)} %collective-permute-done.19.refs_2_, ...), custom_call_target="tpu_custom_call" | custom-call | flops 1495000064 | bytes 4797000 | tf_op jit(solution)/shard_map/pallas_call | solution.py:385
  (60 shorter events, 16.0 us)
Async XLA Ops:
  1.1 28.9 %collective-permute-start.3 = (bf16[576,512]{1,0:T(8,128)(2,1)S(1)}, bf16[576,512]{1,0:T(8,128)(2,1)S(1)}, u32[]{:S(2)}, u32[]{:S(2)}) collective-permute-start(bf16[576,512]{1,0:T(8,128)(2,1)S(1)} %slice.13), channel_id=1, source_target_pairs={{0,24},{1,25},{2,26},{3,27},{4,28},{5,29},{6,30},{7,31},{8,16},{9,... | collective-permute-start | bytes 1769480 | tf_op jit(solution)/shard_map/ppermute | solution.py:22
  10.4 7.7 %collective-permute-start = (bf16[208,256]{1,0:T(8,128)(2,1)S(1)}, bf16[208,256]{1,0:T(8,128)(2,1)S(1)}, u32[]{:S(2)}, u32[]{:S(2)}) collective-permute-start(bf16[208,256]{1,0:T(8,128)(2,1)S(1)} %get-tuple-element.70), channel_id=1, source_target_pairs={{0,4},{1,5},{2,6},{3,7},{4,0},{5,1},{6,2},{7,3},{8,12},{9,13},{10,... | collective-permute-start | bytes 319496 | tf_op jit(solution)/shard_map/ppermute | solution.py:22
  12.0 10.3 %collective-permute-start.1 = (bf16[208,256]{1,0:T(8,128)(2,1)S(1)}, bf16[208,256]{1,0:T(8,128)(2,1)S(1)}, u32[]{:S(2)}, u32[]{:S(2)}) collective-permute-start(bf16[208,256]{1,0:T(8,128)(2,1)S(1)} %get-tuple-element.71), channel_id=1, source_target_pairs={{0,8},{1,9},{2,10},{3,11},{4,12},{5,13},{6,14},{7,15},{8,0},{9,1},... | collective-permute-start | bytes 319496 | tf_op jit(solution)/shard_map/ppermute | solution.py:22
  12.0 13.8 %collective-permute-start.2 = (bf16[208,256]{1,0:T(8,128)(2,1)S(1)}, bf16[208,256]{1,0:T(8,128)(2,1)S(1)}, u32[]{:S(2)}, u32[]{:S(2)}) collective-permute-start(bf16[208,256]{1,0:T(8,128)(2,1)S(1)} %get-tuple-element.72), channel_id=1, source_target_pairs={{0,12},{1,13},{2,14},{3,15},{4,8},{5,9},{6,10},{7,11},{8,4},{9,5},... | collective-permute-start | bytes 319496 | tf_op jit(solution)/shard_map/ppermute | solution.py:22
  16.6 16.5 %collective-permute-start.6 = (bf16[160,256]{1,0:T(8,128)(2,1)S(1)}, bf16[160,256]{1,0:T(8,128)(2,1)S(1)}, u32[]{:S(2)}, u32[]{:S(2)}) collective-permute-start(bf16[160,256]{1,0:T(8,128)(2,1)S(1)} %get-tuple-element.83), channel_id=1, source_target_pairs={{0,4},{1,5},{2,6},{3,7},{4,0},{5,1},{6,2},{7,3},{8,12},{9,13},{10,... | collective-permute-start | bytes 245768 | tf_op jit(solution)/shard_map/ppermute | solution.py:22
  18.1 14.9 %collective-permute-start.7 = (bf16[160,256]{1,0:T(8,128)(2,1)S(1)}, bf16[160,256]{1,0:T(8,128)(2,1)S(1)}, u32[]{:S(2)}, u32[]{:S(2)}) collective-permute-start(bf16[160,256]{1,0:T(8,128)(2,1)S(1)} %get-tuple-element.84), channel_id=1, source_target_pairs={{0,8},{1,9},{2,10},{3,11},{4,12},{5,13},{6,14},{7,15},{8,0},{9,1},... | collective-permute-start | bytes 245768 | tf_op jit(solution)/shard_map/ppermute | solution.py:22
  22.3 10.8 %collective-permute-start.8 = (bf16[160,256]{1,0:T(8,128)(2,1)S(1)}, bf16[160,256]{1,0:T(8,128)(2,1)S(1)}, u32[]{:S(2)}, u32[]{:S(2)}) collective-permute-start(bf16[160,256]{1,0:T(8,128)(2,1)S(1)} %get-tuple-element.85), channel_id=1, source_target_pairs={{0,12},{1,13},{2,14},{3,15},{4,8},{5,9},{6,10},{7,11},{8,4},{9,5},... | collective-permute-start | bytes 245768 | tf_op jit(solution)/shard_map/ppermute | solution.py:22
  30.0 10.2 %collective-permute-start.5 = (bf16[160,256]{1,0:T(8,128)(2,1)S(1)}, bf16[160,256]{1,0:T(8,128)(2,1)S(1)}, u32[]{:S(2)}, u32[]{:S(2)}) collective-permute-start(bf16[160,256]{1,0:T(8,128)(2,1)S(1)} %get-tuple-element.76), channel_id=1, source_target_pairs={{0,16},{1,17},{2,18},{3,19},{4,20},{5,21},{6,22},{7,23},{8,24},{9,... | collective-permute-start | bytes 245768 | tf_op jit(solution)/shard_map/ppermute | solution.py:22
  32.9 7.3 %collective-permute-start.4 = (f32[40,256]{1,0:T(8,128)S(1)}, f32[40,256]{1,0:T(8,128)S(1)}, u32[]{:S(2)}, u32[]{:S(2)}) collective-permute-start(f32[40,256]{1,0:T(8,128)S(1)} %get-tuple-element.75), channel_id=1, source_target_pairs={{0,16},{1,17},{2,18},{3,19},{4,20},{5,21},{6,22},{7,23},{8,24},{9,... | collective-permute-start | bytes 122888 | tf_op jit(solution)/shard_map/ppermute | solution.py:22
  35.2 16.1 %collective-permute-start.10 = (bf16[448,512]{1,0:T(8,128)(2,1)S(1)}, bf16[448,512]{1,0:T(8,128)(2,1)S(1)}, u32[]{:S(2)}, u32[]{:S(2)}) collective-permute-start(bf16[448,512]{1,0:T(8,128)(2,1)S(1)} %slice.14), channel_id=1, source_target_pairs={{0,24},{1,25},{2,26},{3,27},{4,28},{5,29},{6,30},{7,31},{24,0},{25... | collective-permute-start | bytes 1376264 | tf_op jit(solution)/shard_map/ppermute | solution.py:39
  45.2 13.8 %collective-permute-start.12 = (bf16[448,512]{1,0:T(8,128)(2,1)S(1)}, bf16[448,512]{1,0:T(8,128)(2,1)S(1)}, u32[]{:S(2)}, u32[]{:S(2)}) collective-permute-start(bf16[448,512]{1,0:T(8,128)(2,1)S(1)} %slice.14), channel_id=1, source_target_pairs={{8,16},{9,17},{10,18},{11,19},{12,20},{13,21},{14,22},{15,23},{16,... | collective-permute-start | bytes 1376264 | tf_op jit(solution)/shard_map/ppermute | solution.py:39
  45.9 8.8 %collective-permute-start.9 = (bf16[640,256]{1,0:T(8,128)(2,1)S(1)}, bf16[640,256]{1,0:T(8,128)(2,1)S(1)}, u32[]{:S(2)}, u32[]{:S(2)}) collective-permute-start(bf16[640,256]{1,0:T(8,128)(2,1)S(1)} %shard_map.95.h0), channel_id=1, source_target_pairs={{0,4},{1,5},{2,6},{3,7},{4,0},{5,1},{6,2},{7,3},{8,12},{9,13},{10,... | collective-permute-start | bytes 983048 | tf_op jit(solution)/shard_map/ppermute | solution.py:22
  46.4 11.8 %collective-permute-start.11 = (bf16[640,256]{1,0:T(8,128)(2,1)S(1)}, bf16[640,256]{1,0:T(8,128)(2,1)S(1)}, u32[]{:S(2)}, u32[]{:S(2)}) collective-permute-start(bf16[640,256]{1,0:T(8,128)(2,1)S(1)} %shard_map.95.h0), channel_id=1, source_target_pairs={{0,8},{1,9},{2,10},{3,11},{4,12},{5,13},{6,14},{7,15},{8,0},{9,1},... | collective-permute-start | bytes 983048 | tf_op jit(solution)/shard_map/ppermute | solution.py:22
  54.6 8.0 %collective-permute-start.14 = (bf16[480,256]{1,0:T(8,128)(2,1)S(1)}, bf16[480,256]{1,0:T(8,128)(2,1)S(1)}, u32[]{:S(2)}, u32[]{:S(2)}) collective-permute-start(bf16[480,256]{1,0:T(8,128)(2,1)S(1)} %slice.16), channel_id=1, source_target_pairs={{0,8},{1,9},{2,10},{3,11},{4,12},{5,13},{6,14},{7,15},{8,0},{9,1},... | collective-permute-start | bytes 737288 | tf_op jit(solution)/shard_map/ppermute | solution.py:22
  58.2 4.4 %collective-permute-start.13 = (bf16[160,256]{1,0:T(8,128)(2,1)S(1)}, bf16[160,256]{1,0:T(8,128)(2,1)S(1)}, u32[]{:S(2)}, u32[]{:S(2)}) collective-permute-start(bf16[160,256]{1,0:T(8,128)(2,1)S(1)} %slice.17), channel_id=1, source_target_pairs={{0,4},{1,5},{2,6},{3,7},{4,0},{5,1},{6,2},{7,3},{8,12},{9,13},{10,... | collective-permute-start | bytes 245768 | tf_op jit(solution)/shard_map/ppermute | solution.py:22
  64.5 8.1 %collective-permute-start.15 = (bf16[640,256]{1,0:T(8,128)(2,1)S(1)}, bf16[640,256]{1,0:T(8,128)(2,1)S(1)}, u32[]{:S(2)}, u32[]{:S(2)}) collective-permute-start(bf16[640,256]{1,0:T(8,128)(2,1)S(1)} %get-tuple-element.102), channel_id=1, source_target_pairs={{0,1},{1,0},{2,3},{3,2},{4,5},{5,4},{6,7},{7,6},{8,9},{9,8},{10,11... | collective-permute-start | bytes 983048 | tf_op jit(solution)/shard_map/ppermute | solution.py:22
  65.9 8.0 %collective-permute-start.18 = (bf16[160,256]{1,0:T(8,128)(2,1)S(1)}, bf16[160,256]{1,0:T(8,128)(2,1)S(1)}, u32[]{:S(2)}, u32[]{:S(2)}) collective-permute-start(bf16[160,256]{1,0:T(8,128)(2,1)S(1)} %get-tuple-element.106), channel_id=1, source_target_pairs={{0,3},{1,11},{2,0},{3,8},{4,7},{5,15},{6,4},{7,12},{8,2},{9,10},{1... | collective-permute-start | bytes 245768 | tf_op jit(solution)/shard_map/ppermute | solution.py:496
  67.2 7.3 %collective-permute-start.20 = (bf16[160,256]{1,0:T(8,128)(2,1)S(1)}, bf16[160,256]{1,0:T(8,128)(2,1)S(1)}, u32[]{:S(2)}, u32[]{:S(2)}) collective-permute-start(bf16[160,256]{1,0:T(8,128)(2,1)S(1)} %get-tuple-element.108), channel_id=1, source_target_pairs={{0,7},{1,15},{2,4},{3,12},{4,3},{5,11},{6,0},{7,8},{8,6},{9,14},{1... | collective-permute-start | bytes 245768 | tf_op jit(solution)/shard_map/ppermute | solution.py:496
  69.6 9.9 %collective-permute-start.22 = (bf16[160,256]{1,0:T(8,128)(2,1)S(1)}, bf16[160,256]{1,0:T(8,128)(2,1)S(1)}, u32[]{:S(2)}, u32[]{:S(2)}) collective-permute-start(bf16[160,256]{1,0:T(8,128)(2,1)S(1)} %get-tuple-element.110), channel_id=1, source_target_pairs={{0,11},{1,3},{2,8},{3,0},{4,15},{5,7},{6,12},{7,4},{8,10},{9,2},{1... | collective-permute-start | bytes 245768 | tf_op jit(solution)/shard_map/ppermute | solution.py:496
  70.8 9.6 %collective-permute-start.24 = (bf16[160,256]{1,0:T(8,128)(2,1)S(1)}, bf16[160,256]{1,0:T(8,128)(2,1)S(1)}, u32[]{:S(2)}, u32[]{:S(2)}) collective-permute-start(bf16[160,256]{1,0:T(8,128)(2,1)S(1)} %get-tuple-element.112), channel_id=1, source_target_pairs={{0,15},{1,7},{2,12},{3,4},{4,11},{5,3},{6,8},{7,0},{8,14},{9,6},{1... | collective-permute-start | bytes 245768 | tf_op jit(solution)/shard_map/ppermute | solution.py:496
  73.2 7.2 %collective-permute-start.16 = (bf16[160,256]{1,0:T(8,128)(2,1)S(1)}, bf16[160,256]{1,0:T(8,128)(2,1)S(1)}, u32[]{:S(2)}, u32[]{:S(2)}) collective-permute-start(bf16[160,256]{1,0:T(8,128)(2,1)S(1)} %get-tuple-element.103), channel_id=1, source_target_pairs={{0,0},{1,8},{2,3},{3,11},{4,4},{5,12},{6,7},{7,15},{8,1},{9,9},{10... | collective-permute-start | bytes 245768 | tf_op jit(solution)/shard_map/ppermute | solution.py:496
  73.9 6.6 %collective-permute-start.19 = (bf16[160,256]{1,0:T(8,128)(2,1)S(1)}, bf16[160,256]{1,0:T(8,128)(2,1)S(1)}, u32[]{:S(2)}, u32[]{:S(2)}) collective-permute-start(bf16[160,256]{1,0:T(8,128)(2,1)S(1)} %get-tuple-element.107), channel_id=1, source_target_pairs={{0,4},{1,12},{2,7},{3,15},{4,0},{5,8},{6,3},{7,11},{8,5},{9,13},{1... | collective-permute-start | bytes 245768 | tf_op jit(solution)/shard_map/ppermute | solution.py:496
  74.5 7.0 %collective-permute-start.21 = (bf16[160,256]{1,0:T(8,128)(2,1)S(1)}, bf16[160,256]{1,0:T(8,128)(2,1)S(1)}, u32[]{:S(2)}, u32[]{:S(2)}) collective-permute-start(bf16[160,256]{1,0:T(8,128)(2,1)S(1)} %get-tuple-element.109), channel_id=1, source_target_pairs={{0,8},{1,0},{2,11},{3,3},{4,12},{5,4},{6,15},{7,7},{8,9},{9,1},{10... | collective-permute-start | bytes 245768 | tf_op jit(solution)/shard_map/ppermute | solution.py:496
  79.5 4.8 %collective-permute-start.23 = (bf16[160,256]{1,0:T(8,128)(2,1)S(1)}, bf16[160,256]{1,0:T(8,128)(2,1)S(1)}, u32[]{:S(2)}, u32[]{:S(2)}) collective-permute-start(bf16[160,256]{1,0:T(8,128)(2,1)S(1)} %get-tuple-element.111), channel_id=1, source_target_pairs={{0,12},{1,4},{2,15},{3,7},{4,8},{5,0},{6,11},{7,3},{8,13},{9,5},{1... | collective-permute-start | bytes 245768 | tf_op jit(solution)/shard_map/ppermute | solution.py:496
  (10 other events, 52.4 us)

commit v5 on v4

--- a/solution.py
+++ b/solution.py
@@ -456,6 +456,8 @@
     )
     late, later = lax.optimization_barrier((out_weight[cut:], later))
     out_late = far_swap(late, True)
+    late, later = lax.optimization_barrier((out_weight[cut:], later))
+    in_late = far_swap(late, False)
     (hidden,) = call(
         5.2,
         lambda *refs: hidden_kernel(rows, modes, *refs),
@@ -464,8 +466,6 @@
         [((GROUP, modes, 2, 8, quarter), F32), ((rows + 128, quarter), BF16), ((1, rows, quarter), F32),
          ((1, modes, quarter), F32), ((1, modes, quarter), F32), ((1, rows, quarter), F32)],
     )
-    hidden, late = lax.optimization_barrier((hidden, out_weight[cut:]))
-    in_late = far_swap(late, False)
     hid = [hidden] + [swap(hidden, SLOT_BITS[m]) for m in (1, 2)]
     hid[1], out_late = lax.optimization_barrier((hid[1], out_late))
     passed = swap(hid[1][rows:], SLOT_BITS[2])

time: 85.9 us -> 85.9 us (level)
    ppermute x2, waiting for transfers between devices: 3.61 us -> 4.63 us  [far_swap(): lax.ppermute(block, AXES, [(i, i ^ BITS_FAR) for i in range(32) if outer(...]
    ppermute x15, waiting for transfers between devices: 12.1 us -> 11.1 us  [swap(): return lax.ppermute(block, AXES, [(i, i ^ bits) for i in range(32)])]
where the time goes in v5:
time: 85.9 us; the launch traced here: 85.6 us
  starting transfers between devices  40.1 us (47%)
  Pallas kernels  22.3 us (26%)
  waiting for transfers between devices  19.6 us (23%)
  local copies, waits for them, and re-layouts  3.37 us (4%)
    ppermute x15, starting transfers between devices, swap(): return lax.ppermute(block, AXES, [(i, i ^ bits) for i in range(32)])  20.7 us
    pallas_call x10, Pallas kernels, call(): pl.pallas_call(kernel, out_shape=tuple((jax.ShapeDtypeStruct(s, d) for s,...  20.3 us
    ppermute x8, starting transfers between devices, fast_body(): blocks[n, c] = lax.ppermute(part, AXES, homeward(n >> 1, n & 1, c))  13.8 us
    ppermute x15, waiting for transfers between devices, swap(): return lax.ppermute(block, AXES, [(i, i ^ bits) for i in range(32)])  11.1 us
    ppermute x2, starting transfers between devices, far_swap(): lax.ppermute(block, AXES, [(i, i ^ BITS_FAR) for i in range(32) if outer(...  5.62 us
    ppermute x2, waiting for transfers between devices, far_swap(): lax.ppermute(block, AXES, [(i, i ^ BITS_FAR) for i in range(32) if outer(...  4.63 us
    ppermute x8, waiting for transfers between devices, fast_body(): blocks[n, c] = lax.ppermute(part, AXES, homeward(n >> 1, n & 1, c))  3.84 us
    unnamed x18, local copies, waits for them, and re-layouts  2.13 us
  transfers between devices with their start and end apart: 25, of which 8 were waited for; matrix products, arithmetic and copies ran while one was open for 0% of the time, Pallas kernels for 23%

profile of v5, /device:TPU:0, one launch (start us, length us, event | category | flops | bytes accessed | tf_op | source)
XLA Modules:
  0.0 85.6 jit_solution(4001323332226156057)
XLA Ops:
  1.1 5.1 %collective-permute-start.3 = (bf16[576,512]{1,0:T(8,128)(2,1)S(1)}, bf16[576,512]{1,0:T(8,128)(2,1)S(1)}, u32[]{:S(2)}, u32[]{:S(2)}) collective-permute-start(bf16[576,512]{1,0:T(8,128)(2,1)S(1)} %slice.13), channel_id=1, source_target_pairs={{0,24},{1,25},{2,26},{3,27},{4,28},{5,29},{6,30},{7,31},{8,16},{9,... | collective-permute-start | bytes 1769480 | tf_op jit(solution)/shard_map/ppermute | solution.py:22
  8.4 1.9 %shard_map.92 = (bf16[208,256]{1,0:T(8,128)(2,1)S(1)}, bf16[208,256]{1,0:T(8,128)(2,1)S(1)}, bf16[208,256]{1,0:T(8,128)(2,1)S(1)}, bf16[208,256]{1,0:T(8,128)(2,...) custom-call(s32[7]{0:T(128)S(1)} %stack.39.refs_0_.g_ref, ...), custom_call_target="tpu_custom_call" | custom-call | flops 2000000000 | bytes 6000000 | tf_op jit(solution)/shard_map/pallas_call | solution.py:416
  10.4 1.6 %collective-permute-start = (bf16[208,256]{1,0:T(8,128)(2,1)S(1)}, bf16[208,256]{1,0:T(8,128)(2,1)S(1)}, u32[]{:S(2)}, u32[]{:S(2)}) collective-permute-start(bf16[208,256]{1,0:T(8,128)(2,1)S(1)} %get-tuple-element.70), channel_id=1, source_target_pairs={{0,4},{1,5},{2,6},{3,7},{4,0},{5,1},{6,2},{7,3},{8,12},{9,13},{10,... | collective-permute-start | bytes 319496 | tf_op jit(solution)/shard_map/ppermute | solution.py:22
  12.0 2.0 %collective-permute-start.2 = (bf16[208,256]{1,0:T(8,128)(2,1)S(1)}, bf16[208,256]{1,0:T(8,128)(2,1)S(1)}, u32[]{:S(2)}, u32[]{:S(2)}) collective-permute-start(bf16[208,256]{1,0:T(8,128)(2,1)S(1)} %get-tuple-element.72), channel_id=1, source_target_pairs={{0,12},{1,13},{2,14},{3,15},{4,8},{5,9},{6,10},{7,11},{8,4},{9,5},... | collective-permute-start | bytes 319496 | tf_op jit(solution)/shard_map/ppermute | solution.py:22
  14.0 2.6 %shard_map.91 = (f32[288,256]{1,0:T(8,128)S(1)}, f32[320,256]{1,0:T(8,128)S(1)}, f32[16,160,256]{2,1,0:T(8,128)S(1)}, f32[16,160,256]{2,1,0:T(8,128)S(1)}, f32[4...) custom-call(s32[7]{0:T(128)S(1)} %stack.39.refs_0_.g_ref, f32[128,1024]{1,0:T(8,128)S(1)} %copy-done.2, ...), custom_call_target="tpu_custom_call" | custom-call | flops 345000000 | bytes 1107000 | tf_op jit(solution)/shard_map/pallas_call | solution.py:385
  16.6 1.6 %collective-permute-start.6 = (bf16[160,256]{1,0:T(8,128)(2,1)S(1)}, bf16[160,256]{1,0:T(8,128)(2,1)S(1)}, u32[]{:S(2)}, u32[]{:S(2)}) collective-permute-start(bf16[160,256]{1,0:T(8,128)(2,1)S(1)} %get-tuple-element.83), channel_id=1, source_target_pairs={{0,4},{1,5},{2,6},{3,7},{4,0},{5,1},{6,2},{7,3},{8,12},{9,13},{10,... | collective-permute-start | bytes 245768 | tf_op jit(solution)/shard_map/ppermute | solution.py:22
  18.1 4.2 %collective-permute-done.1.refs_9_ = bf16[208,256]{1,0:T(8,128)(2,1)S(1)} collective-permute-done((bf16[208,256]{1,0:T(8,128)(2,1)S(1)}, bf16[208,256]{1,0:T(8,128)(2,1)S(1)}, u32[]{:S(2)}, u32[]{:S(2)}) %collective-permute-start.1) | collective-permute-done | bytes 106528 | tf_op jit(solution)/shard_map/ppermute | solution.py:22
  22.3 3.4 %collective-permute-start.8 = (bf16[160,256]{1,0:T(8,128)(2,1)S(1)}, bf16[160,256]{1,0:T(8,128)(2,1)S(1)}, u32[]{:S(2)}, u32[]{:S(2)}) collective-permute-start(bf16[160,256]{1,0:T(8,128)(2,1)S(1)} %get-tuple-element.85), channel_id=1, source_target_pairs={{0,12},{1,13},{2,14},{3,15},{4,8},{5,9},{6,10},{7,11},{8,4},{9,5},... | collective-permute-start | bytes 245768 | tf_op jit(solution)/shard_map/ppermute | solution.py:22
  25.7 4.3 %shard_map.93 = (f32[4,160,256]{2,1,0:T(8,128)S(1)}, f32[4,2,16,256]{3,2,1,0:T(8,128)S(1)}, f32[40,256]{1,0:T(8,128)S(1)}, bf16[160,256]{1,0:T(8,128)(2,1)S(1)},...) custom-call(s32[7]{0:T(128)S(1)} %stack.39.refs_0_.g_ref, f32[3,7,256]{2,1,0:T(8,128)S(1)} %get-tuple-element.59.refs_1_, ...), custom_call_target="tpu_custom_call" | custom-call | flops 690000000 | bytes 2214000 | tf_op jit(solution)/shard_map/pallas_call | solution.py:385
  30.0 2.9 %collective-permute-start.5 = (bf16[160,256]{1,0:T(8,128)(2,1)S(1)}, bf16[160,256]{1,0:T(8,128)(2,1)S(1)}, u32[]{:S(2)}, u32[]{:S(2)}) collective-permute-start(bf16[160,256]{1,0:T(8,128)(2,1)S(1)} %get-tuple-element.76), channel_id=1, source_target_pairs={{0,16},{1,17},{2,18},{3,19},{4,20},{5,21},{6,22},{7,23},{8,24},{9,... | collective-permute-start | bytes 245768 | tf_op jit(solution)/shard_map/ppermute | solution.py:22
  33.0 2.2 %shard_map.94 = (f32[3,160,256]{2,1,0:T(8,128)S(1)}, f32[640,256]{1,0:T(8,128)S(1)}) custom-call(s32[7]{0:T(128)S(1)} %stack.39.refs_0_.g_ref, f32[3,7,256]{2,1,0:T(8,128)S(1)} %get-tuple-element.59.refs_1_, f32[4,160,256]{2,1,0:T(8,128)S(1)} %get-tuple-element.81.refs_2_, f32[320,256]{1,0:T(8,128)S(1)} %get-tuple-element.79.refs_3_.refs_7_, ...), custom_call_target="tpu_custom_call" | custom-call | flops 3564999936 | bytes 11439000 | tf_op jit(solution)/shard_map/pallas_call | solution.py:385
  35.2 4.9 %collective-permute-start.10 = (bf16[448,512]{1,0:T(8,128)(2,1)S(1)}, bf16[448,512]{1,0:T(8,128)(2,1)S(1)}, u32[]{:S(2)}, u32[]{:S(2)}) collective-permute-start(bf16[448,512]{1,0:T(8,128)(2,1)S(1)} %slice.14), channel_id=1, source_target_pairs={{0,24},{1,25},{2,26},{3,27},{4,28},{5,29},{6,30},{7,31},{24,0},{25... | collective-permute-start | bytes 1376264 | tf_op jit(solution)/shard_map/ppermute | solution.py:39
  40.9 5.0 %shard_map.95.h0 = bf16[640,256]{1,0:T(8,128)(2,1)S(1)} custom-call(s32[7]{0:T(128)S(1)} %stack.39.refs_0_.g_ref, f32[3,7,256]{2,1,0:T(8,128)S(1)} %get-tuple-element.59.refs_1_, f32[40,256]{1,0:T(8,128)S(1)} %collective-permute-done.4.refs_2_, bf16[160,256]{1,0:T(8,128)(2,1)S(1)} %collective-permute-done.5.refs_3_, ...), custom_call_target="tpu_custom_call" | custom-call | flops 5980000256 | bytes 19188000 | tf_op jit(solution)/shard_map/pallas_call | solution.py:385
  47.8 4.6 %collective-permute-done.10.out_late = bf16[448,512]{1,0:T(8,128)(2,1)S(1)} collective-permute-done((bf16[448,512]{1,0:T(8,128)(2,1)S(1)}, bf16[448,512]{1,0:T(8,128)(2,1)S(1)}, u32[]{:S(2)}, u32[]{:S(2)}) %collective-permute-start.10) | collective-permute-done | bytes 458784 | tf_op jit(solution)/shard_map/ppermute | solution.py:39
  52.4 2.2 %collective-permute-done.9.h1 = bf16[640,256]{1,0:T(8,128)(2,1)S(1)} collective-permute-done((bf16[640,256]{1,0:T(8,128)(2,1)S(1)}, bf16[640,256]{1,0:T(8,128)(2,1)S(1)}, u32[]{:S(2)}, u32[]{:S(2)}) %collective-permute-start.9) | collective-permute-done | bytes 327712 | tf_op jit(solution)/shard_map/ppermute | solution.py:22
  54.7 3.6 %collective-permute-done.11.h2 = bf16[640,256]{1,0:T(8,128)(2,1)S(1)} collective-permute-done((bf16[640,256]{1,0:T(8,128)(2,1)S(1)}, bf16[640,256]{1,0:T(8,128)(2,1)S(1)}, u32[]{:S(2)}, u32[]{:S(2)}) %collective-permute-start.11) | collective-permute-done | bytes 327712 | tf_op jit(solution)/shard_map/ppermute | solution.py:22
  58.3 1.5 %collective-permute-start.13 = (bf16[160,256]{1,0:T(8,128)(2,1)S(1)}, bf16[160,256]{1,0:T(8,128)(2,1)S(1)}, u32[]{:S(2)}, u32[]{:S(2)}) collective-permute-start(bf16[160,256]{1,0:T(8,128)(2,1)S(1)} %slice.17), channel_id=1, source_target_pairs={{0,4},{1,5},{2,6},{3,7},{4,0},{5,1},{6,2},{7,3},{8,12},{9,13},{10,... | collective-permute-start | bytes 245768 | tf_op jit(solution)/shard_map/ppermute | solution.py:22
  59.8 2.0 %shard_map.96 = (f32[2,2,640,256]{3,2,1,0:T(8,128)S(1)}, bf16[1024,512]{1,0:T(8,128)(2,1)S(1)}) custom-call(s32[7]{0:T(128)S(1)} %stack.39.refs_0_.g_ref, bf16[640,256]{1,0:T(8,128)(2,1)S(1)} %shard_map.95.h0, bf16[640,256]{1,0:T(8,128)(2,1)S(1)} %collective-permute-done.9.h1, bf16[640,256]{1,0:T(8,128)(2,1)S(1)} %collective-permute-done.11.h2, ...), custom_call_target="tpu_custom_call" | custom-call | flops 2300000000 | bytes 7380000 | tf_op jit(solution)/shard_map/pallas_call | solution.py:385
  66.0 1.3 %collective-permute-start.18 = (bf16[160,256]{1,0:T(8,128)(2,1)S(1)}, bf16[160,256]{1,0:T(8,128)(2,1)S(1)}, u32[]{:S(2)}, u32[]{:S(2)}) collective-permute-start(bf16[160,256]{1,0:T(8,128)(2,1)S(1)} %get-tuple-element.106), channel_id=1, source_target_pairs={{0,3},{1,11},{2,0},{3,8},{4,7},{5,15},{6,4},{7,12},{8,2},{9,10},{1... | collective-permute-start | bytes 245768 | tf_op jit(solution)/shard_map/ppermute | solution.py:496
  67.3 2.2 %collective-permute-start.20 = (bf16[160,256]{1,0:T(8,128)(2,1)S(1)}, bf16[160,256]{1,0:T(8,128)(2,1)S(1)}, u32[]{:S(2)}, u32[]{:S(2)}) collective-permute-start(bf16[160,256]{1,0:T(8,128)(2,1)S(1)} %get-tuple-element.108), channel_id=1, source_target_pairs={{0,7},{1,15},{2,4},{3,12},{4,3},{5,11},{6,0},{7,8},{8,6},{9,14},{1... | collective-permute-start | bytes 245768 | tf_op jit(solution)/shard_map/ppermute | solution.py:496
  70.8 1.8 %collective-permute-start.24 = (bf16[160,256]{1,0:T(8,128)(2,1)S(1)}, bf16[160,256]{1,0:T(8,128)(2,1)S(1)}, u32[]{:S(2)}, u32[]{:S(2)}) collective-permute-start(bf16[160,256]{1,0:T(8,128)(2,1)S(1)} %get-tuple-element.112), channel_id=1, source_target_pairs={{0,15},{1,7},{2,12},{3,4},{4,11},{5,3},{6,8},{7,0},{8,14},{9,6},{1... | collective-permute-start | bytes 245768 | tf_op jit(solution)/shard_map/ppermute | solution.py:496
  74.4 5.0 %collective-permute-start.21 = (bf16[160,256]{1,0:T(8,128)(2,1)S(1)}, bf16[160,256]{1,0:T(8,128)(2,1)S(1)}, u32[]{:S(2)}, u32[]{:S(2)}) collective-permute-start(bf16[160,256]{1,0:T(8,128)(2,1)S(1)} %get-tuple-element.109), channel_id=1, source_target_pairs={{0,8},{1,0},{2,11},{3,3},{4,12},{5,4},{6,15},{7,7},{8,9},{9,1},{10... | collective-permute-start | bytes 245768 | tf_op jit(solution)/shard_map/ppermute | solution.py:496
  81.5 2.8 %collective-permute-done.23.refs_6_ = bf16[160,256]{1,0:T(8,128)(2,1)S(1)} collective-permute-done((bf16[160,256]{1,0:T(8,128)(2,1)S(1)}, bf16[160,256]{1,0:T(8,128)(2,1)S(1)}, u32[]{:S(2)}, u32[]{:S(2)}) %collective-permute-start.23) | collective-permute-done | bytes 81952 | tf_op jit(solution)/shard_map/ppermute | solution.py:496
  84.3 1.3 %shard_map.101 = bf16[160,1024]{1,0:T(8,128)(2,1)} custom-call(s32[7]{0:T(128)S(1)} %stack.39.refs_0_.g_ref, bf16[160,256]{1,0:T(8,128)(2,1)S(1)} %collective-permute-done.16.refs_0_, bf16[160,256]{1,0:T(8,128)(2,1)S(1)} %collective-permute-done.18.refs_1_, bf16[160,256]{1,0:T(8,128)(2,1)S(1)} %collective-permute-done.19.refs_2_, ...), custom_call_target="tpu_custom_call" | custom-call | flops 1495000064 | bytes 4797000 | tf_op jit(solution)/shard_map/pallas_call | solution.py:385
  (60 shorter events, 15.5 us)
Async XLA Ops:
  1.1 28.9 %collective-permute-start.3 = (bf16[576,512]{1,0:T(8,128)(2,1)S(1)}, bf16[576,512]{1,0:T(8,128)(2,1)S(1)}, u32[]{:S(2)}, u32[]{:S(2)}) collective-permute-start(bf16[576,512]{1,0:T(8,128)(2,1)S(1)} %slice.13), channel_id=1, source_target_pairs={{0,24},{1,25},{2,26},{3,27},{4,28},{5,29},{6,30},{7,31},{8,16},{9,... | collective-permute-start | bytes 1769480 | tf_op jit(solution)/shard_map/ppermute | solution.py:22
  10.4 7.7 %collective-permute-start = (bf16[208,256]{1,0:T(8,128)(2,1)S(1)}, bf16[208,256]{1,0:T(8,128)(2,1)S(1)}, u32[]{:S(2)}, u32[]{:S(2)}) collective-permute-start(bf16[208,256]{1,0:T(8,128)(2,1)S(1)} %get-tuple-element.70), channel_id=1, source_target_pairs={{0,4},{1,5},{2,6},{3,7},{4,0},{5,1},{6,2},{7,3},{8,12},{9,13},{10,... | collective-permute-start | bytes 319496 | tf_op jit(solution)/shard_map/ppermute | solution.py:22
  12.0 10.3 %collective-permute-start.1 = (bf16[208,256]{1,0:T(8,128)(2,1)S(1)}, bf16[208,256]{1,0:T(8,128)(2,1)S(1)}, u32[]{:S(2)}, u32[]{:S(2)}) collective-permute-start(bf16[208,256]{1,0:T(8,128)(2,1)S(1)} %get-tuple-element.71), channel_id=1, source_target_pairs={{0,8},{1,9},{2,10},{3,11},{4,12},{5,13},{6,14},{7,15},{8,0},{9,1},... | collective-permute-start | bytes 319496 | tf_op jit(solution)/shard_map/ppermute | solution.py:22
  12.0 13.8 %collective-permute-start.2 = (bf16[208,256]{1,0:T(8,128)(2,1)S(1)}, bf16[208,256]{1,0:T(8,128)(2,1)S(1)}, u32[]{:S(2)}, u32[]{:S(2)}) collective-permute-start(bf16[208,256]{1,0:T(8,128)(2,1)S(1)} %get-tuple-element.72), channel_id=1, source_target_pairs={{0,12},{1,13},{2,14},{3,15},{4,8},{5,9},{6,10},{7,11},{8,4},{9,5},... | collective-permute-start | bytes 319496 | tf_op jit(solution)/shard_map/ppermute | solution.py:22
  16.6 16.5 %collective-permute-start.6 = (bf16[160,256]{1,0:T(8,128)(2,1)S(1)}, bf16[160,256]{1,0:T(8,128)(2,1)S(1)}, u32[]{:S(2)}, u32[]{:S(2)}) collective-permute-start(bf16[160,256]{1,0:T(8,128)(2,1)S(1)} %get-tuple-element.83), channel_id=1, source_target_pairs={{0,4},{1,5},{2,6},{3,7},{4,0},{5,1},{6,2},{7,3},{8,12},{9,13},{10,... | collective-permute-start | bytes 245768 | tf_op jit(solution)/shard_map/ppermute | solution.py:22
  18.1 14.9 %collective-permute-start.7 = (bf16[160,256]{1,0:T(8,128)(2,1)S(1)}, bf16[160,256]{1,0:T(8,128)(2,1)S(1)}, u32[]{:S(2)}, u32[]{:S(2)}) collective-permute-start(bf16[160,256]{1,0:T(8,128)(2,1)S(1)} %get-tuple-element.84), channel_id=1, source_target_pairs={{0,8},{1,9},{2,10},{3,11},{4,12},{5,13},{6,14},{7,15},{8,0},{9,1},... | collective-permute-start | bytes 245768 | tf_op jit(solution)/shard_map/ppermute | solution.py:22
  22.3 10.8 %collective-permute-start.8 = (bf16[160,256]{1,0:T(8,128)(2,1)S(1)}, bf16[160,256]{1,0:T(8,128)(2,1)S(1)}, u32[]{:S(2)}, u32[]{:S(2)}) collective-permute-start(bf16[160,256]{1,0:T(8,128)(2,1)S(1)} %get-tuple-element.85), channel_id=1, source_target_pairs={{0,12},{1,13},{2,14},{3,15},{4,8},{5,9},{6,10},{7,11},{8,4},{9,5},... | collective-permute-start | bytes 245768 | tf_op jit(solution)/shard_map/ppermute | solution.py:22
  30.0 10.9 %collective-permute-start.5 = (bf16[160,256]{1,0:T(8,128)(2,1)S(1)}, bf16[160,256]{1,0:T(8,128)(2,1)S(1)}, u32[]{:S(2)}, u32[]{:S(2)}) collective-permute-start(bf16[160,256]{1,0:T(8,128)(2,1)S(1)} %get-tuple-element.76), channel_id=1, source_target_pairs={{0,16},{1,17},{2,18},{3,19},{4,20},{5,21},{6,22},{7,23},{8,24},{9,... | collective-permute-start | bytes 245768 | tf_op jit(solution)/shard_map/ppermute | solution.py:22
  32.9 8.0 %collective-permute-start.4 = (f32[40,256]{1,0:T(8,128)S(1)}, f32[40,256]{1,0:T(8,128)S(1)}, u32[]{:S(2)}, u32[]{:S(2)}) collective-permute-start(f32[40,256]{1,0:T(8,128)S(1)} %get-tuple-element.75), channel_id=1, source_target_pairs={{0,16},{1,17},{2,18},{3,19},{4,20},{5,21},{6,22},{7,23},{8,24},{9,... | collective-permute-start | bytes 122888 | tf_op jit(solution)/shard_map/ppermute | solution.py:22
  35.2 17.1 %collective-permute-start.10 = (bf16[448,512]{1,0:T(8,128)(2,1)S(1)}, bf16[448,512]{1,0:T(8,128)(2,1)S(1)}, u32[]{:S(2)}, u32[]{:S(2)}) collective-permute-start(bf16[448,512]{1,0:T(8,128)(2,1)S(1)} %slice.14), channel_id=1, source_target_pairs={{0,24},{1,25},{2,26},{3,27},{4,28},{5,29},{6,30},{7,31},{24,0},{25... | collective-permute-start | bytes 1376264 | tf_op jit(solution)/shard_map/ppermute | solution.py:39
  40.2 19.6 %collective-permute-start.12 = (bf16[448,512]{1,0:T(8,128)(2,1)S(1)}, bf16[448,512]{1,0:T(8,128)(2,1)S(1)}, u32[]{:S(2)}, u32[]{:S(2)}) collective-permute-start(bf16[448,512]{1,0:T(8,128)(2,1)S(1)} %slice.14), channel_id=1, source_target_pairs={{8,16},{9,17},{10,18},{11,19},{12,20},{13,21},{14,22},{15,23},{16,... | collective-permute-start | bytes 1376264 | tf_op jit(solution)/shard_map/ppermute | solution.py:39
  45.9 8.8 %collective-permute-start.9 = (bf16[640,256]{1,0:T(8,128)(2,1)S(1)}, bf16[640,256]{1,0:T(8,128)(2,1)S(1)}, u32[]{:S(2)}, u32[]{:S(2)}) collective-permute-start(bf16[640,256]{1,0:T(8,128)(2,1)S(1)} %shard_map.95.h0), channel_id=1, source_target_pairs={{0,4},{1,5},{2,6},{3,7},{4,0},{5,1},{6,2},{7,3},{8,12},{9,13},{10,... | collective-permute-start | bytes 983048 | tf_op jit(solution)/shard_map/ppermute | solution.py:22
  46.5 11.8 %collective-permute-start.11 = (bf16[640,256]{1,0:T(8,128)(2,1)S(1)}, bf16[640,256]{1,0:T(8,128)(2,1)S(1)}, u32[]{:S(2)}, u32[]{:S(2)}) collective-permute-start(bf16[640,256]{1,0:T(8,128)(2,1)S(1)} %shard_map.95.h0), channel_id=1, source_target_pairs={{0,8},{1,9},{2,10},{3,11},{4,12},{5,13},{6,14},{7,15},{8,0},{9,1},... | collective-permute-start | bytes 983048 | tf_op jit(solution)/shard_map/ppermute | solution.py:22
  54.6 8.1 %collective-permute-start.14 = (bf16[480,256]{1,0:T(8,128)(2,1)S(1)}, bf16[480,256]{1,0:T(8,128)(2,1)S(1)}, u32[]{:S(2)}, u32[]{:S(2)}) collective-permute-start(bf16[480,256]{1,0:T(8,128)(2,1)S(1)} %slice.16), channel_id=1, source_target_pairs={{0,8},{1,9},{2,10},{3,11},{4,12},{5,13},{6,14},{7,15},{8,0},{9,1},... | collective-permute-start | bytes 737288 | tf_op jit(solution)/shard_map/ppermute | solution.py:22
  58.3 4.4 %collective-permute-start.13 = (bf16[160,256]{1,0:T(8,128)(2,1)S(1)}, bf16[160,256]{1,0:T(8,128)(2,1)S(1)}, u32[]{:S(2)}, u32[]{:S(2)}) collective-permute-start(bf16[160,256]{1,0:T(8,128)(2,1)S(1)} %slice.17), channel_id=1, source_target_pairs={{0,4},{1,5},{2,6},{3,7},{4,0},{5,1},{6,2},{7,3},{8,12},{9,13},{10,... | collective-permute-start | bytes 245768 | tf_op jit(solution)/shard_map/ppermute | solution.py:22
  64.6 8.0 %collective-permute-start.15 = (bf16[640,256]{1,0:T(8,128)(2,1)S(1)}, bf16[640,256]{1,0:T(8,128)(2,1)S(1)}, u32[]{:S(2)}, u32[]{:S(2)}) collective-permute-start(bf16[640,256]{1,0:T(8,128)(2,1)S(1)} %get-tuple-element.102), channel_id=1, source_target_pairs={{0,1},{1,0},{2,3},{3,2},{4,5},{5,4},{6,7},{7,6},{8,9},{9,8},{10,11... | collective-permute-start | bytes 983048 | tf_op jit(solution)/shard_map/ppermute | solution.py:22
  66.0 7.9 %collective-permute-start.18 = (bf16[160,256]{1,0:T(8,128)(2,1)S(1)}, bf16[160,256]{1,0:T(8,128)(2,1)S(1)}, u32[]{:S(2)}, u32[]{:S(2)}) collective-permute-start(bf16[160,256]{1,0:T(8,128)(2,1)S(1)} %get-tuple-element.106), channel_id=1, source_target_pairs={{0,3},{1,11},{2,0},{3,8},{4,7},{5,15},{6,4},{7,12},{8,2},{9,10},{1... | collective-permute-start | bytes 245768 | tf_op jit(solution)/shard_map/ppermute | solution.py:496
  67.3 7.2 %collective-permute-start.20 = (bf16[160,256]{1,0:T(8,128)(2,1)S(1)}, bf16[160,256]{1,0:T(8,128)(2,1)S(1)}, u32[]{:S(2)}, u32[]{:S(2)}) collective-permute-start(bf16[160,256]{1,0:T(8,128)(2,1)S(1)} %get-tuple-element.108), channel_id=1, source_target_pairs={{0,7},{1,15},{2,4},{3,12},{4,3},{5,11},{6,0},{7,8},{8,6},{9,14},{1... | collective-permute-start | bytes 245768 | tf_op jit(solution)/shard_map/ppermute | solution.py:496
  69.5 10.0 %collective-permute-start.22 = (bf16[160,256]{1,0:T(8,128)(2,1)S(1)}, bf16[160,256]{1,0:T(8,128)(2,1)S(1)}, u32[]{:S(2)}, u32[]{:S(2)}) collective-permute-start(bf16[160,256]{1,0:T(8,128)(2,1)S(1)} %get-tuple-element.110), channel_id=1, source_target_pairs={{0,11},{1,3},{2,8},{3,0},{4,15},{5,7},{6,12},{7,4},{8,10},{9,2},{1... | collective-permute-start | bytes 245768 | tf_op jit(solution)/shard_map/ppermute | solution.py:496
  70.8 9.7 %collective-permute-start.24 = (bf16[160,256]{1,0:T(8,128)(2,1)S(1)}, bf16[160,256]{1,0:T(8,128)(2,1)S(1)}, u32[]{:S(2)}, u32[]{:S(2)}) collective-permute-start(bf16[160,256]{1,0:T(8,128)(2,1)S(1)} %get-tuple-element.112), channel_id=1, source_target_pairs={{0,15},{1,7},{2,12},{3,4},{4,11},{5,3},{6,8},{7,0},{8,14},{9,6},{1... | collective-permute-start | bytes 245768 | tf_op jit(solution)/shard_map/ppermute | solution.py:496
  73.2 7.2 %collective-permute-start.16 = (bf16[160,256]{1,0:T(8,128)(2,1)S(1)}, bf16[160,256]{1,0:T(8,128)(2,1)S(1)}, u32[]{:S(2)}, u32[]{:S(2)}) collective-permute-start(bf16[160,256]{1,0:T(8,128)(2,1)S(1)} %get-tuple-element.103), channel_id=1, source_target_pairs={{0,0},{1,8},{2,3},{3,11},{4,4},{5,12},{6,7},{7,15},{8,1},{9,9},{10... | collective-permute-start | bytes 245768 | tf_op jit(solution)/shard_map/ppermute | solution.py:496
  73.9 6.6 %collective-permute-start.19 = (bf16[160,256]{1,0:T(8,128)(2,1)S(1)}, bf16[160,256]{1,0:T(8,128)(2,1)S(1)}, u32[]{:S(2)}, u32[]{:S(2)}) collective-permute-start(bf16[160,256]{1,0:T(8,128)(2,1)S(1)} %get-tuple-element.107), channel_id=1, source_target_pairs={{0,4},{1,12},{2,7},{3,15},{4,0},{5,8},{6,3},{7,11},{8,5},{9,13},{1... | collective-permute-start | bytes 245768 | tf_op jit(solution)/shard_map/ppermute | solution.py:496
  74.4 7.1 %collective-permute-start.21 = (bf16[160,256]{1,0:T(8,128)(2,1)S(1)}, bf16[160,256]{1,0:T(8,128)(2,1)S(1)}, u32[]{:S(2)}, u32[]{:S(2)}) collective-permute-start(bf16[160,256]{1,0:T(8,128)(2,1)S(1)} %get-tuple-element.109), channel_id=1, source_target_pairs={{0,8},{1,0},{2,11},{3,3},{4,12},{5,4},{6,15},{7,7},{8,9},{9,1},{10... | collective-permute-start | bytes 245768 | tf_op jit(solution)/shard_map/ppermute | solution.py:496
  79.5 4.8 %collective-permute-start.23 = (bf16[160,256]{1,0:T(8,128)(2,1)S(1)}, bf16[160,256]{1,0:T(8,128)(2,1)S(1)}, u32[]{:S(2)}, u32[]{:S(2)}) collective-permute-start(bf16[160,256]{1,0:T(8,128)(2,1)S(1)} %get-tuple-element.111), channel_id=1, source_target_pairs={{0,12},{1,4},{2,15},{3,7},{4,8},{5,0},{6,11},{7,3},{8,13},{9,5},{1... | collective-permute-start | bytes 245768 | tf_op jit(solution)/shard_map/ppermute | solution.py:496
  (10 other events, 52.4 us)

commit v6 on v5

--- a/solution.py
+++ b/solution.py
@@ -468,8 +468,8 @@
     )
     hid = [hidden] + [swap(hidden, SLOT_BITS[m]) for m in (1, 2)]
     hid[1], out_late = lax.optimization_barrier((hid[1], out_late))
-    passed = swap(hid[1][rows:], SLOT_BITS[2])
-    hid += [swap(hid[2][:rows], SLOT_BITS[1]), passed]
+    passed = swap(hid[1][96:], SLOT_BITS[2])
+    hid += [swap(hid[2][:96], SLOT_BITS[1]), passed]
     half = out_weight.shape[1] // 2
     acc, far = call(
         2.0,

time: 85.9 us -> 85.8 us (level)
  transfers between devices with their start and end apart: 25 -> 25, of which waited for: 8 -> 9; matrix products, arithmetic and copies ran while one was open for 0% -> 0% of each run, Pallas kernels for 23% -> 23%
where the time goes in v6:
time: 85.8 us; the launch traced here: 85.6 us
  starting transfers between devices  39.5 us (46%)
  Pallas kernels  22.3 us (26%)
  waiting for transfers between devices  20.2 us (24%)
  local copies, waits for them, and re-layouts  3.37 us (4%)
    ppermute x15, starting transfers between devices, swap(): return lax.ppermute(block, AXES, [(i, i ^ bits) for i in range(32)])  20.7 us
    pallas_call x10, Pallas kernels, call(): pl.pallas_call(kernel, out_shape=tuple((jax.ShapeDtypeStruct(s, d) for s,...  20.3 us
    ppermute x8, starting transfers between devices, fast_body(): blocks[n, c] = lax.ppermute(part, AXES, homeward(n >> 1, n & 1, c))  13.2 us
    ppermute x15, waiting for transfers between devices, swap(): return lax.ppermute(block, AXES, [(i, i ^ bits) for i in range(32)])  11.7 us
    ppermute x2, starting transfers between devices, far_swap(): lax.ppermute(block, AXES, [(i, i ^ BITS_FAR) for i in range(32) if outer(...  5.62 us
    ppermute x2, waiting for transfers between devices, far_swap(): lax.ppermute(block, AXES, [(i, i ^ BITS_FAR) for i in range(32) if outer(...  4.63 us
    ppermute x8, waiting for transfers between devices, fast_body(): blocks[n, c] = lax.ppermute(part, AXES, homeward(n >> 1, n & 1, c))  3.87 us
    unnamed x18, local copies, waits for them, and re-layouts  2.13 us
  transfers between devices with their start and end apart: 25, of which 9 were waited for; matrix products, arithmetic and copies ran while one was open for 0% of the time, Pallas kernels for 23%

profile of v6, /device:TPU:0, one launch (start us, length us, event | category | flops | bytes accessed | tf_op | source)
XLA Modules:
  0.0 85.6 jit_solution(7083836248612668591)
XLA Ops:
  1.1 5.1 %collective-permute-start.3 = (bf16[576,512]{1,0:T(8,128)(2,1)S(1)}, bf16[576,512]{1,0:T(8,128)(2,1)S(1)}, u32[]{:S(2)}, u32[]{:S(2)}) collective-permute-start(bf16[576,512]{1,0:T(8,128)(2,1)S(1)} %slice.13), channel_id=1, source_target_pairs={{0,24},{1,25},{2,26},{3,27},{4,28},{5,29},{6,30},{7,31},{8,16},{9,... | collective-permute-start | bytes 1769480 | tf_op jit(solution)/shard_map/ppermute | solution.py:22
  8.4 1.9 %shard_map.92 = (bf16[208,256]{1,0:T(8,128)(2,1)S(1)}, bf16[208,256]{1,0:T(8,128)(2,1)S(1)}, bf16[208,256]{1,0:T(8,128)(2,1)S(1)}, bf16[208,256]{1,0:T(8,128)(2,...) custom-call(s32[7]{0:T(128)S(1)} %stack.39.refs_0_.g_ref, ...), custom_call_target="tpu_custom_call" | custom-call | flops 2000000000 | bytes 6000000 | tf_op jit(solution)/shard_map/pallas_call | solution.py:416
  10.4 1.6 %collective-permute-start = (bf16[208,256]{1,0:T(8,128)(2,1)S(1)}, bf16[208,256]{1,0:T(8,128)(2,1)S(1)}, u32[]{:S(2)}, u32[]{:S(2)}) collective-permute-start(bf16[208,256]{1,0:T(8,128)(2,1)S(1)} %get-tuple-element.70), channel_id=1, source_target_pairs={{0,4},{1,5},{2,6},{3,7},{4,0},{5,1},{6,2},{7,3},{8,12},{9,13},{10,... | collective-permute-start | bytes 319496 | tf_op jit(solution)/shard_map/ppermute | solution.py:22
  12.0 2.0 %collective-permute-start.2 = (bf16[208,256]{1,0:T(8,128)(2,1)S(1)}, bf16[208,256]{1,0:T(8,128)(2,1)S(1)}, u32[]{:S(2)}, u32[]{:S(2)}) collective-permute-start(bf16[208,256]{1,0:T(8,128)(2,1)S(1)} %get-tuple-element.72), channel_id=1, source_target_pairs={{0,12},{1,13},{2,14},{3,15},{4,8},{5,9},{6,10},{7,11},{8,4},{9,5},... | collective-permute-start | bytes 319496 | tf_op jit(solution)/shard_map/ppermute | solution.py:22
  14.0 2.6 %shard_map.91 = (f32[288,256]{1,0:T(8,128)S(1)}, f32[320,256]{1,0:T(8,128)S(1)}, f32[16,160,256]{2,1,0:T(8,128)S(1)}, f32[16,160,256]{2,1,0:T(8,128)S(1)}, f32[4...) custom-call(s32[7]{0:T(128)S(1)} %stack.39.refs_0_.g_ref, f32[128,1024]{1,0:T(8,128)S(1)} %copy-done.2, ...), custom_call_target="tpu_custom_call" | custom-call | flops 345000000 | bytes 1107000 | tf_op jit(solution)/shard_map/pallas_call | solution.py:385
  16.6 1.6 %collective-permute-start.6 = (bf16[160,256]{1,0:T(8,128)(2,1)S(1)}, bf16[160,256]{1,0:T(8,128)(2,1)S(1)}, u32[]{:S(2)}, u32[]{:S(2)}) collective-permute-start(bf16[160,256]{1,0:T(8,128)(2,1)S(1)} %get-tuple-element.83), channel_id=1, source_target_pairs={{0,4},{1,5},{2,6},{3,7},{4,0},{5,1},{6,2},{7,3},{8,12},{9,13},{10,... | collective-permute-start | bytes 245768 | tf_op jit(solution)/shard_map/ppermute | solution.py:22
  18.1 4.2 %collective-permute-done.1.refs_9_ = bf16[208,256]{1,0:T(8,128)(2,1)S(1)} collective-permute-done((bf16[208,256]{1,0:T(8,128)(2,1)S(1)}, bf16[208,256]{1,0:T(8,128)(2,1)S(1)}, u32[]{:S(2)}, u32[]{:S(2)}) %collective-permute-start.1) | collective-permute-done | bytes 106528 | tf_op jit(solution)/shard_map/ppermute | solution.py:22
  22.3 3.4 %collective-permute-start.8 = (bf16[160,256]{1,0:T(8,128)(2,1)S(1)}, bf16[160,256]{1,0:T(8,128)(2,1)S(1)}, u32[]{:S(2)}, u32[]{:S(2)}) collective-permute-start(bf16[160,256]{1,0:T(8,128)(2,1)S(1)} %get-tuple-element.85), channel_id=1, source_target_pairs={{0,12},{1,13},{2,14},{3,15},{4,8},{5,9},{6,10},{7,11},{8,4},{9,5},... | collective-permute-start | bytes 245768 | tf_op jit(solution)/shard_map/ppermute | solution.py:22
  25.7 4.3 %shard_map.93 = (f32[4,160,256]{2,1,0:T(8,128)S(1)}, f32[4,2,16,256]{3,2,1,0:T(8,128)S(1)}, f32[40,256]{1,0:T(8,128)S(1)}, bf16[160,256]{1,0:T(8,128)(2,1)S(1)},...) custom-call(s32[7]{0:T(128)S(1)} %stack.39.refs_0_.g_ref, f32[3,7,256]{2,1,0:T(8,128)S(1)} %get-tuple-element.59.refs_1_, ...), custom_call_target="tpu_custom_call" | custom-call | flops 690000000 | bytes 2214000 | tf_op jit(solution)/shard_map/pallas_call | solution.py:385
  30.0 2.9 %collective-permute-start.5 = (bf16[160,256]{1,0:T(8,128)(2,1)S(1)}, bf16[160,256]{1,0:T(8,128)(2,1)S(1)}, u32[]{:S(2)}, u32[]{:S(2)}) collective-permute-start(bf16[160,256]{1,0:T(8,128)(2,1)S(1)} %get-tuple-element.76), channel_id=1, source_target_pairs={{0,16},{1,17},{2,18},{3,19},{4,20},{5,21},{6,22},{7,23},{8,24},{9,... | collective-permute-start | bytes 245768 | tf_op jit(solution)/shard_map/ppermute | solution.py:22
  33.0 2.2 %shard_map.94 = (f32[3,160,256]{2,1,0:T(8,128)S(1)}, f32[640,256]{1,0:T(8,128)S(1)}) custom-call(s32[7]{0:T(128)S(1)} %stack.39.refs_0_.g_ref, f32[3,7,256]{2,1,0:T(8,128)S(1)} %get-tuple-element.59.refs_1_, f32[4,160,256]{2,1,0:T(8,128)S(1)} %get-tuple-element.81.refs_2_, f32[320,256]{1,0:T(8,128)S(1)} %get-tuple-element.79.refs_3_.refs_7_, ...), custom_call_target="tpu_custom_call" | custom-call | flops 3564999936 | bytes 11439000 | tf_op jit(solution)/shard_map/pallas_call | solution.py:385
  35.2 4.9 %collective-permute-start.10 = (bf16[448,512]{1,0:T(8,128)(2,1)S(1)}, bf16[448,512]{1,0:T(8,128)(2,1)S(1)}, u32[]{:S(2)}, u32[]{:S(2)}) collective-permute-start(bf16[448,512]{1,0:T(8,128)(2,1)S(1)} %slice.14), channel_id=1, source_target_pairs={{0,24},{1,25},{2,26},{3,27},{4,28},{5,29},{6,30},{7,31},{24,0},{25... | collective-permute-start | bytes 1376264 | tf_op jit(solution)/shard_map/ppermute | solution.py:39
  40.9 5.0 %shard_map.95.h0 = bf16[640,256]{1,0:T(8,128)(2,1)S(1)} custom-call(s32[7]{0:T(128)S(1)} %stack.39.refs_0_.g_ref, f32[3,7,256]{2,1,0:T(8,128)S(1)} %get-tuple-element.59.refs_1_, f32[40,256]{1,0:T(8,128)S(1)} %collective-permute-done.4.refs_2_, bf16[160,256]{1,0:T(8,128)(2,1)S(1)} %collective-permute-done.5.refs_3_, ...), custom_call_target="tpu_custom_call" | custom-call | flops 5980000256 | bytes 19188000 | tf_op jit(solution)/shard_map/pallas_call | solution.py:385
  47.8 4.6 %collective-permute-done.10.out_late = bf16[448,512]{1,0:T(8,128)(2,1)S(1)} collective-permute-done((bf16[448,512]{1,0:T(8,128)(2,1)S(1)}, bf16[448,512]{1,0:T(8,128)(2,1)S(1)}, u32[]{:S(2)}, u32[]{:S(2)}) %collective-permute-start.10) | collective-permute-done | bytes 458784 | tf_op jit(solution)/shard_map/ppermute | solution.py:39
  52.4 2.2 %collective-permute-done.9.h1 = bf16[640,256]{1,0:T(8,128)(2,1)S(1)} collective-permute-done((bf16[640,256]{1,0:T(8,128)(2,1)S(1)}, bf16[640,256]{1,0:T(8,128)(2,1)S(1)}, u32[]{:S(2)}, u32[]{:S(2)}) %collective-permute-start.9) | collective-permute-done | bytes 327712 | tf_op jit(solution)/shard_map/ppermute | solution.py:22
  54.7 3.6 %collective-permute-done.11.h2 = bf16[640,256]{1,0:T(8,128)(2,1)S(1)} collective-permute-done((bf16[640,256]{1,0:T(8,128)(2,1)S(1)}, bf16[640,256]{1,0:T(8,128)(2,1)S(1)}, u32[]{:S(2)}, u32[]{:S(2)}) %collective-permute-start.11) | collective-permute-done | bytes 327712 | tf_op jit(solution)/shard_map/ppermute | solution.py:22
  58.3 1.5 %collective-permute-start.13 = (bf16[96,256]{1,0:T(8,128)(2,1)S(1)}, bf16[96,256]{1,0:T(8,128)(2,1)S(1)}, u32[]{:S(2)}, u32[]{:S(2)}) collective-permute-start(bf16[96,256]{1,0:T(8,128)(2,1)S(1)} %slice.17), channel_id=1, source_target_pairs={{0,4},{1,5},{2,6},{3,7},{4,0},{5,1},{6,2},{7,3},{8,12},{9,13},{10,... | collective-permute-start | bytes 147464 | tf_op jit(solution)/shard_map/ppermute | solution.py:22
  59.7 2.0 %shard_map.96 = (f32[2,2,640,256]{3,2,1,0:T(8,128)S(1)}, bf16[1024,512]{1,0:T(8,128)(2,1)S(1)}) custom-call(s32[7]{0:T(128)S(1)} %stack.39.refs_0_.g_ref, bf16[640,256]{1,0:T(8,128)(2,1)S(1)} %shard_map.95.h0, bf16[640,256]{1,0:T(8,128)(2,1)S(1)} %collective-permute-done.9.h1, bf16[640,256]{1,0:T(8,128)(2,1)S(1)} %collective-permute-done.11.h2, ...), custom_call_target="tpu_custom_call" | custom-call | flops 2300000000 | bytes 7380000 | tf_op jit(solution)/shard_map/pallas_call | solution.py:385
  66.5 1.3 %collective-permute-start.18 = (bf16[160,256]{1,0:T(8,128)(2,1)S(1)}, bf16[160,256]{1,0:T(8,128)(2,1)S(1)}, u32[]{:S(2)}, u32[]{:S(2)}) collective-permute-start(bf16[160,256]{1,0:T(8,128)(2,1)S(1)} %get-tuple-element.106), channel_id=1, source_target_pairs={{0,3},{1,11},{2,0},{3,8},{4,7},{5,15},{6,4},{7,12},{8,2},{9,10},{1... | collective-permute-start | bytes 245768 | tf_op jit(solution)/shard_map/ppermute | solution.py:496
  67.8 1.6 %collective-permute-start.20 = (bf16[160,256]{1,0:T(8,128)(2,1)S(1)}, bf16[160,256]{1,0:T(8,128)(2,1)S(1)}, u32[]{:S(2)}, u32[]{:S(2)}) collective-permute-start(bf16[160,256]{1,0:T(8,128)(2,1)S(1)} %get-tuple-element.108), channel_id=1, source_target_pairs={{0,7},{1,15},{2,4},{3,12},{4,3},{5,11},{6,0},{7,8},{8,6},{9,14},{1... | collective-permute-start | bytes 245768 | tf_op jit(solution)/shard_map/ppermute | solution.py:496
  70.6 1.8 %collective-permute-start.24 = (bf16[160,256]{1,0:T(8,128)(2,1)S(1)}, bf16[160,256]{1,0:T(8,128)(2,1)S(1)}, u32[]{:S(2)}, u32[]{:S(2)}) collective-permute-start(bf16[160,256]{1,0:T(8,128)(2,1)S(1)} %get-tuple-element.112), channel_id=1, source_target_pairs={{0,15},{1,7},{2,12},{3,4},{4,11},{5,3},{6,8},{7,0},{8,14},{9,6},{1... | collective-permute-start | bytes 245768 | tf_op jit(solution)/shard_map/ppermute | solution.py:496
  74.3 5.1 %collective-permute-start.21 = (bf16[160,256]{1,0:T(8,128)(2,1)S(1)}, bf16[160,256]{1,0:T(8,128)(2,1)S(1)}, u32[]{:S(2)}, u32[]{:S(2)}) collective-permute-start(bf16[160,256]{1,0:T(8,128)(2,1)S(1)} %get-tuple-element.109), channel_id=1, source_target_pairs={{0,8},{1,0},{2,11},{3,3},{4,12},{5,4},{6,15},{7,7},{8,9},{9,1},{10... | collective-permute-start | bytes 245768 | tf_op jit(solution)/shard_map/ppermute | solution.py:496
  81.4 2.8 %collective-permute-done.23.refs_6_ = bf16[160,256]{1,0:T(8,128)(2,1)S(1)} collective-permute-done((bf16[160,256]{1,0:T(8,128)(2,1)S(1)}, bf16[160,256]{1,0:T(8,128)(2,1)S(1)}, u32[]{:S(2)}, u32[]{:S(2)}) %collective-permute-start.23) | collective-permute-done | bytes 81952 | tf_op jit(solution)/shard_map/ppermute | solution.py:496
  84.2 1.3 %shard_map.101 = bf16[160,1024]{1,0:T(8,128)(2,1)} custom-call(s32[7]{0:T(128)S(1)} %stack.39.refs_0_.g_ref, bf16[160,256]{1,0:T(8,128)(2,1)S(1)} %collective-permute-done.16.refs_0_, bf16[160,256]{1,0:T(8,128)(2,1)S(1)} %collective-permute-done.18.refs_1_, bf16[160,256]{1,0:T(8,128)(2,1)S(1)} %collective-permute-done.19.refs_2_, ...), custom_call_target="tpu_custom_call" | custom-call | flops 1495000064 | bytes 4797000 | tf_op jit(solution)/shard_map/pallas_call | solution.py:385
  (60 shorter events, 16.0 us)
Async XLA Ops:
  1.1 28.9 %collective-permute-start.3 = (bf16[576,512]{1,0:T(8,128)(2,1)S(1)}, bf16[576,512]{1,0:T(8,128)(2,1)S(1)}, u32[]{:S(2)}, u32[]{:S(2)}) collective-permute-start(bf16[576,512]{1,0:T(8,128)(2,1)S(1)} %slice.13), channel_id=1, source_target_pairs={{0,24},{1,25},{2,26},{3,27},{4,28},{5,29},{6,30},{7,31},{8,16},{9,... | collective-permute-start | bytes 1769480 | tf_op jit(solution)/shard_map/ppermute | solution.py:22
  10.4 7.7 %collective-permute-start = (bf16[208,256]{1,0:T(8,128)(2,1)S(1)}, bf16[208,256]{1,0:T(8,128)(2,1)S(1)}, u32[]{:S(2)}, u32[]{:S(2)}) collective-permute-start(bf16[208,256]{1,0:T(8,128)(2,1)S(1)} %get-tuple-element.70), channel_id=1, source_target_pairs={{0,4},{1,5},{2,6},{3,7},{4,0},{5,1},{6,2},{7,3},{8,12},{9,13},{10,... | collective-permute-start | bytes 319496 | tf_op jit(solution)/shard_map/ppermute | solution.py:22
  12.0 10.3 %collective-permute-start.1 = (bf16[208,256]{1,0:T(8,128)(2,1)S(1)}, bf16[208,256]{1,0:T(8,128)(2,1)S(1)}, u32[]{:S(2)}, u32[]{:S(2)}) collective-permute-start(bf16[208,256]{1,0:T(8,128)(2,1)S(1)} %get-tuple-element.71), channel_id=1, source_target_pairs={{0,8},{1,9},{2,10},{3,11},{4,12},{5,13},{6,14},{7,15},{8,0},{9,1},... | collective-permute-start | bytes 319496 | tf_op jit(solution)/shard_map/ppermute | solution.py:22
  12.0 13.8 %collective-permute-start.2 = (bf16[208,256]{1,0:T(8,128)(2,1)S(1)}, bf16[208,256]{1,0:T(8,128)(2,1)S(1)}, u32[]{:S(2)}, u32[]{:S(2)}) collective-permute-start(bf16[208,256]{1,0:T(8,128)(2,1)S(1)} %get-tuple-element.72), channel_id=1, source_target_pairs={{0,12},{1,13},{2,14},{3,15},{4,8},{5,9},{6,10},{7,11},{8,4},{9,5},... | collective-permute-start | bytes 319496 | tf_op jit(solution)/shard_map/ppermute | solution.py:22
  16.6 16.5 %collective-permute-start.6 = (bf16[160,256]{1,0:T(8,128)(2,1)S(1)}, bf16[160,256]{1,0:T(8,128)(2,1)S(1)}, u32[]{:S(2)}, u32[]{:S(2)}) collective-permute-start(bf16[160,256]{1,0:T(8,128)(2,1)S(1)} %get-tuple-element.83), channel_id=1, source_target_pairs={{0,4},{1,5},{2,6},{3,7},{4,0},{5,1},{6,2},{7,3},{8,12},{9,13},{10,... | collective-permute-start | bytes 245768 | tf_op jit(solution)/shard_map/ppermute | solution.py:22
  18.1 14.9 %collective-permute-start.7 = (bf16[160,256]{1,0:T(8,128)(2,1)S(1)}, bf16[160,256]{1,0:T(8,128)(2,1)S(1)}, u32[]{:S(2)}, u32[]{:S(2)}) collective-permute-start(bf16[160,256]{1,0:T(8,128)(2,1)S(1)} %get-tuple-element.84), channel_id=1, source_target_pairs={{0,8},{1,9},{2,10},{3,11},{4,12},{5,13},{6,14},{7,15},{8,0},{9,1},... | collective-permute-start | bytes 245768 | tf_op jit(solution)/shard_map/ppermute | solution.py:22
  22.3 10.8 %collective-permute-start.8 = (bf16[160,256]{1,0:T(8,128)(2,1)S(1)}, bf16[160,256]{1,0:T(8,128)(2,1)S(1)}, u32[]{:S(2)}, u32[]{:S(2)}) collective-permute-start(bf16[160,256]{1,0:T(8,128)(2,1)S(1)} %get-tuple-element.85), channel_id=1, source_target_pairs={{0,12},{1,13},{2,14},{3,15},{4,8},{5,9},{6,10},{7,11},{8,4},{9,5},... | collective-permute-start | bytes 245768 | tf_op jit(solution)/shard_map/ppermute | solution.py:22
  30.0 10.9 %collective-permute-start.5 = (bf16[160,256]{1,0:T(8,128)(2,1)S(1)}, bf16[160,256]{1,0:T(8,128)(2,1)S(1)}, u32[]{:S(2)}, u32[]{:S(2)}) collective-permute-start(bf16[160,256]{1,0:T(8,128)(2,1)S(1)} %get-tuple-element.76), channel_id=1, source_target_pairs={{0,16},{1,17},{2,18},{3,19},{4,20},{5,21},{6,22},{7,23},{8,24},{9,... | collective-permute-start | bytes 245768 | tf_op jit(solution)/shard_map/ppermute | solution.py:22
  32.9 8.0 %collective-permute-start.4 = (f32[40,256]{1,0:T(8,128)S(1)}, f32[40,256]{1,0:T(8,128)S(1)}, u32[]{:S(2)}, u32[]{:S(2)}) collective-permute-start(f32[40,256]{1,0:T(8,128)S(1)} %get-tuple-element.75), channel_id=1, source_target_pairs={{0,16},{1,17},{2,18},{3,19},{4,20},{5,21},{6,22},{7,23},{8,24},{9,... | collective-permute-start | bytes 122888 | tf_op jit(solution)/shard_map/ppermute | solution.py:22
  35.2 17.1 %collective-permute-start.10 = (bf16[448,512]{1,0:T(8,128)(2,1)S(1)}, bf16[448,512]{1,0:T(8,128)(2,1)S(1)}, u32[]{:S(2)}, u32[]{:S(2)}) collective-permute-start(bf16[448,512]{1,0:T(8,128)(2,1)S(1)} %slice.14), channel_id=1, source_target_pairs={{0,24},{1,25},{2,26},{3,27},{4,28},{5,29},{6,30},{7,31},{24,0},{25... | collective-permute-start | bytes 1376264 | tf_op jit(solution)/shard_map/ppermute | solution.py:39
  40.2 19.6 %collective-permute-start.12 = (bf16[448,512]{1,0:T(8,128)(2,1)S(1)}, bf16[448,512]{1,0:T(8,128)(2,1)S(1)}, u32[]{:S(2)}, u32[]{:S(2)}) collective-permute-start(bf16[448,512]{1,0:T(8,128)(2,1)S(1)} %slice.14), channel_id=1, source_target_pairs={{8,16},{9,17},{10,18},{11,19},{12,20},{13,21},{14,22},{15,23},{16,... | collective-permute-start | bytes 1376264 | tf_op jit(solution)/shard_map/ppermute | solution.py:39
  45.9 8.8 %collective-permute-start.9 = (bf16[640,256]{1,0:T(8,128)(2,1)S(1)}, bf16[640,256]{1,0:T(8,128)(2,1)S(1)}, u32[]{:S(2)}, u32[]{:S(2)}) collective-permute-start(bf16[640,256]{1,0:T(8,128)(2,1)S(1)} %shard_map.95.h0), channel_id=1, source_target_pairs={{0,4},{1,5},{2,6},{3,7},{4,0},{5,1},{6,2},{7,3},{8,12},{9,13},{10,... | collective-permute-start | bytes 983048 | tf_op jit(solution)/shard_map/ppermute | solution.py:22
  46.5 11.8 %collective-permute-start.11 = (bf16[640,256]{1,0:T(8,128)(2,1)S(1)}, bf16[640,256]{1,0:T(8,128)(2,1)S(1)}, u32[]{:S(2)}, u32[]{:S(2)}) collective-permute-start(bf16[640,256]{1,0:T(8,128)(2,1)S(1)} %shard_map.95.h0), channel_id=1, source_target_pairs={{0,8},{1,9},{2,10},{3,11},{4,12},{5,13},{6,14},{7,15},{8,0},{9,1},... | collective-permute-start | bytes 983048 | tf_op jit(solution)/shard_map/ppermute | solution.py:22
  54.6 8.7 %collective-permute-start.14 = (bf16[544,256]{1,0:T(8,128)(2,1)S(1)}, bf16[544,256]{1,0:T(8,128)(2,1)S(1)}, u32[]{:S(2)}, u32[]{:S(2)}) collective-permute-start(bf16[544,256]{1,0:T(8,128)(2,1)S(1)} %slice.16), channel_id=1, source_target_pairs={{0,8},{1,9},{2,10},{3,11},{4,12},{5,13},{6,14},{7,15},{8,0},{9,1},... | collective-permute-start | bytes 835592 | tf_op jit(solution)/shard_map/ppermute | solution.py:22
  58.3 4.1 %collective-permute-start.13 = (bf16[96,256]{1,0:T(8,128)(2,1)S(1)}, bf16[96,256]{1,0:T(8,128)(2,1)S(1)}, u32[]{:S(2)}, u32[]{:S(2)}) collective-permute-start(bf16[96,256]{1,0:T(8,128)(2,1)S(1)} %slice.17), channel_id=1, source_target_pairs={{0,4},{1,5},{2,6},{3,7},{4,0},{5,1},{6,2},{7,3},{8,12},{9,13},{10,... | collective-permute-start | bytes 147464 | tf_op jit(solution)/shard_map/ppermute | solution.py:22
  65.2 7.3 %collective-permute-start.15 = (bf16[640,256]{1,0:T(8,128)(2,1)S(1)}, bf16[640,256]{1,0:T(8,128)(2,1)S(1)}, u32[]{:S(2)}, u32[]{:S(2)}) collective-permute-start(bf16[640,256]{1,0:T(8,128)(2,1)S(1)} %get-tuple-element.102), channel_id=1, source_target_pairs={{0,1},{1,0},{2,3},{3,2},{4,5},{5,4},{6,7},{7,6},{8,9},{9,8},{10,11... | collective-permute-start | bytes 983048 | tf_op jit(solution)/shard_map/ppermute | solution.py:22
  66.5 7.3 %collective-permute-start.18 = (bf16[160,256]{1,0:T(8,128)(2,1)S(1)}, bf16[160,256]{1,0:T(8,128)(2,1)S(1)}, u32[]{:S(2)}, u32[]{:S(2)}) collective-permute-start(bf16[160,256]{1,0:T(8,128)(2,1)S(1)} %get-tuple-element.106), channel_id=1, source_target_pairs={{0,3},{1,11},{2,0},{3,8},{4,7},{5,15},{6,4},{7,12},{8,2},{9,10},{1... | collective-permute-start | bytes 245768 | tf_op jit(solution)/shard_map/ppermute | solution.py:496
  67.8 6.5 %collective-permute-start.20 = (bf16[160,256]{1,0:T(8,128)(2,1)S(1)}, bf16[160,256]{1,0:T(8,128)(2,1)S(1)}, u32[]{:S(2)}, u32[]{:S(2)}) collective-permute-start(bf16[160,256]{1,0:T(8,128)(2,1)S(1)} %get-tuple-element.108), channel_id=1, source_target_pairs={{0,7},{1,15},{2,4},{3,12},{4,3},{5,11},{6,0},{7,8},{8,6},{9,14},{1... | collective-permute-start | bytes 245768 | tf_op jit(solution)/shard_map/ppermute | solution.py:496
  69.4 10.0 %collective-permute-start.22 = (bf16[160,256]{1,0:T(8,128)(2,1)S(1)}, bf16[160,256]{1,0:T(8,128)(2,1)S(1)}, u32[]{:S(2)}, u32[]{:S(2)}) collective-permute-start(bf16[160,256]{1,0:T(8,128)(2,1)S(1)} %get-tuple-element.110), channel_id=1, source_target_pairs={{0,11},{1,3},{2,8},{3,0},{4,15},{5,7},{6,12},{7,4},{8,10},{9,2},{1... | collective-permute-start | bytes 245768 | tf_op jit(solution)/shard_map/ppermute | solution.py:496
  70.6 9.7 %collective-permute-start.24 = (bf16[160,256]{1,0:T(8,128)(2,1)S(1)}, bf16[160,256]{1,0:T(8,128)(2,1)S(1)}, u32[]{:S(2)}, u32[]{:S(2)}) collective-permute-start(bf16[160,256]{1,0:T(8,128)(2,1)S(1)} %get-tuple-element.112), channel_id=1, source_target_pairs={{0,15},{1,7},{2,12},{3,4},{4,11},{5,3},{6,8},{7,0},{8,14},{9,6},{1... | collective-permute-start | bytes 245768 | tf_op jit(solution)/shard_map/ppermute | solution.py:496
  73.1 7.2 %collective-permute-start.16 = (bf16[160,256]{1,0:T(8,128)(2,1)S(1)}, bf16[160,256]{1,0:T(8,128)(2,1)S(1)}, u32[]{:S(2)}, u32[]{:S(2)}) collective-permute-start(bf16[160,256]{1,0:T(8,128)(2,1)S(1)} %get-tuple-element.103), channel_id=1, source_target_pairs={{0,0},{1,8},{2,3},{3,11},{4,4},{5,12},{6,7},{7,15},{8,1},{9,9},{10... | collective-permute-start | bytes 245768 | tf_op jit(solution)/shard_map/ppermute | solution.py:496
  73.8 6.6 %collective-permute-start.19 = (bf16[160,256]{1,0:T(8,128)(2,1)S(1)}, bf16[160,256]{1,0:T(8,128)(2,1)S(1)}, u32[]{:S(2)}, u32[]{:S(2)}) collective-permute-start(bf16[160,256]{1,0:T(8,128)(2,1)S(1)} %get-tuple-element.107), channel_id=1, source_target_pairs={{0,4},{1,12},{2,7},{3,15},{4,0},{5,8},{6,3},{7,11},{8,5},{9,13},{1... | collective-permute-start | bytes 245768 | tf_op jit(solution)/shard_map/ppermute | solution.py:496
  74.3 7.1 %collective-permute-start.21 = (bf16[160,256]{1,0:T(8,128)(2,1)S(1)}, bf16[160,256]{1,0:T(8,128)(2,1)S(1)}, u32[]{:S(2)}, u32[]{:S(2)}) collective-permute-start(bf16[160,256]{1,0:T(8,128)(2,1)S(1)} %get-tuple-element.109), channel_id=1, source_target_pairs={{0,8},{1,0},{2,11},{3,3},{4,12},{5,4},{6,15},{7,7},{8,9},{9,1},{10... | collective-permute-start | bytes 245768 | tf_op jit(solution)/shard_map/ppermute | solution.py:496
  79.4 4.8 %collective-permute-start.23 = (bf16[160,256]{1,0:T(8,128)(2,1)S(1)}, bf16[160,256]{1,0:T(8,128)(2,1)S(1)}, u32[]{:S(2)}, u32[]{:S(2)}) collective-permute-start(bf16[160,256]{1,0:T(8,128)(2,1)S(1)} %get-tuple-element.111), channel_id=1, source_target_pairs={{0,12},{1,4},{2,15},{3,7},{4,8},{5,0},{6,11},{7,3},{8,13},{9,5},{1... | collective-permute-start | bytes 245768 | tf_op jit(solution)/shard_map/ppermute | solution.py:496
  (10 other events, 52.4 us)
